TPU v7x, 256 devices: a whole 4x4x8 slice. The times are simulated.
256 devices in a mesh: lat: 8 (over x, core), lon: 32 (over z, y).
Axes of the slice: x: 4, y: 4, z: 8, core: 2. Of those that a mesh axis runs over, the one named last changes fastest.
Arguments:
- patches: bfloat16 [128, 1024, 512], P('lat', 'lon'), may hold values from -6 to 6
- patch_mask: int32 [128, 1024], P('lat', 'lon'), may hold values 0 or 1
- mask_token: bfloat16 [512], replicated, may hold values from -6 to 6
- w_qkv: bfloat16 [512, 1536], replicated, may hold values from -0.25 to 0.25
- w_proj: bfloat16 [512, 512], replicated, may hold values from -0.25 to 0.25
- logit_scale: float32 [16], replicated, may hold values from 2 to 20
- rel_bias: float32 [16, 64, 64], replicated, may hold values from -4 to 4
- attn_gain: float32 [512], replicated, may hold values from 0.1 to 1.9
- moe_gain: float32 [512], replicated, may hold values from 0.1 to 1.9
- router: bfloat16 [512, 32], replicated, may hold values from -0.5 to 0.5
- expert_ids: int32 [8, 32, 512, 1], P('lat', 'lon'), may hold values from 0 to 31; in each aligned block of 512 rows (0 to 511, 512 to 1023, ..., all dimensions but the last counted through in order) at most 32 rows name the same one
- w_in: bfloat16 [32, 512, 2048], P('lon'), may hold values from -0.25 to 0.25
- w_out: bfloat16 [32, 512, 2048], P('lon'), may hold values from -0.125 to 0.125
- cotangent: bfloat16 [128, 1024, 512], P('lat', 'lon'), may hold values from -6 to 6
Outputs:
- block_out: bfloat16 [128, 1024, 512], P('lat', 'lon')
- mixer_grad: float32 [128, 1024, 512], P('lat', 'lon')
- weight_grads: float32 [512, 32, 4096], P('lat', 'lon')
Inputs may be any that keep to these rules, and one draw needn't show every extreme that they name: `expert_ids`: among the 512 patches of one device no expert is named more than 32 times.
All inputs are finite; a program needn't handle non-finite values. No bound on the sum of `patch_mask` on one device may be relied on, other than what follows from the above.
Results may differ from a plain program's by a relative error of at most 0.03.
Values may be sent and summed in bfloat16 or wider, within the bound.
No kernel may reach another device: no remote copies, remote signals or barrier semaphores. Data moves between devices by JAX's collectives and lax.ppermute only.
A program may use at most 128 MiB of HBM per device.

v0:
```python
import jax
import jax.numpy as jnp
from jax import lax
from jax.sharding import PartitionSpec as P

WIN = 8
SHIFT = 4


def passed_along(block, axis, distance):
    devices = range(lax.axis_size(axis))
    route = [((i - distance) % len(devices), i) for i in devices]
    return lax.ppermute(block, axis, route)


def layer_norm(values, gain):
    average = jnp.mean(values, axis=-1, keepdims=True)
    centred = values - average
    variance = jnp.mean(centred * centred, axis=-1, keepdims=True)
    return centred * lax.rsqrt(variance + 1e-05) * gain


def norm_backward(values, gain, upstream):
    average = jnp.mean(values, axis=-1, keepdims=True)
    centred = values - average
    variance = jnp.mean(centred * centred, axis=-1, keepdims=True)
    inv_std = lax.rsqrt(variance + 1e-05)
    normal_part = centred * inv_std
    scaled = upstream * gain
    first_mean = jnp.mean(scaled, axis=-1, keepdims=True)
    second_mean = jnp.mean(scaled * normal_part, axis=-1, keepdims=True)
    return inv_std * (scaled - first_mean - normal_part * second_mean)


def gelu_parts(preact):
    normal_cdf = 0.5 * (1.0 + jax.scipy.special.erf(preact * 0.7071067811865476))
    density = jnp.exp(-0.5 * preact * preact) * 0.3989422804014327
    return (preact * normal_cdf, normal_cdf + preact * density)


def to_windows(block):
    height, lateral, channels = block.shape
    tiled = block.reshape(height // WIN, WIN, lateral // WIN, WIN, channels).transpose(
        0, 2, 1, 3, 4
    )
    return tiled.reshape(height // WIN * (lateral // WIN), WIN * WIN, channels)


def from_windows(windows, height, lateral):
    channels = windows.shape[-1]
    block = windows.reshape(height // WIN, lateral // WIN, WIN, WIN, channels).transpose(
        0, 2, 1, 3, 4
    )
    return block.reshape(height, lateral, channels)


def window_labels(row_labels, lateral):
    height = row_labels.shape[0]
    grid = jnp.broadcast_to(
        row_labels.reshape(height // WIN, 1, WIN, 1), (height // WIN, lateral // WIN, WIN, WIN)
    )
    return grid.reshape(height // WIN * (lateral // WIN), WIN * WIN)


def window_attention(windows, labels, w_qkv, w_proj, logit_scale, rel_bias, attn_gain):
    window_count, window_size, channels = windows.shape
    head_count = rel_bias.shape[0]
    flat = windows.reshape(window_count * window_size, channels)
    projected = jnp.dot(flat, w_qkv, preferred_element_type=jnp.float32).astype(jnp.bfloat16)
    projected = projected.reshape(window_count, window_size, 3, head_count, channels // head_count)
    queries = projected[:, :, 0].astype(jnp.float32)
    key_vecs = projected[:, :, 1].astype(jnp.float32)
    value_vecs = projected[:, :, 2]
    queries = queries * lax.rsqrt(jnp.sum(queries * queries, axis=-1, keepdims=True) + 1e-06)
    key_vecs = key_vecs * lax.rsqrt(jnp.sum(key_vecs * key_vecs, axis=-1, keepdims=True) + 1e-06)
    scores = (
        jnp.einsum("wqhc,wkhc->whqk", queries, key_vecs) * logit_scale[None, :, None, None]
        + rel_bias[None]
    )
    allowed = (labels[:, :, None] == labels[:, None, :])[:, None]
    weights = jnp.where(allowed, jnp.exp(scores), 0.0)
    weights = (weights / jnp.sum(weights, axis=-1, keepdims=True)).astype(jnp.bfloat16)
    blended = jnp.einsum(
        "whqk,wkhc->wqhc", weights, value_vecs, preferred_element_type=jnp.float32
    ).astype(jnp.bfloat16)
    projection = jnp.dot(
        blended.reshape(window_count * window_size, channels),
        w_proj,
        preferred_element_type=jnp.float32,
    )
    resid = flat.astype(jnp.float32) + layer_norm(projection, attn_gain)
    return resid.astype(jnp.bfloat16).reshape(window_count, window_size, channels)


def to_experts(buffers):
    lon_count = lax.axis_size("lon")
    stacked, expert_total, capacity, channels = buffers.shape
    received = lax.all_to_all(buffers, "lon", split_axis=1, concat_axis=1, tiled=True)
    local_count = expert_total // lon_count
    received = received.reshape(stacked, lon_count, local_count, capacity, channels).transpose(
        0, 2, 1, 3, 4
    )
    return received.reshape(stacked, local_count, lon_count * capacity, channels)


def from_experts(results, capacity):
    lon_count = lax.axis_size("lon")
    stacked, local_count, slot_total, channels = results.shape
    ordered = results.reshape(stacked, local_count, lon_count, capacity, channels).transpose(
        0, 2, 1, 3, 4
    )
    ordered = ordered.reshape(stacked, lon_count * local_count, capacity, channels)
    returned = lax.all_to_all(ordered, "lon", split_axis=1, concat_axis=1, tiled=True)
    return returned.reshape(stacked, lon_count * local_count * capacity, channels)


def per_device(
    patches,
    patch_mask,
    mask_token,
    w_qkv,
    w_proj,
    logit_scale,
    rel_bias,
    attn_gain,
    moe_gain,
    router,
    expert_ids,
    w_in,
    w_out,
    cotangent,
):
    height, lateral, channels = patches.shape
    masked = jnp.where(patch_mask[:, :, None] == 1, mask_token[None, None, :], patches)
    right_rim = passed_along(masked[:, :SHIFT], "lon", -1)
    widened = jnp.concatenate([masked[:, SHIFT:], right_rim], axis=1)
    lower_rim = passed_along(widened[:SHIFT], "lat", -1)
    displaced = jnp.concatenate([widened[SHIFT:], lower_rim], axis=0)
    band_rows = lax.axis_index("lat") * height + jnp.arange(height, dtype=jnp.int32)
    row_labels = (band_rows >= height * lax.axis_size("lat") - SHIFT).astype(jnp.int32)
    attended = window_attention(
        to_windows(displaced),
        window_labels(row_labels, lateral),
        w_qkv,
        w_proj,
        logit_scale,
        rel_bias,
        attn_gain,
    )
    hidden = from_windows(attended, height, lateral)
    token_total = height * lateral
    hidden_f = hidden.reshape(token_total, channels).astype(jnp.float32)
    cot_f = cotangent.reshape(token_total, channels).astype(jnp.float32)
    normed = layer_norm(hidden_f, moe_gain).astype(jnp.bfloat16)
    expert_total = router.shape[1]
    capacity = 2 * token_total // expert_total
    logits = jnp.dot(normed, router, preferred_element_type=jnp.float32)
    chosen_ids = expert_ids.reshape(token_total)
    onehot = (chosen_ids[:, None] == jnp.arange(expert_total, dtype=jnp.int32)[None, :]).astype(
        jnp.float32
    )
    gate = jax.nn.sigmoid(jnp.sum(logits * onehot, axis=-1))
    scaled_cot = (gate[:, None] * cot_f).astype(jnp.bfloat16)
    positions = jnp.arange(token_total, dtype=jnp.int32)
    strict_lower = (positions[:, None] > positions[None, :]).astype(jnp.float32)
    earlier = jnp.dot(strict_lower, onehot, precision=lax.Precision.HIGHEST)
    slots = jnp.sum(earlier * onehot, axis=-1).astype(jnp.int32)
    targets = chosen_ids * capacity + slots
    normed_send = (
        jnp.zeros((expert_total * capacity, channels), jnp.bfloat16).at[targets].set(normed)
    )
    cot_send = (
        jnp.zeros((expert_total * capacity, channels), jnp.bfloat16).at[targets].set(scaled_cot)
    )
    normed_send = normed_send.reshape(expert_total, capacity, channels)
    cot_send = cot_send.reshape(expert_total, capacity, channels)
    z_slots = to_experts(normed_send[None])[0]
    preact = jnp.einsum("esd,edf->esf", z_slots, w_in, preferred_element_type=jnp.float32)
    expert_activation, slopes = gelu_parts(preact)
    expert_activation = expert_activation.astype(jnp.bfloat16)
    outputs = jnp.einsum(
        "esf,edf->esd", expert_activation, w_out, preferred_element_type=jnp.float32
    ).astype(jnp.bfloat16)
    activation, slopes, outputs = (expert_activation, slopes, outputs)
    expert_back = from_experts(outputs[None], capacity)[0]
    d_slots = to_experts(cot_send[None])[0]
    dact = jnp.einsum("esd,edf->esf", d_slots, w_out, preferred_element_type=jnp.float32)
    expert_dpreact = (dact * slopes).astype(jnp.bfloat16)
    dnormed_slots = jnp.einsum(
        "esf,edf->esd", expert_dpreact, w_in, preferred_element_type=jnp.float32
    ).astype(jnp.bfloat16)
    dpreact, dnormed_slots = (expert_dpreact, dnormed_slots)
    dnormed_back = from_experts(dnormed_slots[None], capacity)[0]
    grad_in = jnp.einsum("esd,esf->def", z_slots, dpreact, preferred_element_type=jnp.float32)
    grad_out = jnp.einsum("esd,esf->def", d_slots, activation, preferred_element_type=jnp.float32)
    weight_grads = lax.psum_scatter(
        jnp.concatenate([grad_in, grad_out], axis=2).astype(jnp.bfloat16),
        "lat",
        scatter_dimension=0,
        tiled=True,
    ).astype(jnp.float32)
    expert_out = expert_back[targets].astype(jnp.float32)
    dnormed_exp = dnormed_back[targets].astype(jnp.float32)
    block_out = (hidden_f + gate[:, None] * expert_out).astype(jnp.bfloat16)
    dgate = jnp.sum(cot_f * expert_out, axis=-1)
    dlogit = dgate * gate * (1.0 - gate)
    coeffs = dlogit[:, None] * onehot
    router_part = jnp.dot(coeffs, router.astype(jnp.float32).T, precision=lax.Precision.HIGHEST)
    dnormed = dnormed_exp + router_part
    mixer_grad = cot_f + norm_backward(hidden_f, moe_gain, dnormed)
    return (
        block_out.reshape(height, lateral, channels),
        mixer_grad.reshape(height, lateral, channels),
        weight_grads,
    )


def solution(mesh):
    placed = (
        P("lat", "lon", None),
        P("lat", "lon"),
        P(),
        P(),
        P(),
        P(),
        P(),
        P(),
        P(),
        P(),
        P("lat", "lon", None, None),
        P("lon", None, None),
        P("lon", None, None),
        P("lat", "lon", None),
    )
    return jax.shard_map(
        per_device,
        mesh=mesh,
        in_specs=placed,
        out_specs=(P("lat", "lon", None), P("lat", "lon", None), P("lat", "lon", None)),
        check_vma=False,
    )
```

profile of v0, /device:TPU:6, one launch (start us, length us, event | category | flops | bytes accessed | tf_op | source)
XLA Modules:
  0.0 260.6 jit_solution(4628282794245057005)
XLA Ops:
  7.2 0.8 broadcast_compare_fusion.1
  8.0 1.2 broadcast_select_fusion
  9.2 8.4 %collective-permute-start = (bf16[16,4,512]{2,1,0:T(4,128)(2,1)S(1)}, bf16[16,4,512]{2,1,0:T(4,128)(2,1)S(1)}, u32[]{:S(2)}, u32[]{:S(2)}) collective-permute-start(bf16[16,4,512]{2,1,0:T(4,128)(2,1)S(1)} %slice.33), channel_id=1, source_target_pairs={{1,0},{2,1},{3,2},{4,3},{5,4},{6,5},{7,6},{8,7},{9,8},{10,9},{11,1... | collective-permute-start | bytes 196616 | tf_op jit(solution)/shard_map/ppermute | solution.py:13
  18.1 1.0 fusion.32
  19.6 0.7 compare_select_fusion
  20.3 1.2 copy.43
  21.6 0.5 collective-permute-done.1
  22.2 0.8 copy-done.2
  23.0 3.6 %convolution_convert_fusion.2 = bf16[512,1536]{1,0:T(8,128)(2,1)} fusion(bf16[512,512]{1,0:T(8,128)(2,1)S(1)} %bitcast.134, bf16[512,1536]{1,0:T(8,128)(2,1)} %param.17), kind=kOutput, calls=%fused_computation.19 | convolution fusion | flops 806092800 | bytes 3670016 | tf_op jit(solution)/shard_map/dot_general | solution.py:69
  26.5 2.6 copy.39
  29.1 5.1 %reshape.273 = bf16[8,64,3,16,32]{1,0,4,3,2:T(8,128)(2,1)} reshape(bf16[512,1536]{0,1:T(8,128)(2,1)} %copy.39) | data formatting | bytes 3145728 | tf_op jit(solution)/shard_map/reshape | solution.py:70
  34.3 2.2 fusion.9
  36.8 0.6 convert_multiply_fusion.2
  37.4 1.8 fusion.6
  39.2 1.3 fusion.29
  40.5 0.7 copy.45
  41.2 1.4 reshape.274
  42.6 1.8 fusion.52
  44.7 1.3 convert_bitcast_fusion
  46.9 1.0 multiply_convert_fusion.1
  47.9 4.0 %scatter_custom_fusion = bf16[1024,512]{1,0:T(8,128)(2,1)} fusion(s32[512]{0:T(512)S(1)} %bitcast.145, bf16[512,512]{1,0:T(8,128)(2,1)} %multiply_convert_fusion.1, bf16[]{:T(256)} %constant.44.clone.1), kind=kCustom, calls=%fused_computation.76 | custom fusion | bytes 1049088 | tf_op jit(solution)/shard_map/scatter | solution.py:170
  51.8 36.4 %all_to_all.20 = bf16[1,32,32,512]{3,2,0,1:T(8,128)(2,1)S(1)} all-to-all(bf16[1,32,32,512]{3,2,0,1:T(8,128)(2,1)} %bitcast.132), channel_id=1, replica_groups=mesh['lat'=8,'lon'=32] {'lon'}, dimensions={1} | all-to-all | bytes 2097152 | tf_op jit(solution)/shard_map/all_to_all | solution.py:98
  88.2 5.2 %multiply_convert_fusion = (bf16[1024,2048]{1,0:T(8,128)(2,1)S(1)}, f32[1024,2048]{1,0:T(8,128)}) fusion(bf16[1024,512]{1,0:T(8,128)(2,1)S(1)} %bitcast.136, bf16[1,512,2048]{2,1,0:T(8,128)(2,1)S(1)} %copy-done), kind=kOutput, calls=%fused_computation.11 | convolution fusion | flops 2157969408 | bytes 15728640 | tf_op jit(solution)/shard_map/esd,edf->esf/dot_general | solution.py:178
  93.4 3.3 %fusion.26 = bf16[1024,512]{1,0:T(8,128)(2,1)} fusion(bf16[1024,2048]{1,0:T(8,128)(2,1)S(1)} %get-tuple-element.26, bf16[1,512,2048]{2,1,0:T(8,128)(2,1)S(1)} %copy-done.9), kind=kOutput, calls=%fused_computation.41 | convolution fusion | flops 2148007936 | bytes 7340032 | tf_op jit(solution)/shard_map/esf,edf->esd/dot_general | solution.py:181
  96.8 5.5 %all-to-all-start.1 = ((bf16[1,32,32,512]{3,2,0,1:T(8,128)(2,1)}), bf16[1,32,32,512]{3,2,0,1:T(8,128)(2,1)}, u32[]{:S(2)}, u32[]{:S(2)}) async-start(bf16[1,32,32,512]{3,2,0,1:T(8,128)(2,1)} %bitcast.139), calls=%async_computation.1 | async-start | bytes 2097152 | tf_op jit(solution)/shard_map/all_to_all | solution.py:113
  102.4 1.3 fusion.31
  103.7 27.3 %all-to-all-done.1 = bf16[1,32,32,512]{3,2,0,1:T(8,128)(2,1)} async-done(((bf16[1,32,32,512]{3,2,0,1:T(8,128)(2,1)}), bf16[1,32,32,512]{3,2,0,1:T(8,128)(2,1)}, u32[]{:S(2)}, u32[]{:S(2)}) %all-to-all-start.1) | async-done | bytes 1048608 | tf_op jit(solution)/shard_map/all_to_all | solution.py:113
  131.0 4.0 %gather_fusion = bf16[512,512]{1,0:T(8,128)(2,1)} fusion(bf16[1024,512]{1,0:T(8,128)(2,1)} %bitcast.25, s32[1024]{0:T(1024)S(1)} %pad_clamp_fusion), kind=kCustom, calls=%fused_computation | custom fusion | bytes 1050624 | tf_op jit(solution)/shard_map/gather | solution.py:202
  135.0 1.4 fusion.35
  136.5 2.0 fusion.36
  138.5 4.0 %scatter_custom_fusion.1 = bf16[1024,512]{1,0:T(8,128)(2,1)} fusion(s32[512]{0:T(512)S(1)} %bitcast.147, bf16[512,512]{1,0:T(8,128)(2,1)} %fusion.36, bf16[]{:T(256)} %constant.44.clone.1), kind=kCustom, calls=%fused_computation.74 | custom fusion | bytes 1049088 | tf_op jit(solution)/shard_map/scatter | solution.py:173
  142.5 33.0 %all_to_all.21 = bf16[1,32,32,512]{3,2,0,1:T(8,128)(2,1)S(1)} all-to-all(bf16[1,32,32,512]{3,2,0,1:T(8,128)(2,1)} %bitcast.131), channel_id=1, replica_groups=mesh['lat'=8,'lon'=32] {'lon'}, dimensions={1} | all-to-all | bytes 2097152 | tf_op jit(solution)/shard_map/all_to_all | solution.py:98
  175.5 4.7 %fusion.8 = bf16[512,1,2048]{0,2,1:T(8,128)(2,1)S(1)} fusion(bf16[1024,2048]{1,0:T(8,128)(2,1)} %copy-done.12, bf16[1024,512]{1,0:T(8,128)(2,1)S(1)} %bitcast.140), kind=kOutput, calls=%fused_computation.21 | convolution fusion | flops 2148532224 | bytes 7340032 | tf_op jit(solution)/shard_map/esd,esf->def/dot_general | solution.py:195
  180.2 7.0 %fusion.5 = bf16[1024,2048]{1,0:T(8,128)(2,1)S(1)} fusion(f32[1024,2048]{1,0:T(8,128)} %get-tuple-element.27, bf16[1024,512]{1,0:T(8,128)(2,1)S(1)} %bitcast.141, bf16[1,512,2048]{2,1,0:T(8,128)(2,1)S(1)} %copy-done.10), kind=kOutput, calls=%fused_computation.10 | convolution fusion | flops 2168455168 | bytes 15728640 | tf_op jit(solution)/shard_map/esd,edf->esf/dot_general | solution.py:187
  187.3 2.0 copy-done.13
  189.3 2.5 fusion.7
  191.7 2.2 maximum_bitcast_fusion
  194.0 6.4 %copy.56 = bf16[512,4096]{1,0:T(8,128)(2,1)} copy(bf16[512,4096]{0,1:T(8,128)(2,1)} %maximum_bitcast_fusion) | data formatting | bytes 8388608
  200.4 5.5 %fusion.23 = bf16[1024,512]{1,0:T(8,128)(2,1)} fusion(bf16[1024,2048]{1,0:T(8,128)(2,1)} %copy-done.13, bf16[1,512,2048]{2,1,0:T(8,128)(2,1)S(1)} %copy-done), kind=kOutput, calls=%fused_computation.40 | convolution fusion | flops 2148007936 | bytes 7340032 | tf_op jit(solution)/shard_map/esf,edf->esd/dot_general | solution.py:189
  205.9 5.7 %all-to-all-start.3 = ((bf16[1,32,32,512]{3,2,0,1:T(8,128)(2,1)}), bf16[1,32,32,512]{3,2,0,1:T(8,128)(2,1)}, u32[]{:S(2)}, u32[]{:S(2)}) async-start(bf16[1,32,32,512]{3,2,0,1:T(8,128)(2,1)} %bitcast.138), calls=%async_computation.3 | async-start | bytes 2097152 | tf_op jit(solution)/shard_map/all_to_all | solution.py:113
  211.8 2.0 fusion.34
  213.8 24.6 %all-to-all-done.3 = bf16[1,32,32,512]{3,2,0,1:T(8,128)(2,1)} async-done(((bf16[1,32,32,512]{3,2,0,1:T(8,128)(2,1)}), bf16[1,32,32,512]{3,2,0,1:T(8,128)(2,1)}, u32[]{:S(2)}, u32[]{:S(2)}) %all-to-all-start.3) | async-done | bytes 1048608 | tf_op jit(solution)/shard_map/all_to_all | solution.py:113
  238.4 4.0 %gather_fusion.1 = bf16[512,512]{1,0:T(8,128)(2,1)} fusion(bf16[1024,512]{1,0:T(8,128)(2,1)} %bitcast.32, s32[1024]{0:T(1024)S(1)} %pad_clamp_fusion), kind=kCustom, calls=%fused_computation.1 | custom fusion | bytes 1050624 | tf_op jit(solution)/shard_map/gather | solution.py:203
  242.4 2.1 fusion.51
  244.4 2.4 bitcast_add_fusion
  246.8 1.5 copy.57
  248.4 1.5 bitcast_convert_fusion
  249.8 3.9 %copy.52 = f32[64,1,4096]{2,1,0:T(1,128)} copy(f32[64,1,4096]{0,2,1:T(8,128)} %bitcast_convert_fusion) | data formatting | bytes 2097152
  (63 shorter events, 2.6 us)
Async XLA Ops:
  7.2 81.1 %copy-start = (bf16[1,512,2048]{2,1,0:T(8,128)(2,1)S(1)}, bf16[1,512,2048]{2,1,0:T(8,128)(2,1)}, u32[]{:S(2)}) copy-start(bf16[1,512,2048]{2,1,0:T(8,128)(2,1)} %param.25) | copy-start | bytes 6291460
  9.2 10.3 %collective-permute-start = (bf16[16,4,512]{2,1,0:T(4,128)(2,1)S(1)}, bf16[16,4,512]{2,1,0:T(4,128)(2,1)S(1)}, u32[]{:S(2)}, u32[]{:S(2)}) collective-permute-start(bf16[16,4,512]{2,1,0:T(4,128)(2,1)S(1)} %slice.33), channel_id=1, source_target_pairs={{1,0},{2,1},{3,2},{4,3},{5,4},{6,5},{7,6},{8,7},{9,8},{10,9},{11,1... | collective-permute-start | bytes 196616 | tf_op jit(solution)/shard_map/ppermute | solution.py:13
  19.6 2.5 collective-permute-start.1
  22.2 0.8 copy-start.2
  34.3 2.5 copy-start.1
  34.3 3.1 %copy-start.11 = (f32[16]{0:T(128)S(1)}, f32[16]{0:T(128)}, u32[]{:S(2)}) copy-start(f32[16]{0:T(128)} %param.19) | copy-start | bytes 196
  37.4 1.8 slice-start
  40.5 4.2 %copy-start.8 = (f32[512]{0:T(512)S(1)}, f32[512]{0:T(512)}, u32[]{:S(2)}) copy-start(f32[512]{0:T(512)} %param.21) | copy-start | bytes 6148
  44.4 2.5 copy-start.7
  88.2 5.2 %copy-start.3 = (bf16[1,32,32,512]{3,2,0,1:T(8,128)(2,1)}, bf16[1,32,32,512]{3,2,0,1:T(8,128)(2,1)S(1)}, u32[]{:S(2)}) copy-start(bf16[1,32,32,512]{3,2,0,1:T(8,128)(2,1)S(1)} %all_to_all.20) | copy-start | bytes 3145732
  88.2 5.2 %copy-start.9 = (bf16[1,512,2048]{2,1,0:T(8,128)(2,1)S(1)}, bf16[1,512,2048]{2,1,0:T(8,128)(2,1)}, u32[]{:S(2)}) copy-start(bf16[1,512,2048]{2,1,0:T(8,128)(2,1)} %param.26) | copy-start | bytes 6291460
  93.4 3.4 %copy-start.12 = (bf16[1024,2048]{1,0:T(8,128)(2,1)}, bf16[1024,2048]{1,0:T(8,128)(2,1)S(1)}, u32[]{:S(2)}) copy-start(bf16[1024,2048]{1,0:T(8,128)(2,1)S(1)} %get-tuple-element.26) | copy-start | bytes 12582916
  93.4 8.9 %copy-start.5 = (bf16[512,32]{0,1:T(8,128)(2,1)S(1)}, bf16[512,32]{0,1:T(8,128)(2,1)}, u32[]{:S(2)}) copy-start(bf16[512,32]{0,1:T(8,128)(2,1)} %param.23) | copy-start | bytes 98308
  93.4 8.9 %copy-start.6 = (s32[1,1,512,1]{2,3,1,0:T(1,128)S(1)}, s32[1,1,512,1]{2,3,1,0:T(1,128)}, u32[]{:S(2)}) copy-start(s32[1,1,512,1]{2,3,1,0:T(1,128)} %param.24) | copy-start | bytes 6148
  96.8 34.2 %all-to-all-start.1 = ((bf16[1,32,32,512]{3,2,0,1:T(8,128)(2,1)}), bf16[1,32,32,512]{3,2,0,1:T(8,128)(2,1)}, u32[]{:S(2)}, u32[]{:S(2)}) async-start(bf16[1,32,32,512]{3,2,0,1:T(8,128)(2,1)} %bitcast.139), calls=%async_computation.1 | async-start | bytes 2097152 | tf_op jit(solution)/shard_map/all_to_all | solution.py:113
  102.3 144.6 %reduce-scatter.4.cloned.1.call-start = ((), (), s32[]{:S(2)}) async-start(), calls=%async_computation.5 | async-start | bytes 4718592
  175.5 4.7 %copy-start.10 = (bf16[1,512,2048]{2,1,0:T(8,128)(2,1)S(1)}, bf16[1,512,2048]{2,1,0:T(8,128)(2,1)}, u32[]{:S(2)}) copy-start(bf16[1,512,2048]{2,1,0:T(8,128)(2,1)} %param.26) | copy-start | bytes 6291460
  180.2 9.0 %copy-start.4 = (bf16[1,32,32,512]{3,2,0,1:T(8,128)(2,1)S(1)}, bf16[1,32,32,512]{3,2,0,1:T(8,128)(2,1)}, u32[]{:S(2)}) copy-start(bf16[1,32,32,512]{3,2,0,1:T(8,128)(2,1)} %copy-done.3) | copy-start | bytes 3145732
  187.3 2.0 copy-start.13
  205.9 32.4 %all-to-all-start.3 = ((bf16[1,32,32,512]{3,2,0,1:T(8,128)(2,1)}), bf16[1,32,32,512]{3,2,0,1:T(8,128)(2,1)}, u32[]{:S(2)}, u32[]{:S(2)}) async-start(bf16[1,32,32,512]{3,2,0,1:T(8,128)(2,1)} %bitcast.138), calls=%async_computation.3 | async-start | bytes 2097152 | tf_op jit(solution)/shard_map/all_to_all | solution.py:113
Sparse Core Ops, SparseCore 0:
  200.5 34.7 reduce-scatter.3
where the time goes:
time: 262 us; the launch traced here: 261 us
  blocking collectives  69.4 us (26%)
  waiting for transfers between devices  52.8 us (20%)
  local copies, waits for them, and re-layouts  42.6 us (16%)
  matrix products  41.1 us (16%)
  other arithmetic  20.5 us (8%)
  starting transfers between devices  19.7 us (8%)
  between operations  14.5 us (6%)
    all_to_all x2, blocking collectives, to_experts(): lax.all_to_all(buffers, 'lon', split_axis=1, concat_axis=1, tiled=True)  69.4 us
    all_to_all x2, waiting for transfers between devices, from_experts(): lax.all_to_all(ordered, 'lon', split_axis=1, concat_axis=1, tiled=True)  51.9 us
    unnamed x32, local copies, waits for them, and re-layouts  16.1 us
    all_to_all x2, starting transfers between devices, from_experts(): lax.all_to_all(ordered, 'lon', split_axis=1, concat_axis=1, tiled=True)  11.2 us
    ppermute x2, starting transfers between devices, passed_along(): return lax.ppermute(block, axis, route)  8.4 us
    scatter x2, local copies, waits for them, and re-layouts, per_device(): jnp.zeros((expert_total * capacity, channels), jnp.bfloat16).at[targets]  7.9 us
    dot_general x1, matrix products, per_device(): jnp.einsum('esd,edf->esf', d_slots, w_out, preferred_element_type=jnp.flo...  7.05 us
    dot_general x1, matrix products, per_device(): jnp.einsum('esf,edf->esd', expert_dpreact, w_in, preferred_element_type=j...  5.52 us
  transfers between devices with their start and end apart: 5, of which 4 were waited for; matrix products, arithmetic and copies ran while one was open for 8% of the time, Pallas kernels for 0%

commit v1 on v0

v1 whole, which is shorter than its diff:
```python
import jax
import jax.numpy as jnp
from jax import lax
from jax.experimental import pallas as pl
from jax.experimental.pallas import tpu as pltpu
from jax.sharding import PartitionSpec as P

WIN = 8
SHIFT = 4
BF16 = jnp.bfloat16
F32 = jnp.float32
I32 = jnp.int32
VMEM_BYTES = 48 * 1024 * 1024


def call(body, outs, *operands, scratch=(), smem=()):
    specs = [
        pl.BlockSpec(memory_space=pltpu.SMEM if i in smem else pltpu.VMEM)
        for i in range(len(operands))
    ]
    return pl.pallas_call(
        body,
        out_shape=outs,
        in_specs=specs,
        out_specs=jax.tree.map(lambda _: pl.BlockSpec(memory_space=pltpu.VMEM), outs),
        scratch_shapes=list(scratch),
        compiler_params=pltpu.CompilerParams(vmem_limit_bytes=VMEM_BYTES),
    )(*operands)


def shape(dims, dtype):
    return jax.ShapeDtypeStruct(dims, dtype)


def dot(a, b):
    return jnp.dot(a, b, preferred_element_type=F32)


def dot_nt(a, b):
    return lax.dot_general(a, b, (((1,), (1,)), ((), ())), preferred_element_type=F32)


def dot_tn(a, b):
    return lax.dot_general(a, b, (((0,), (0,)), ((), ())), preferred_element_type=F32)


def halves(values):
    high = values.astype(BF16)
    return high, (values - high.astype(F32)).astype(BF16)


def dot_split(values, ones):
    high, low = halves(values)
    return dot(high, ones) + dot(low, ones)


def iota(dims, axis):
    return lax.broadcasted_iota(I32, dims, axis)


def flag(condition):
    return jnp.where(condition, 1.0, 0.0).astype(BF16)


def normal_form(values):
    centred = values - jnp.mean(values, axis=-1, keepdims=True)
    inv_std = lax.rsqrt(jnp.mean(centred * centred, axis=-1, keepdims=True) + 1e-05)
    return centred * inv_std, inv_std


def gelu_parts(preact):
    normal_cdf = 0.5 * (1.0 + lax.erf(preact * 0.7071067811865476))
    density = jnp.exp(-0.5 * preact * preact) * 0.3989422804014327
    return preact * normal_cdf, normal_cdf + preact * density


def passed_along(block, axis, distance):
    devices = range(lax.axis_size(axis))
    route = [((i - distance) % len(devices), i) for i in devices]
    return lax.ppermute(block, axis, route)


def passed_diagonally(block):
    rows, columns = lax.axis_size("lat"), lax.axis_size("lon")
    route = [
        ((i + 1) % rows * columns + (j + 1) % columns, i * columns + j)
        for i in range(rows)
        for j in range(columns)
    ]
    return lax.ppermute(block, ("lat", "lon"), route)


def exchanged(slots):
    return lax.all_to_all(slots, "lon", split_axis=0, concat_axis=0, tiled=True)


def slot_kernel(expert_total, capacity, ids_ref, cot_ref, send_ref, row_ref, col_ref):
    tokens = cot_ref.shape[0]
    ids = ids_ref[...]
    onehot = iota((expert_total, tokens), 0) == ids
    before = flag(iota((tokens, tokens), 0) < iota((tokens, tokens), 1))
    earlier = dot(flag(onehot), before)
    slot = jnp.sum(jnp.where(onehot, earlier, 0.0), axis=0, keepdims=True).astype(I32)
    target = ids * capacity + slot
    row_ref[...] = target
    diagonal = iota((tokens, tokens), 0) == iota((tokens, tokens), 1)
    column = jnp.sum(jnp.where(diagonal, target, 0).astype(F32), axis=1, keepdims=True)
    col_ref[...] = jnp.broadcast_to(column.astype(I32), col_ref.shape)
    placed = flag(iota((send_ref.shape[0], tokens), 0) == target)
    send_ref[...] = dot(placed, cot_ref[...]).astype(BF16)


def attention_kernel(
    heads,
    flag_ref,
    patches_ref,
    mask_ref,
    token_ref,
    right_ref,
    low_ref,
    corner_ref,
    qkv_ref,
    proj_ref,
    scale_ref,
    bias_ref,
    attn_gain_ref,
    moe_gain_ref,
    router_ref,
    row_ref,
    col_ref,
    hidden_ref,
    send_ref,
    gate_ref,
    blended_ref,
):
    tokens, width = patches_ref.shape
    height, lateral = mask_ref.shape
    features = width // heads
    window = WIN * WIN
    across = lateral // WIN
    group = 128 // features
    expert_total = router_ref.shape[0]
    capacity = send_ref.shape[0] // expert_total

    in_row = flag(iota((tokens, height), 0) // lateral == iota((tokens, height), 1))
    spread = dot(in_row, mask_ref[...].astype(F32).astype(BF16))
    own = iota((tokens, lateral), 0) % lateral == iota((tokens, lateral), 1)
    hidden_patch = jnp.sum(jnp.where(own, spread, 0.0), axis=1, keepdims=True)
    masked = jnp.where(
        hidden_patch > 0.5, token_ref[...].astype(F32), patches_ref[...].astype(F32)
    ).astype(BF16)
    source = jnp.concatenate([masked, right_ref[...], low_ref[...], corner_ref[...]], axis=0)

    place = iota((tokens, 1), 0)
    which, inside = place // window, place % window
    row = which // across * WIN + inside // WIN + SHIFT
    column = which % across * WIN + inside % WIN + SHIFT
    right_base = tokens
    low_base = right_base + height * SHIFT
    corner_base = low_base + SHIFT * lateral
    local = row * lateral + column
    from_right = right_base + row * SHIFT + column - lateral
    from_low = low_base + (row - height) * lateral + column
    from_corner = corner_base + (row - height) * SHIFT + column - lateral
    origin = jnp.where(
        row < height,
        jnp.where(column < lateral, local, from_right),
        jnp.where(column < lateral, from_low, from_corner),
    )
    moves = flag(iota((tokens, source.shape[0]), 1) == origin)
    displaced_f = dot(moves, source)
    displaced = displaced_f.astype(BF16)

    projected = dot(displaced, qkv_ref[...]).astype(BF16)
    head_of = flag(iota((width, heads), 0) // features == iota((width, heads), 1))
    of_head = flag(iota((heads, width), 1) // features == iota((heads, width), 0))
    queries = projected[:, :width].astype(F32)
    keys = projected[:, width : 2 * width].astype(F32)
    query_norm = lax.rsqrt(dot_split(queries * queries, head_of) + 1e-06) * scale_ref[...]
    key_norm = lax.rsqrt(dot_split(keys * keys, head_of) + 1e-06)
    queries = (queries * dot_split(query_norm, of_head)).astype(BF16)
    keys = (keys * dot_split(key_norm, of_head)).astype(BF16)

    block = group * window
    member = flag(
        iota((block, 128), 0) // window == iota((block, 128), 1) // features
    )
    split = (iota((window, block), 0) >= window // 2) == (
        iota((window, block), 1) % window >= window // 2
    )
    allowed = jnp.where(split, 1.0, jnp.where(flag_ref[0] == 1, 0.0, 1.0))
    for w in range(tokens // window):
        rows = slice(w * window, (w + 1) * window)
        for g in range(width // 128):
            lanes = slice(g * 128, (g + 1) * 128)
            q = queries[rows, lanes]
            k = keys[rows, lanes]
            v = projected[rows, 2 * width + g * 128 : 2 * width + (g + 1) * 128]
            wide_k = jnp.concatenate([k] * group, axis=0) * member
            wide_v = jnp.concatenate([v] * group, axis=0) * member
            scores = dot_nt(q, wide_k) + bias_ref[:, g * block : (g + 1) * block]
            weights = jnp.exp(scores)
            if w >= across * (height // WIN - 1):
                weights = weights * allowed
            both = dot(weights.astype(BF16), jnp.concatenate([wide_v, member], axis=1))
            blended_ref[rows, lanes] = (both[:, :128] / both[:, 128:]).astype(BF16)

    projection = dot(blended_ref[...], proj_ref[...])
    branch, _ = normal_form(projection)
    hidden = displaced_f + branch * attn_gain_ref[...]
    hidden = hidden.reshape(height // WIN, across, WIN, WIN, width).transpose(0, 2, 1, 3, 4)
    hidden = hidden.reshape(tokens, width).astype(BF16)
    hidden_ref[...] = hidden
    normed, _ = normal_form(hidden.astype(F32))
    normed = (normed * moe_gain_ref[...]).astype(BF16)
    logits = dot_nt(normed, router_ref[...])
    chosen = iota((tokens, expert_total), 1) == col_ref[:, :1] // capacity
    gate = jax.nn.sigmoid(jnp.sum(jnp.where(chosen, logits, 0.0), axis=1, keepdims=True))
    gate_ref[...] = jnp.broadcast_to(gate, gate_ref.shape)
    placed = flag(iota((send_ref.shape[0], tokens), 0) == row_ref[...])
    send_ref[...] = dot(placed, normed).astype(BF16)


CHUNK = 512


def early_kernel(d_ref, w_out_ref, dact_ref):
    for start in range(0, w_out_ref.shape[1], CHUNK):
        part = slice(start, start + CHUNK)
        dact_ref[:, part] = dot(d_ref[...], w_out_ref[:, part])


def forward_kernel(index_ref, z_ref, w_in_ref, w_out_ref, router_ref, out_ref, act_ref, slope_ref, gate_ref):
    z = z_ref[...]
    total = None
    for start in range(0, w_in_ref.shape[1], CHUNK):
        part = slice(start, start + CHUNK)
        activation, slopes = gelu_parts(dot(z, w_in_ref[:, part]))
        activation = activation.astype(BF16)
        act_ref[:, part] = activation
        slope_ref[:, part] = slopes
        piece = dot_nt(activation, w_out_ref[:, part])
        total = piece if total is None else total + piece
    out_ref[...] = total.astype(BF16)
    logits = dot_nt(z, router_ref[...])
    mine = iota(logits.shape, 1) == index_ref[0]
    gate = jax.nn.sigmoid(jnp.sum(jnp.where(mine, logits, 0.0), axis=1, keepdims=True))
    gate_ref[...] = jnp.broadcast_to(gate, gate_ref.shape)


def backward_kernel(gate_ref, d_ref, dact_ref, slope_ref, w_in_ref, back_ref, dpre_ref, scaled_ref):
    gate = gate_ref[:, :1]
    scaled_ref[...] = (d_ref[...].astype(F32) * gate).astype(BF16)
    total = None
    for start in range(0, w_in_ref.shape[1], CHUNK):
        part = slice(start, start + CHUNK)
        dpre = (dact_ref[:, part] * gate * slope_ref[:, part]).astype(BF16)
        dpre_ref[:, part] = dpre
        piece = dot_nt(dpre, w_in_ref[:, part])
        total = piece if total is None else total + piece
    back_ref[...] = total.astype(BF16)


def grads_kernel(z_ref, dpre_ref, d_ref, act_ref, grad_ref):
    hidden_units = dpre_ref.shape[1]
    for start in range(0, hidden_units, CHUNK):
        part = slice(start, start + CHUNK)
        grad_ref[:, part] = dot_tn(z_ref[...], dpre_ref[:, part]).astype(BF16)
    for start in range(0, hidden_units, CHUNK):
        part = slice(start, start + CHUNK)
        later = slice(hidden_units + start, hidden_units + start + CHUNK)
        grad_ref[:, later] = dot_tn(d_ref[...], act_ref[:, part]).astype(BF16)


def picked(col_ref, slots_ref):
    tokens, total = col_ref.shape[0], slots_ref.shape[0]
    picks = flag(iota((tokens, total), 1) == col_ref[:, :1])
    return dot(picks, slots_ref[...])


def output_kernel(col_ref, back_ref, hidden_ref, gate_ref, cot_ref, block_ref, dlogit_ref):
    expert_out = picked(col_ref, back_ref)
    gate = gate_ref[:, :1]
    block_ref[...] = (hidden_ref[...].astype(F32) + gate * expert_out).astype(BF16)
    dgate = jnp.sum(cot_ref[...].astype(F32) * expert_out, axis=1, keepdims=True)
    dlogit_ref[...] = jnp.broadcast_to(dgate * gate * (1.0 - gate), dlogit_ref.shape)


def mixer_kernel(
    capacity, col_ref, back_ref, hidden_ref, dlogit_ref, cot_ref, router_ref, gain_ref, mixer_ref
):
    tokens = col_ref.shape[0]
    dnormed = picked(col_ref, back_ref)
    chosen = iota((tokens, router_ref.shape[0]), 1) == col_ref[:, :1] // capacity
    dnormed = dnormed + dlogit_ref[:, :1] * dot(flag(chosen), router_ref[...])
    xhat, inv_std = normal_form(hidden_ref[...].astype(F32))
    scaled = dnormed * gain_ref[...]
    first = jnp.mean(scaled, axis=-1, keepdims=True)
    second = jnp.mean(scaled * xhat, axis=-1, keepdims=True)
    mixer_ref[...] = cot_ref[...].astype(F32) + inv_std * (scaled - first - xhat * second)


def per_device(
    patches,
    patch_mask,
    mask_token,
    w_qkv,
    w_proj,
    logit_scale,
    rel_bias,
    attn_gain,
    moe_gain,
    router,
    expert_ids,
    w_in,
    w_out,
    cotangent,
):
    height, lateral, width = patches.shape
    tokens = height * lateral
    heads, window, _ = rel_bias.shape
    expert_total = router.shape[1]
    capacity = 2 * tokens // expert_total
    slot_total = expert_total * capacity
    w_in, w_out = w_in[0], w_out[0]
    units = w_in.shape[1]

    def rim(rows, columns):
        return jnp.where(
            patch_mask[rows, columns, None] == 1, mask_token[None, None, :], patches[rows, columns]
        )

    few, whole = slice(0, SHIFT), slice(None)
    right = passed_along(rim(whole, few).reshape(height * SHIFT, width), "lon", -1)
    low = passed_along(rim(few, whole).reshape(SHIFT * lateral, width), "lat", -1)
    corner = passed_diagonally(rim(few, few).reshape(SHIFT * SHIFT, width))

    cot = cotangent.reshape(tokens, width)
    router_t = router.T
    cot_send, target_row, target_col = call(
        lambda *refs: slot_kernel(expert_total, capacity, *refs),
        (
            shape((slot_total, width), BF16),
            shape((1, tokens), I32),
            shape((tokens, 128), I32),
        ),
        expert_ids.reshape(1, tokens),
        cot,
    )
    d_slots = exchanged(cot_send.reshape(expert_total, capacity, width)).reshape(slot_total, width)

    last = (lax.axis_index("lat") == lax.axis_size("lat") - 1).astype(I32).reshape(1)
    bias = rel_bias.transpose(1, 0, 2).reshape(window, heads * window)
    hidden, normed_send, gate = call(
        lambda *refs: attention_kernel(heads, *refs),
        (
            shape((tokens, width), BF16),
            shape((slot_total, width), BF16),
            shape((tokens, 128), F32),
        ),
        last,
        patches.reshape(tokens, width),
        patch_mask,
        mask_token.reshape(1, width),
        right,
        low,
        corner,
        w_qkv,
        w_proj,
        logit_scale.reshape(1, heads),
        bias,
        attn_gain.reshape(1, width),
        moe_gain.reshape(1, width),
        router_t,
        target_row,
        target_col,
        scratch=[pltpu.VMEM((tokens, width), BF16)],
        smem=(0,),
    )
    z_slots = exchanged(normed_send.reshape(expert_total, capacity, width)).reshape(
        slot_total, width
    )
    dact = call(early_kernel, shape((slot_total, units), F32), d_slots, w_out)
    outputs, activation, slopes, slot_gate = call(
        forward_kernel,
        (
            shape((slot_total, width), BF16),
            shape((slot_total, units), BF16),
            shape((slot_total, units), F32),
            shape((slot_total, 128), F32),
        ),
        lax.axis_index("lon").astype(I32).reshape(1),
        z_slots,
        w_in,
        w_out,
        router_t,
        smem=(0,),
    )
    out_back = exchanged(outputs.reshape(expert_total, capacity, width)).reshape(slot_total, width)
    dnormed, dpre, scaled = call(
        backward_kernel,
        (
            shape((slot_total, width), BF16),
            shape((slot_total, units), BF16),
            shape((slot_total, width), BF16),
        ),
        slot_gate,
        d_slots,
        dact,
        slopes,
        w_in,
    )
    dnormed_back = exchanged(dnormed.reshape(expert_total, capacity, width)).reshape(
        slot_total, width
    )
    grads = call(grads_kernel, shape((width, 2 * units), BF16), z_slots, dpre, scaled, activation)
    weight_grads = lax.psum_scatter(grads, "lat", scatter_dimension=0, tiled=True).astype(F32)
    block_out, dlogit = call(
        output_kernel,
        (shape((tokens, width), BF16), shape((tokens, 128), F32)),
        target_col,
        out_back,
        hidden,
        gate,
        cot,
    )
    mixer_grad = call(
        lambda *refs: mixer_kernel(capacity, *refs),
        shape((tokens, width), F32),
        target_col,
        dnormed_back,
        hidden,
        dlogit,
        cot,
        router_t,
        moe_gain.reshape(1, width),
    )
    return (
        block_out.reshape(height, lateral, width),
        mixer_grad.reshape(height, lateral, width),
        weight_grads.reshape(-1, 1, 2 * units),
    )


def solution(mesh):
    placed = (
        P("lat", "lon", None),
        P("lat", "lon"),
        P(),
        P(),
        P(),
        P(),
        P(),
        P(),
        P(),
        P(),
        P("lat", "lon", None, None),
        P("lon", None, None),
        P("lon", None, None),
        P("lat", "lon", None),
    )
    return jax.shard_map(
        per_device,
        mesh=mesh,
        in_specs=placed,
        out_specs=(P("lat", "lon", None), P("lat", "lon", None), P("lat", "lon", None)),
        check_vma=False,
    )
```

time: 262 us -> 211 us (0.81)
  Pallas kernels: 0 us -> 49.3 us
  matrix products: 41.1 us -> 0 us
  blocking collectives: 69.4 us -> 32.7 us
  local copies, waits for them, and re-layouts: 42.6 us -> 18 us
  starting transfers between devices: 19.7 us -> 35.3 us
  other arithmetic: 20.5 us -> 6.69 us
    pallas_call x0 -> x8, Pallas kernels: none -> 49.3 us  [call(): pl.pallas_call(body, out_shape=outs, in_specs=specs, out_specs=jax.tree.m...]
    dot_general x13 -> x0, matrix products: 41.1 us -> none  [the longest x1 7.05 us: per_device(): jnp.einsum('esd,edf->esf', d_slots, w_out, preferred_element_type=jnp.flo...]
    all_to_all x2 -> x1, blocking collectives: 69.4 us -> 32.7 us  [exchanged(): return lax.all_to_all(slots, 'lon', split_axis=0, concat_axis=0, tiled=True)]
    all_to_all x2 -> x3, starting transfers between devices: 11.2 us -> 28.5 us  [exchanged(): return lax.all_to_all(slots, 'lon', split_axis=0, concat_axis=0, tiled=True)]
    ppermute x0 -> x1, waiting for transfers between devices: none -> 8.52 us  [passed_diagonally(): return lax.ppermute(block, ('lat', 'lon'), route)]
    all_to_all x2 -> x3, waiting for transfers between devices: 51.9 us -> 43.8 us  [exchanged(): return lax.all_to_all(slots, 'lon', split_axis=0, concat_axis=0, tiled=True)]
    gather x2 -> x0, local copies, waits for them, and re-layouts: 8 us -> none  [the longest x1 4.01 us: per_device(): dnormed_exp = dnormed_back[targets].astype(jnp.float32)]
    scatter x2 -> x0, local copies, waits for them, and re-layouts: 7.9 us -> none  [per_device(): jnp.zeros((expert_total * capacity, channels), jnp.bfloat16).at[targets]]
  transfers between devices with their start and end apart: 5 -> 7, of which waited for: 4 -> 3; matrix products, arithmetic and copies ran while one was open for 8% -> 4% of each run, Pallas kernels for 0% -> 8%
where the time goes in v1:
time: 211 us; the launch traced here: 209 us
  waiting for transfers between devices  52.3 us (25%)
  Pallas kernels  49.3 us (23%)
  starting transfers between devices  35.3 us (17%)
  blocking collectives  32.7 us (15%)
  local copies, waits for them, and re-layouts  18 us (9%)
  between operations  14.2 us (7%)
  other arithmetic  6.69 us (3%)
    pallas_call x8, Pallas kernels, call(): pl.pallas_call(body, out_shape=outs, in_specs=specs, out_specs=jax.tree.m...  49.3 us
    all_to_all x3, waiting for transfers between devices, exchanged(): return lax.all_to_all(slots, 'lon', split_axis=0, concat_axis=0, tiled=True)  43.8 us
    all_to_all x1, blocking collectives, exchanged(): return lax.all_to_all(slots, 'lon', split_axis=0, concat_axis=0, tiled=True)  32.7 us
    all_to_all x3, starting transfers between devices, exchanged(): return lax.all_to_all(slots, 'lon', split_axis=0, concat_axis=0, tiled=True)  28.5 us
    unnamed x45, local copies, waits for them, and re-layouts  15.8 us
    ppermute x1, waiting for transfers between devices, passed_diagonally(): return lax.ppermute(block, ('lat', 'lon'), route)  8.52 us
    ppermute x2, starting transfers between devices, passed_along(): return lax.ppermute(block, axis, route)  5.28 us
  transfers between devices with their start and end apart: 7, of which 3 were waited for; matrix products, arithmetic and copies ran while one was open for 4% of the time, Pallas kernels for 8%

profile of v1, /device:TPU:6, one launch (start us, length us, event | category | flops | bytes accessed | tf_op | source)
XLA Modules:
  0.0 208.6 jit_solution(10079447971292333019)
XLA Ops:
  7.2 0.0 copy-start.3
  7.2 1.0 copy-done.3
  8.2 0.7 copy-done.19
  8.9 1.9 shard_map.157
  10.8 11.5 %all-to-all-start.2 = ((bf16[32,32,512]{2,1,0:T(8,128)(2,1)}), bf16[32,32,512]{2,1,0:T(8,128)(2,1)S(1)}, u32[]{:S(2)}, u32[]{:S(2)}) async-start(bf16[32,32,512]{2,1,0:T(8,128)(2,1)} %bitcast.18), calls=%async_computation.2 | async-start | bytes 2097152 | tf_op jit(solution)/shard_map/all_to_all | solution.py:94
  22.3 0.7 slice_compare_fusion
  23.0 1.0 slice_select_fusion.1
  24.1 5.3 %collective-permute-start = (bf16[64,512]{1,0:T(8,128)(2,1)S(1)}, bf16[64,512]{1,0:T(8,128)(2,1)S(1)}, u32[]{:S(2)}, u32[]{:S(2)}) collective-permute-start(bf16[64,512]{1,0:T(8,128)(2,1)S(1)} %reshape.98), channel_id=1, source_target_pairs={{1,0},{2,1},{3,2},{4,3},{5,4},{6,5},{7,6},{8,7},{9,8},{10,9},{11,1... | collective-permute-start | bytes 196616 | tf_op jit(solution)/shard_map/ppermute | solution.py:80
  29.3 0.7 slice_compare_fusion.2
  30.0 1.6 slice_select_fusion
  31.7 0.7 slice_compare_fusion.1
  32.4 0.8 slice_select_fusion.2
  33.2 1.3 collective-permute-start.2
  34.5 0.7 reshape.97.refs_3_
  35.2 1.3 copy.19
  36.6 0.2 reshape.102.refs_10_
  36.7 8.5 %collective-permute-done.2.refs_6_ = bf16[16,512]{1,0:T(8,128)(2,1)S(1)} collective-permute-done((bf16[16,512]{1,0:T(8,128)(2,1)S(1)}, bf16[16,512]{1,0:T(8,128)(2,1)S(1)}, u32[]{:S(2)}, u32[]{:S(2)}) %collective-permute-start.2) | collective-permute-done | bytes 16416 | tf_op jit(solution)/shard_map/ppermute | solution.py:90
  45.3 0.0 copy-start.5
  45.3 1.4 copy-done.5
  46.7 6.2 %shard_map.158 = (bf16[512,512]{1,0:T(8,128)(2,1)S(1)}, bf16[1024,512]{1,0:T(8,128)(2,1)S(1)}, f32[512,128]{1,0:T(8,128)S(1)}) custom-call(s32[1]{0:T(128)} %bitcast.3.refs_0_, bf16[512,512]{1,0:T(8,128)(2,1)S(1)} %bitcast.42, s32[16,32]{1,0:T(8,128)S(1)} %copy-done.17, bf16[1,512]{1,0:T(2,128)(2,1)S(1)} %reshape.97.refs_3_, ...), custom_call_target="tpu_custom_call" | custom-call | tf_op jit(solution)/shard_map/pallas_call | solution.py:21
  53.0 0.0 copy-start.7
  53.0 1.0 copy-done.7
  53.9 0.7 copy-done.13
  54.6 11.5 %all-to-all-start = ((bf16[32,32,512]{2,1,0:T(8,128)(2,1)}), bf16[32,32,512]{2,1,0:T(8,128)(2,1)S(1)}, u32[]{:S(2)}, u32[]{:S(2)}) async-start(bf16[32,32,512]{2,1,0:T(8,128)(2,1)} %bitcast.40), calls=%async_computation | async-start | bytes 2097152 | tf_op jit(solution)/shard_map/all_to_all | solution.py:94
  66.1 0.2 reduce-scatter.2.cloned.1.call-start
  66.3 0.0 copy-start.2
  66.3 1.6 copy-done.2
  67.9 5.6 %shard_map.161.dact_ref = f32[1024,2048]{1,0:T(8,128)} custom-call(bf16[1024,512]{1,0:T(8,128)(2,1)S(1)} %bitcast.28, bf16[512,2048]{1,0:T(8,128)(2,1)S(1)} %bitcast.33), custom_call_target="tpu_custom_call" | custom-call | tf_op jit(solution)/shard_map/pallas_call | solution.py:21
  73.5 20.7 %all-to-all-done = bf16[32,32,512]{2,1,0:T(8,128)(2,1)S(1)} async-done(((bf16[32,32,512]{2,1,0:T(8,128)(2,1)}), bf16[32,32,512]{2,1,0:T(8,128)(2,1)S(1)}, u32[]{:S(2)}, u32[]{:S(2)}) %all-to-all-start) | async-done | bytes 1048608 | tf_op jit(solution)/shard_map/all_to_all | solution.py:94
  94.2 1.6 copy-done
  95.8 11.6 %shard_map.159 = (bf16[1024,512]{1,0:T(8,128)(2,1)S(1)}, bf16[1024,2048]{1,0:T(8,128)(2,1)}, f32[1024,2048]{1,0:T(8,128)}, f32[1024,128]{1,0:T(8,128)S(1)}) custom-call(s32[1]{0:T(128)} %bitcast.2.index_ref, bf16[1024,512]{1,0:T(8,128)(2,1)S(1)} %bitcast.26, bf16[512,2048]{1,0:T(8,128)(2,1)S(1)} %bitcast.30, bf16[512,2048]{1,0:T(8,128)(2,1)} %bitcast.32, ...), custom_call_target="tpu_custom_call" | custom-call | tf_op jit(solution)/shard_map/pallas_call | solution.py:21
  107.4 1.0 copy-done.8
  108.4 9.5 %shard_map.162 = (bf16[1024,512]{1,0:T(8,128)(2,1)S(1)}, bf16[1024,2048]{1,0:T(8,128)(2,1)}, bf16[1024,512]{1,0:T(8,128)(2,1)S(1)}) custom-call(f32[1024,128]{1,0:T(8,128)S(1)} %get-tuple-element.25.gate_ref, bf16[1024,512]{1,0:T(8,128)(2,1)S(1)} %bitcast.29, f32[1024,2048]{1,0:T(8,128)} %shard_map.161.dact_ref, f32[1024,2048]{1,0:T(8,128)} %get-tuple-element.27.slope_ref, ...), custom_call_target="tpu_custom_call" | custom-call | tf_op jit(solution)/shard_map/pallas_call | solution.py:21
  117.9 1.0 copy-done.6
  118.8 10.2 %shard_map.164 = bf16[512,4096]{1,0:T(8,128)(2,1)} custom-call(bf16[1024,512]{1,0:T(8,128)(2,1)S(1)} %bitcast.27, bf16[1024,2048]{1,0:T(8,128)(2,1)} %get-tuple-element.30.dpre_ref, bf16[1024,512]{1,0:T(8,128)(2,1)S(1)} %get-tuple-element.31.d_ref, bf16[1024,2048]{1,0:T(8,128)(2,1)} %get-tuple-element.32.act_ref), custom_call_target="tpu_custom_call" | custom-call | tf_op jit(solution)/shard_map/pallas_call | solution.py:21
  129.0 0.0 reduce-scatter.2.cloned.1.call-update
  129.1 1.2 copy-done.9
  130.3 32.7 %all_to_all.20 = bf16[32,32,512]{2,1,0:T(8,128)(2,1)S(1)} all-to-all(bf16[32,32,512]{2,1,0:T(8,128)(2,1)S(1)} %bitcast.41), channel_id=1, replica_groups=mesh['lat'=8,'lon'=32] {'lon'}, dimensions={0} | all-to-all | bytes 2097152 | tf_op jit(solution)/shard_map/all_to_all | solution.py:94
  163.0 5.6 %all-to-all-start.3 = ((bf16[32,32,512]{2,1,0:T(8,128)(2,1)}), bf16[32,32,512]{2,1,0:T(8,128)(2,1)S(1)}, u32[]{:S(2)}, u32[]{:S(2)}) async-start(bf16[32,32,512]{2,1,0:T(8,128)(2,1)} %bitcast.39), calls=%async_computation.3 | async-start | bytes 2097152 | tf_op jit(solution)/shard_map/all_to_all | solution.py:94
  168.6 0.0 copy-start.14
  168.6 0.9 copy-done.14
  169.5 1.9 shard_map.160
  171.5 0.7 copy-done.15
  172.2 23.1 %all-to-all-done.3 = bf16[32,32,512]{2,1,0:T(8,128)(2,1)S(1)} async-done(((bf16[32,32,512]{2,1,0:T(8,128)(2,1)}), bf16[32,32,512]{2,1,0:T(8,128)(2,1)S(1)}, u32[]{:S(2)}, u32[]{:S(2)}) %all-to-all-start.3) | async-done | bytes 1048608 | tf_op jit(solution)/shard_map/all_to_all | solution.py:94
  195.3 0.9 copy-done.16
  196.2 2.4 %shard_map.163 = f32[512,512]{1,0:T(8,128)} custom-call(s32[512,128]{1,0:T(8,128)S(1)} %get-tuple-element.18.refs_15_.col_ref.refs_0_, bf16[1024,512]{1,0:T(8,128)(2,1)S(1)} %bitcast.37, bf16[512,512]{1,0:T(8,128)(2,1)S(1)} %get-tuple-element.22.hidden_ref.refs_2_, f32[512,128]{1,0:T(8,128)S(1)} %copy-done.16, bf16[512,512]{1,0:T(8,128)(2,1)S(1)} %bitcast.36, ...), custom_call_target="tpu_custom_call" | custom-call | tf_op jit(solution)/shard_map/pallas_call | solution.py:21
  198.6 1.1 bitcast_convert_fusion
  199.7 2.0 copy.20
  (33 shorter events, 0.1 us)
Async XLA Ops:
  7.2 38.1 %copy-start.21 = (f32[16]{0:T(128)S(1)}, f32[16]{0:T(128)}, u32[]{:S(2)}) copy-start(f32[16]{0:T(128)} %param.19) | copy-start | bytes 196
  7.2 38.1 %copy-start.18 = (f32[512]{0:T(512)S(1)}, f32[512]{0:T(512)}, u32[]{:S(2)}) copy-start(f32[512]{0:T(512)} %param.22) | copy-start | bytes 6148
  7.2 1.1 copy-start.3
  8.2 0.7 copy-start.19
  8.9 36.4 %copy-start.10 = (bf16[16,32,512]{2,1,0:T(8,128)(2,1)S(1)}, bf16[16,32,512]{2,1,0:T(8,128)(2,1)}, u32[]{:S(2)}) copy-start(bf16[16,32,512]{2,1,0:T(8,128)(2,1)} %param.14) | copy-start | bytes 1572868
  8.9 36.4 %copy-start.11 = (bf16[512,512]{1,0:T(8,128)(2,1)S(1)}, bf16[512,512]{1,0:T(8,128)(2,1)}, u32[]{:S(2)}) copy-start(bf16[512,512]{1,0:T(8,128)(2,1)} %refs_8_.1) | copy-start | bytes 1572868
  8.9 36.4 %copy-start.12 = (bf16[512,32]{0,1:T(8,128)(2,1)S(1)}, bf16[512,32]{0,1:T(8,128)(2,1)}, u32[]{:S(2)}) copy-start(bf16[512,32]{0,1:T(8,128)(2,1)} %param.23) | copy-start | bytes 98308
  8.9 36.4 %copy-start.17 = (s32[16,32]{1,0:T(8,128)S(1)}, s32[16,32]{1,0:T(8,128)}, u32[]{:S(2)}) copy-start(s32[16,32]{1,0:T(8,128)} %refs_2_.1) | copy-start | bytes 6148
  8.9 36.4 %copy-start.20 = (f32[512]{0:T(512)S(1)}, f32[512]{0:T(512)}, u32[]{:S(2)}) copy-start(f32[512]{0:T(512)} %param.21) | copy-start | bytes 6148
  10.8 43.8 %all-to-all-start.2 = ((bf16[32,32,512]{2,1,0:T(8,128)(2,1)}), bf16[32,32,512]{2,1,0:T(8,128)(2,1)S(1)}, u32[]{:S(2)}, u32[]{:S(2)}) async-start(bf16[32,32,512]{2,1,0:T(8,128)(2,1)} %bitcast.18), calls=%async_computation.2 | async-start | bytes 2097152 | tf_op jit(solution)/shard_map/all_to_all | solution.py:94
  24.1 21.2 %collective-permute-start = (bf16[64,512]{1,0:T(8,128)(2,1)S(1)}, bf16[64,512]{1,0:T(8,128)(2,1)S(1)}, u32[]{:S(2)}, u32[]{:S(2)}) collective-permute-start(bf16[64,512]{1,0:T(8,128)(2,1)S(1)} %reshape.98), channel_id=1, source_target_pairs={{1,0},{2,1},{3,2},{4,3},{5,4},{6,5},{7,6},{8,7},{9,8},{10,9},{11,1... | collective-permute-start | bytes 196616 | tf_op jit(solution)/shard_map/ppermute | solution.py:80
  31.7 13.6 %collective-permute-start.1 = (bf16[128,512]{1,0:T(8,128)(2,1)}, bf16[128,512]{1,0:T(8,128)(2,1)S(1)}, u32[]{:S(2)}, u32[]{:S(2)}) collective-permute-start(bf16[128,512]{1,0:T(8,128)(2,1)} %bitcast.5), channel_id=1, source_target_pairs={{32,0},{64,32},{96,64},{128,96},{160,128},{192,160},{224,192},{0,2... | collective-permute-start | bytes 393224 | tf_op jit(solution)/shard_map/ppermute | solution.py:80
  33.2 12.0 %collective-permute-start.2 = (bf16[16,512]{1,0:T(8,128)(2,1)S(1)}, bf16[16,512]{1,0:T(8,128)(2,1)S(1)}, u32[]{:S(2)}, u32[]{:S(2)}) collective-permute-start(bf16[16,512]{1,0:T(8,128)(2,1)S(1)} %reshape.100), channel_id=1, source_target_pairs={{33,0},{34,1},{35,2},{36,3},{37,4},{38,5},{39,6},{40,7},{41,8},{42... | collective-permute-start | bytes 49160 | tf_op jit(solution)/shard_map/ppermute | solution.py:90
  45.3 1.4 copy-start.5
  53.0 1.0 copy-start.7
  53.9 0.7 copy-start.13
  54.6 39.6 %all-to-all-start = ((bf16[32,32,512]{2,1,0:T(8,128)(2,1)}), bf16[32,32,512]{2,1,0:T(8,128)(2,1)S(1)}, u32[]{:S(2)}, u32[]{:S(2)}) async-start(bf16[32,32,512]{2,1,0:T(8,128)(2,1)} %bitcast.40), calls=%async_computation | async-start | bytes 2097152 | tf_op jit(solution)/shard_map/all_to_all | solution.py:94
  66.1 132.5 %reduce-scatter.2.cloned.1.call-start = ((), (), s32[]{:S(2)}) async-start(), calls=%async_computation.5 | async-start | bytes 4718592 | tf_op jit(solution)/shard_map/reduce_scatter | solution.py:417
  66.3 1.6 copy-start.2
  94.2 1.6 copy-start
  95.8 12.6 %copy-start.1 = (bf16[1,512,2048]{2,1,0:T(8,128)(2,1)S(1)}, bf16[1,512,2048]{2,1,0:T(8,128)(2,1)}, u32[]{:S(2)}) copy-start(bf16[1,512,2048]{2,1,0:T(8,128)(2,1)} %param.25) | copy-start | bytes 6291460
  107.4 1.0 copy-start.8
  117.9 1.0 copy-start.6
  129.0 1.2 copy-start.9
  129.0 39.5 %copy-start.4 = (bf16[16,32,512]{2,1,0:T(8,128)(2,1)S(1)}, bf16[16,32,512]{2,1,0:T(8,128)(2,1)}, u32[]{:S(2)}) copy-start(bf16[16,32,512]{2,1,0:T(8,128)(2,1)} %param.27) | copy-start | bytes 1572868
  163.0 32.3 %all-to-all-start.3 = ((bf16[32,32,512]{2,1,0:T(8,128)(2,1)}), bf16[32,32,512]{2,1,0:T(8,128)(2,1)S(1)}, u32[]{:S(2)}, u32[]{:S(2)}) async-start(bf16[32,32,512]{2,1,0:T(8,128)(2,1)} %bitcast.39), calls=%async_computation.3 | async-start | bytes 2097152 | tf_op jit(solution)/shard_map/all_to_all | solution.py:94
  168.6 1.0 copy-start.14
  171.5 0.7 copy-start.15
  195.3 1.0 copy-start.16
Sparse Core Ops, SparseCore 0:
  129.2 35.1 reduce-scatter.1

commit v2 on v1

v2 whole, which is shorter than its diff:
```python
import math

import jax
import jax.numpy as jnp
from jax import lax
from jax.experimental import pallas as pl
from jax.experimental.pallas import tpu as pltpu
from jax.sharding import PartitionSpec as P

WIN = 8
SHIFT = 4
BF16 = jnp.bfloat16
F32 = jnp.float32
I32 = jnp.int32


MIB = 1024 * 1024
WHOLE = pl.BlockSpec(memory_space=pltpu.VMEM)
SCALAR = pl.BlockSpec(memory_space=pltpu.SMEM)
FAR = pl.BlockSpec(memory_space=pltpu.HBM)
UNREAD = pl.BlockSpec(memory_space=pl.ANY)


def call(body, outs, ins, *operands, scratch=(), grid=(), out_specs=None, vmem=16, flops=0):
    if out_specs is None:
        out_specs = jax.tree.map(lambda _: WHOLE, outs)
    moved = sum(math.prod(x.shape) * x.dtype.itemsize for x in (*operands, *jax.tree.leaves(outs)))
    return pl.pallas_call(
        body,
        grid=grid,
        out_shape=outs,
        in_specs=list(ins),
        out_specs=out_specs,
        scratch_shapes=list(scratch),
        cost_estimate=pl.CostEstimate(
            flops=int(flops), transcendentals=0, bytes_accessed=int(moved)
        ),
        compiler_params=pltpu.CompilerParams(vmem_limit_bytes=vmem * MIB),
    )(*operands)


def shape(dims, dtype):
    return jax.ShapeDtypeStruct(dims, dtype)


def far(dims, dtype):
    return pltpu.HBM(dims, dtype)


def kept_far(array):
    return pltpu.with_memory_space_constraint(array, pltpu.HBM)


def slot_gates(slots, router_t, index):
    logits = dot_nt(slots, router_t)
    mine = iota(logits.shape, 1) == index
    return jax.nn.sigmoid(jnp.sum(jnp.where(mine, logits, 0.0), axis=1, keepdims=True))


def dot(a, b):
    return jnp.dot(a, b, preferred_element_type=F32)


def dot_nt(a, b):
    return lax.dot_general(a, b, (((1,), (1,)), ((), ())), preferred_element_type=F32)


def dot_tn(a, b):
    return lax.dot_general(a, b, (((0,), (0,)), ((), ())), preferred_element_type=F32)


def halves(values):
    high = values.astype(BF16)
    return high, (values - high.astype(F32)).astype(BF16)


def dot_split(values, ones):
    high, low = halves(values)
    return dot(high, ones) + dot(low, ones)


def iota(dims, axis):
    return lax.broadcasted_iota(I32, dims, axis)


def flag(condition):
    return jnp.where(condition, 1.0, 0.0).astype(BF16)


def normal_form(values):
    centred = values - jnp.mean(values, axis=-1, keepdims=True)
    inv_std = lax.rsqrt(jnp.mean(centred * centred, axis=-1, keepdims=True) + 1e-05)
    return centred * inv_std, inv_std


def doubled_gelu_parts(preact):
    scaled = preact * 0.7071067811865476
    doubled_cdf = 1.0 + lax.erf(scaled)
    bell = jnp.exp(-(scaled * scaled))
    return preact * doubled_cdf, doubled_cdf + preact * 0.7978845608028654 * bell


def passed_along(block, axis, distance):
    devices = range(lax.axis_size(axis))
    route = [((i - distance) % len(devices), i) for i in devices]
    return lax.ppermute(block, axis, route)


def passed_diagonally(block):
    rows, columns = lax.axis_size("lat"), lax.axis_size("lon")
    route = [
        ((i + 1) % rows * columns + (j + 1) % columns, i * columns + j)
        for i in range(rows)
        for j in range(columns)
    ]
    return lax.ppermute(block, ("lat", "lon"), route)


def exchanged(slots):
    return lax.all_to_all(slots, "lon", split_axis=0, concat_axis=0, tiled=True)


def send_rows(placed_rows, rows, staged_ref, out_ref, sems):
    copies = []
    for i in range(sems.shape[0]):
        step = out_ref.shape[0] // sems.shape[0]
        part = slice(i * step, (i + 1) * step)
        staged_ref[part] = dot(placed_rows(i * step, step), rows).astype(BF16)
        copies.append(pltpu.make_async_copy(staged_ref.at[part], out_ref.at[part], sems.at[i]))
        copies[-1].start()
    return copies


def slot_kernel(
    expert_total,
    capacity,
    masked_ref,
    ids_ref,
    cot_ref,
    send_ref,
    row_ref,
    col_ref,
    cots,
    staged,
    sem,
    sems,
):
    del masked_ref
    load = pltpu.make_async_copy(cot_ref, cots, sem.at[0])
    load.start()
    tokens = cot_ref.shape[0]
    ids = ids_ref[...]
    onehot = iota((expert_total, tokens), 0) == ids
    before = flag(iota((tokens, tokens), 0) < iota((tokens, tokens), 1))
    earlier = dot(flag(onehot), before)
    slot = jnp.sum(jnp.where(onehot, earlier, 0.0), axis=0, keepdims=True).astype(I32)
    target = ids * capacity + slot
    load.wait()
    copies = send_rows(
        lambda start, step: flag(iota((step, tokens), 0) + start == target),
        cots[...],
        staged,
        send_ref,
        sems,
    )
    row_ref[...] = target
    diagonal = iota((tokens, tokens), 0) == iota((tokens, tokens), 1)
    column = jnp.sum(jnp.where(diagonal, target, 0).astype(F32), axis=1, keepdims=True)
    col_ref[...] = jnp.broadcast_to(column.astype(I32), col_ref.shape)
    for copy in copies:
        copy.wait()


def mask_kernel(patches_ref, mask_ref, token_ref, masked_ref, right_ref, low_ref, corner_ref):
    tokens = patches_ref.shape[0]
    height, lateral = mask_ref.shape
    in_row = flag(iota((tokens, height), 0) // lateral == iota((tokens, height), 1))
    spread = dot(in_row, mask_ref[...].astype(F32).astype(BF16))
    own = iota((tokens, lateral), 0) % lateral == iota((tokens, lateral), 1)
    hidden_patch = jnp.sum(jnp.where(own, spread, 0.0), axis=1, keepdims=True)
    masked = jnp.where(
        hidden_patch > 0.5, token_ref[...].astype(F32), patches_ref[...].astype(F32)
    ).astype(BF16)
    masked_ref[...] = masked
    low_ref[...] = masked[: SHIFT * lateral]
    place = iota((height * SHIFT, tokens), 0)
    picks = flag(place // SHIFT * lateral + place % SHIFT == iota((height * SHIFT, tokens), 1))
    right = dot(picks, masked).astype(BF16)
    right_ref[...] = right
    corner_ref[...] = right[: SHIFT * SHIFT]


def attention_kernel(
    heads,
    height,
    lateral,
    flag_ref,
    masked_ref,
    right_ref,
    low_ref,
    corner_ref,
    qkv_ref,
    proj_ref,
    scale_ref,
    bias_ref,
    attn_gain_ref,
    moe_gain_ref,
    router_ref,
    row_ref,
    col_ref,
    hidden_ref,
    send_ref,
    gate_ref,
    blended_ref,
    staged,
    sems,
):
    tokens, width = masked_ref.shape
    features = width // heads
    window = WIN * WIN
    across = lateral // WIN
    group = 128 // features
    expert_total = router_ref.shape[0]
    capacity = send_ref.shape[0] // expert_total

    source = jnp.concatenate([masked_ref[...], right_ref[...], low_ref[...], corner_ref[...]], axis=0)

    place = iota((tokens, 1), 0)
    which, inside = place // window, place % window
    row = which // across * WIN + inside // WIN + SHIFT
    column = which % across * WIN + inside % WIN + SHIFT
    right_base = tokens
    low_base = right_base + height * SHIFT
    corner_base = low_base + SHIFT * lateral
    local = row * lateral + column
    from_right = right_base + row * SHIFT + column - lateral
    from_low = low_base + (row - height) * lateral + column
    from_corner = corner_base + (row - height) * SHIFT + column - lateral
    origin = jnp.where(
        row < height,
        jnp.where(column < lateral, local, from_right),
        jnp.where(column < lateral, from_low, from_corner),
    )
    moves = flag(iota((tokens, source.shape[0]), 1) == origin)
    displaced_f = dot(moves, source)
    displaced = displaced_f.astype(BF16)

    projected = dot(displaced, qkv_ref[...]).astype(BF16)
    head_of = flag(iota((width, heads), 0) // features == iota((width, heads), 1))
    of_head = flag(iota((heads, width), 1) // features == iota((heads, width), 0))
    queries = projected[:, :width].astype(F32)
    keys = projected[:, width : 2 * width].astype(F32)
    query_norm = lax.rsqrt(dot_split(queries * queries, head_of) + 1e-06) * scale_ref[...]
    key_norm = lax.rsqrt(dot_split(keys * keys, head_of) + 1e-06)
    queries = (queries * dot_split(query_norm, of_head)).astype(BF16)
    keys = (keys * dot_split(key_norm, of_head)).astype(BF16)

    block = group * window
    biases = [
        jnp.concatenate([bias_ref[g * group + i] for i in range(group)], axis=1)
        for g in range(width // 128)
    ]
    member = flag(
        iota((block, 128), 0) // window == iota((block, 128), 1) // features
    )
    split = (iota((window, block), 0) >= window // 2) == (
        iota((window, block), 1) % window >= window // 2
    )
    allowed = jnp.where(split, 1.0, jnp.where(flag_ref[0] == 1, 0.0, 1.0))
    for w in range(tokens // window):
        rows = slice(w * window, (w + 1) * window)
        for g in range(width // 128):
            lanes = slice(g * 128, (g + 1) * 128)
            q = queries[rows, lanes]
            k = keys[rows, lanes]
            v = projected[rows, 2 * width + g * 128 : 2 * width + (g + 1) * 128]
            wide_k = jnp.concatenate([k] * group, axis=0) * member
            wide_v = jnp.concatenate([v] * group, axis=0) * member
            scores = dot_nt(q, wide_k) + biases[g]
            weights = jnp.exp(scores)
            if w >= across * (height // WIN - 1):
                weights = weights * allowed
            both = dot(weights.astype(BF16), jnp.concatenate([wide_v, member], axis=1))
            blended_ref[rows, lanes] = (both[:, :128] / both[:, 128:]).astype(BF16)

    projection = dot(blended_ref[...], proj_ref[...])
    branch, _ = normal_form(projection)
    hidden = displaced_f + branch * attn_gain_ref[...]
    hidden = hidden.reshape(height // WIN, across, WIN, WIN, width).transpose(0, 2, 1, 3, 4)
    hidden = hidden.reshape(tokens, width).astype(BF16)
    hidden_ref[...] = hidden
    normed, _ = normal_form(hidden.astype(F32))
    normed = (normed * moe_gain_ref[...]).astype(BF16)
    copies = send_rows(
        lambda start, step: flag(iota((step, tokens), 0) + start == row_ref[...]),
        normed,
        staged,
        send_ref,
        sems,
    )
    logits = dot_nt(normed, router_ref[...])
    chosen = iota((tokens, expert_total), 1) == col_ref[:, :1] // capacity
    gate = jax.nn.sigmoid(jnp.sum(jnp.where(chosen, logits, 0.0), axis=1, keepdims=True))
    gate_ref[...] = jnp.broadcast_to(gate, gate_ref.shape)
    for copy in copies:
        copy.wait()


PARTS = 4


def early_kernel(d_ref, w_out_ref, dact_ref):
    dact_ref[...] = dot(d_ref[...], w_out_ref[...])


def expert_kernel(
    index_ref,
    z_ref,
    router_ref,
    w_in_ref,
    w_out_ref,
    dact_ref,
    back_ref,
    act_ref,
    dpre_ref,
    w_in,
    w_out,
    dact,
    act,
    dpre,
    back,
    load_sems,
    store_sems,
):
    rows, width = z_ref.shape
    units = w_in.shape[1]
    tile, chunk, piece = rows // PARTS, units // PARTS, width // 2

    def load(source, target, i):
        copy = pltpu.make_async_copy(source, target, load_sems.at[i])
        copy.start()
        return copy

    def tiled(i, step):
        return slice(i * step, (i + 1) * step)

    load_in = [
        load(w_in_ref.at[:, tiled(i, chunk)], w_in.at[:, tiled(i, chunk)], i) for i in range(PARTS)
    ]
    load_dact = [load(dact_ref.at[tiled(0, tile)], dact.at[tiled(0, tile)], PARTS)]
    load_out = load(w_out_ref, w_out, 2 * PARTS)
    load_dact += [
        load(dact_ref.at[tiled(i, tile)], dact.at[tiled(i, tile)], PARTS + i)
        for i in range(1, PARTS)
    ]
    half_gate = 0.5 * slot_gates(z_ref[...], router_ref[...], index_ref[0])
    stores = []

    def store(source, target):
        copy = pltpu.make_async_copy(source, target, store_sems.at[len(stores)])
        copy.start()
        stores.append(copy)

    for r in range(PARTS + 1):
        if r < PARTS:
            load_dact[r].wait()
        if r == 1:
            load_out.wait()
        here, last = tiled(r, tile), tiled(r - 1, tile)
        for c in range(PARTS):
            part = tiled(c, chunk)
            if r < PARTS:
                if r == 0:
                    load_in[c].wait()
                activation, slopes = doubled_gelu_parts(dot(z_ref[here], w_in[:, part]))
                act[here, part] = activation.astype(BF16)
                dpre[here, part] = (dact[here, part] * slopes).astype(BF16)
            if r > 0:
                half = tiled(c % 2, piece)
                if c < 2:
                    result = 0.5 * dot_nt(act[last], w_out[half])
                else:
                    result = half_gate[last] * dot_nt(dpre[last], w_in[half])
                back[last, tiled(c, piece)] = result.astype(BF16)
        if r < PARTS:
            store(act.at[here], act_ref.at[here])
            store(dpre.at[here], dpre_ref.at[here])
        if r > 0:
            store(back.at[last], back_ref.at[last])
    for copy in stores:
        copy.wait()


def grads_kernel(
    lat_total, index_ref, z_ref, d_ref, router_ref, dpre_ref, act_ref, keep_ref, give_ref, zt, dt
):
    width = z_ref.shape[1]
    rows = width // lat_total

    @pl.when(pl.program_id(0) == 0)
    def _():
        place = iota((width, 1), 0)
        half, step, inside = place // (width // 2), place % (width // 2) // rows, place % rows
        column, core = index_ref[1] // 2, index_ref[1] % 2
        block = (step + column) % (lat_total // 2) * 2 + (half + core) % 2
        moves = flag(iota((width, width), 1) == block * rows + inside)
        half_gate = 0.5 * slot_gates(z_ref[...], router_ref[...], index_ref[0])
        for slots_ref, turned in ((z_ref, zt), (d_ref, dt)):
            scaled = (slots_ref[...].astype(F32) * half_gate).astype(BF16)
            turned[...] = dot_nt(moves, scaled).astype(BF16)

    for i, (left, right) in enumerate(((zt, dpre_ref), (dt, act_ref))):
        total = dot(left[...], right[...]).astype(BF16)
        keep_ref[i] = total[: width // 2]
        give_ref[i] = total[width // 2 :]


def pair_kernel(keep_ref, given_ref, own_ref, up_ref, down_ref, up_part_ref, down_part_ref):
    rows = own_ref.shape[1]

    def total(i, step):
        part = slice(step * rows, (step + 1) * rows)
        return (keep_ref[i, part].astype(F32) + given_ref[i, part].astype(F32)).astype(BF16)

    for i in range(2):
        own_ref[i] = total(i, 0)
        up_ref[i] = total(i, 1)
        down_ref[i] = total(i, 3)
    up_part_ref[...] = total(0, 2)
    down_part_ref[...] = total(1, 2)


def relay_kernel(up_ref, down_ref, up_part_ref, down_part_ref, up_out_ref, down_out_ref):
    up_out_ref[0] = (up_ref[0].astype(F32) + up_part_ref[...].astype(F32)).astype(BF16)
    up_out_ref[1] = up_ref[1]
    down_out_ref[0] = down_ref[0]
    down_out_ref[1] = (down_ref[1].astype(F32) + down_part_ref[...].astype(F32)).astype(BF16)


def total_kernel(own_ref, up_ref, down_ref, out_ref):
    units = own_ref.shape[2]
    for i in range(2):
        total = own_ref[i].astype(F32) + up_ref[i].astype(F32) + down_ref[i].astype(F32)
        out_ref[:, 0, i * units : (i + 1) * units] = total


def final_kernel(
    capacity,
    grads_ref,
    col_ref,
    back_ref,
    hidden_ref,
    gate_ref,
    cot_ref,
    router_ref,
    gain_ref,
    block_ref,
    mixer_ref,
):
    del grads_ref
    tokens, width = hidden_ref.shape
    picks = flag(iota((tokens, back_ref.shape[0]), 1) == col_ref[:, :1])
    both = dot(picks, back_ref[...])
    expert_out, dnormed = both[:, :width], both[:, width:]
    gate, cot, hidden = gate_ref[:, :1], cot_ref[...].astype(F32), hidden_ref[...].astype(F32)
    block_ref[...] = (hidden + gate * expert_out).astype(BF16)
    dgate = jnp.sum(cot * expert_out, axis=1, keepdims=True)
    dlogit = dgate * gate * (1.0 - gate)
    chosen = flag(iota((tokens, router_ref.shape[0]), 1) == col_ref[:, :1] // capacity)
    dnormed = dnormed + dlogit * dot(chosen, router_ref[...])
    xhat, inv_std = normal_form(hidden)
    scaled = dnormed * gain_ref[...]
    first = jnp.mean(scaled, axis=-1, keepdims=True)
    second = jnp.mean(scaled * xhat, axis=-1, keepdims=True)
    mixer_ref[...] = cot + inv_std * (scaled - first - xhat * second)


def per_device(
    patches,
    patch_mask,
    mask_token,
    w_qkv,
    w_proj,
    logit_scale,
    rel_bias,
    attn_gain,
    moe_gain,
    router,
    expert_ids,
    w_in,
    w_out,
    cotangent,
):
    height, lateral, width = patches.shape
    tokens = height * lateral
    heads = rel_bias.shape[0]
    expert_total = router.shape[1]
    capacity = 2 * tokens // expert_total
    slot_total = expert_total * capacity
    w_in, w_out = w_in[0], w_out[0]
    units = w_in.shape[1]

    cot = cotangent.reshape(tokens, width)
    router_t = router.T
    dma = pltpu.SemaphoreType.DMA
    masked, right, low, corner = call(
        mask_kernel,
        (
            shape((tokens, width), BF16),
            shape((height * SHIFT, width), BF16),
            shape((SHIFT * lateral, width), BF16),
            shape((SHIFT * SHIFT, width), BF16),
        ),
        (WHOLE,) * 3,
        patches.reshape(tokens, width),
        patch_mask,
        mask_token.reshape(1, width),
    )
    right = passed_along(right, "lon", -1)
    low = passed_along(low, "lat", -1)
    corner = passed_diagonally(corner)

    cot_send, target_row, target_col = call(
        lambda *refs: slot_kernel(expert_total, capacity, *refs),
        (
            far((slot_total, width), BF16),
            shape((1, tokens), I32),
            shape((tokens, 128), I32),
        ),
        (UNREAD, WHOLE, FAR),
        masked,
        expert_ids.reshape(1, tokens),
        kept_far(cot),
        out_specs=(FAR, WHOLE, WHOLE),
        scratch=[
            pltpu.VMEM((tokens, width), BF16),
            pltpu.VMEM((slot_total, width), BF16),
            dma((1,)),
            dma((PARTS,)),
        ],
        flops=2 * slot_total * tokens * width,
    )
    d_slots = exchanged(cot_send.reshape(expert_total, capacity, width)).reshape(slot_total, width)

    last = (lax.axis_index("lat") == lax.axis_size("lat") - 1).astype(I32).reshape(1)
    hidden, normed_send, gate = call(
        lambda *refs: attention_kernel(heads, height, lateral, *refs),
        (
            shape((tokens, width), BF16),
            far((slot_total, width), BF16),
            shape((tokens, 128), F32),
        ),
        (SCALAR,) + (WHOLE,) * 13,
        last,
        masked,
        right,
        low,
        corner,
        w_qkv,
        w_proj,
        logit_scale.reshape(1, heads),
        rel_bias,
        attn_gain.reshape(1, width),
        moe_gain.reshape(1, width),
        router_t,
        target_row,
        target_col,
        out_specs=(WHOLE, FAR, WHOLE),
        scratch=[
            pltpu.VMEM((tokens, width), BF16),
            pltpu.VMEM((slot_total, width), BF16),
            dma((PARTS,)),
        ],
        vmem=28,
        flops=2 * tokens * width * (6 * width + slot_total),
    )
    z_slots = exchanged(normed_send.reshape(expert_total, capacity, width)).reshape(
        slot_total, width
    )
    chunk = units // PARTS
    dact = call(
        early_kernel,
        far((slot_total, units), F32),
        (WHOLE, pl.BlockSpec((width, chunk), lambda i: (0, i))),
        d_slots,
        kept_far(w_out),
        grid=(PARTS,),
        out_specs=pl.BlockSpec((slot_total, chunk), lambda i: (0, i)),
        flops=2 * slot_total * width * units,
    )
    index = jnp.stack([lax.axis_index("lon"), lax.axis_index("lat")]).astype(I32)
    back, activation, dpre = call(
        expert_kernel,
        (
            far((slot_total, 2 * width), BF16),
            far((slot_total, units), BF16),
            far((slot_total, units), BF16),
        ),
        (SCALAR, WHOLE, WHOLE, FAR, FAR, FAR),
        index,
        z_slots,
        router_t,
        kept_far(w_in),
        kept_far(w_out),
        dact,
        out_specs=(FAR, FAR, FAR),
        scratch=[
            pltpu.VMEM((width, units), BF16),
            pltpu.VMEM((width, units), BF16),
            pltpu.VMEM((slot_total, units), F32),
            pltpu.VMEM((slot_total, units), BF16),
            pltpu.VMEM((slot_total, units), BF16),
            pltpu.VMEM((slot_total, 2 * width), BF16),
            dma((2 * PARTS + 1,)),
            dma((3 * PARTS,)),
        ],
        vmem=40,
        flops=6 * slot_total * width * units,
    )
    back = exchanged(back.reshape(expert_total, capacity, 2 * width)).reshape(
        slot_total, 2 * width
    )

    lat_total = lax.axis_size("lat")
    rows = width // lat_total
    half = width // 2
    keep, give = call(
        lambda *refs: grads_kernel(lat_total, *refs),
        (shape((2, half, units), BF16),) * 2,
        (SCALAR, WHOLE, WHOLE, WHOLE) + (pl.BlockSpec((slot_total, chunk), lambda i: (0, i)),) * 2,
        index,
        z_slots,
        d_slots,
        router_t,
        dpre,
        activation,
        grid=(PARTS,),
        out_specs=(pl.BlockSpec((2, half, chunk), lambda i: (0, 0, i)),) * 2,
        scratch=[pltpu.VMEM((width, slot_total), BF16)] * 2,
        vmem=28,
        flops=4 * slot_total * width * units,
    )
    given = lax.ppermute(give, "lat", [(i, i ^ 1) for i in range(lat_total)])
    block, part = shape((2, rows, units), BF16), shape((rows, units), BF16)
    own, up, down, up_part, down_part = call(
        pair_kernel, (block, block, block, part, part), (WHOLE,) * 2, keep, given
    )
    up_part = passed_along(up_part, "lat", 2)
    down_part = passed_along(down_part, "lat", -2)
    up, down = call(relay_kernel, (block, block), (WHOLE,) * 4, up, down, up_part, down_part)
    up = passed_along(up, "lat", 2)
    down = passed_along(down, "lat", -2)
    weight_grads = call(
        total_kernel, far((rows, 1, 2 * units), F32), (WHOLE,) * 3, own, up, down
    )
    span = tokens // PARTS
    tall = pl.BlockSpec((span, width), lambda i: (i, 0))
    thin = pl.BlockSpec((span, 128), lambda i: (i, 0))
    block_out, mixer_grad = call(
        lambda *refs: final_kernel(capacity, *refs),
        (far((tokens, width), BF16), far((tokens, width), F32)),
        (UNREAD, thin, WHOLE, tall, thin, tall, WHOLE, WHOLE),
        weight_grads,
        target_col,
        back,
        hidden,
        gate,
        cot,
        router_t,
        moe_gain.reshape(1, width),
        grid=(PARTS,),
        out_specs=(tall, tall),
        flops=4 * slot_total * tokens * width,
    )
    return (
        block_out.reshape(height, lateral, width),
        mixer_grad.reshape(height, lateral, width),
        weight_grads,
    )


def solution(mesh):
    placed = (
        P("lat", "lon", None),
        P("lat", "lon"),
        P(),
        P(),
        P(),
        P(),
        P(),
        P(),
        P(),
        P(),
        P("lat", "lon", None, None),
        P("lon", None, None),
        P("lon", None, None),
        P("lat", "lon", None),
    )
    return jax.shard_map(
        per_device,
        mesh=mesh,
        in_specs=placed,
        out_specs=(P("lat", "lon", None), P("lat", "lon", None), P("lat", "lon", None)),
        check_vma=False,
    )
```

time: 211 us -> 173 us (0.82)
  blocking collectives: 32.7 us -> 0 us
  waiting for transfers between devices: 52.3 us -> 65.7 us
  between operations: 14.2 us -> 0.85 us
  other arithmetic: 6.69 us -> 0.08 us
  Pallas kernels: 49.3 us -> 44.2 us
  starting transfers between devices: 35.3 us -> 39.5 us
    all_to_all x1 -> x0, blocking collectives: 32.7 us -> none  [exchanged(): return lax.all_to_all(slots, 'lon', split_axis=0, concat_axis=0, tiled=True)]
    ppermute x2 -> x6, waiting for transfers between devices: 0.01 us -> 21 us  [passed_along(): return lax.ppermute(block, axis, route)]
    all_to_all x3, waiting for transfers between devices: 43.8 us -> 23.9 us  [exchanged(): return lax.all_to_all(slots, 'lon', split_axis=0, concat_axis=0, tiled=True)]
    ppermute x1, waiting for transfers between devices: 8.52 us -> 16.8 us  [passed_diagonally(): return lax.ppermute(block, ('lat', 'lon'), route)]
    pallas_call x8 -> x10, Pallas kernels: 49.3 us -> 44.2 us  [call(): pl.pallas_call(body, grid=grid, out_shape=outs, in_specs=list(ins), out_s...]
    ppermute x2 -> x6, starting transfers between devices: 5.28 us -> 9.5 us  [passed_along(): return lax.ppermute(block, axis, route)]
    ppermute x0 -> x1, waiting for transfers between devices: none -> 4.15 us  [per_device(): given = lax.ppermute(give, 'lat', [(i, i ^ 1) for i in range(lat_total)])]
    select_n x3 -> x0, other arithmetic: 3.49 us -> none  [rim(): jnp.where(patch_mask[rows, columns, None] == 1, mask_token[None, None, :]...]
  transfers between devices with their start and end apart: 7 -> 11, of which waited for: 3 -> 8; matrix products, arithmetic and copies ran while one was open for 4% -> 0% of each run, Pallas kernels for 8% -> 15%
where the time goes in v2:
time: 173 us; the launch traced here: 170 us
  waiting for transfers between devices  65.7 us (38%)
  Pallas kernels  44.2 us (26%)
  starting transfers between devices  39.5 us (23%)
  local copies, waits for them, and re-layouts  19.8 us (11%)
    pallas_call x10, Pallas kernels, call(): pl.pallas_call(body, grid=grid, out_shape=outs, in_specs=list(ins), out_s...  44.2 us
    all_to_all x3, starting transfers between devices, exchanged(): return lax.all_to_all(slots, 'lon', split_axis=0, concat_axis=0, tiled=True)  29 us
    all_to_all x3, waiting for transfers between devices, exchanged(): return lax.all_to_all(slots, 'lon', split_axis=0, concat_axis=0, tiled=True)  23.9 us
    ppermute x6, waiting for transfers between devices, passed_along(): return lax.ppermute(block, axis, route)  21 us
    unnamed x48, local copies, waits for them, and re-layouts  19.1 us
    ppermute x1, waiting for transfers between devices, passed_diagonally(): return lax.ppermute(block, ('lat', 'lon'), route)  16.8 us
    ppermute x6, starting transfers between devices, passed_along(): return lax.ppermute(block, axis, route)  9.5 us
    ppermute x1, waiting for transfers between devices, per_device(): given = lax.ppermute(give, 'lat', [(i, i ^ 1) for i in range(lat_total)])  4.15 us
  transfers between devices with their start and end apart: 11, of which 8 were waited for; matrix products, arithmetic and copies ran while one was open for 0% of the time, Pallas kernels for 15%

profile of v2, /device:TPU:6, one launch (start us, length us, event | category | flops | bytes accessed | tf_op | source)
XLA Modules:
  0.0 170.2 jit_solution(12559036009291574084)
XLA Ops:
  0.6 0.7 reshape.60.token_ref
  1.3 1.0 copy-done.7
  2.4 0.7 copy-done.11
  3.1 0.5 shard_map.157
  3.5 0.0 copy-start.18
  3.5 0.6 copy-done.18
  4.2 0.0 copy-start.19
  4.2 0.8 copy-done.19
  5.0 2.5 %shard_map.158 = (bf16[1024,512]{1,0:T(8,128)(2,1)}, s32[1,512]{1,0:T(1,128)S(1)}, s32[512,128]{1,0:T(8,128)S(1)}) custom-call(bf16[512,512]{1,0:T(8,128)(2,1)S(1)} %get-tuple-element.27.refs_0_.refs_1_, s32[1,512]{1,0:T(1,128)S(1)} %bitcast.34, bf16[512,512]{1,0:T(8,128)(2,1)} %bitcast.25), custom_call_target="tpu_custom_call" | custom-call | flops 536870912 | bytes 2363392 | tf_op jit(solution)/shard_map/pallas_call | solution.py:28
  7.6 0.8 copy-done.16
  8.3 11.5 %all-to-all-start.1 = ((bf16[32,32,512]{2,1,0:T(8,128)(2,1)}), bf16[32,32,512]{2,1,0:T(8,128)(2,1)S(1)}, u32[]{:S(2)}, u32[]{:S(2)}) async-start(bf16[32,32,512]{2,1,0:T(8,128)(2,1)} %bitcast.40), calls=%async_computation.1 | async-start | bytes 2097152 | tf_op jit(solution)/shard_map/all_to_all | solution.py:120
  19.8 0.0 collective-permute-start.1
  19.9 5.3 %collective-permute-start = (bf16[64,512]{1,0:T(8,128)(2,1)S(1)}, bf16[64,512]{1,0:T(8,128)(2,1)}, u32[]{:S(2)}, u32[]{:S(2)}) collective-permute-start(bf16[64,512]{1,0:T(8,128)(2,1)S(1)} %get-tuple-element.28), channel_id=1, source_target_pairs={{1,0},{2,1},{3,2},{4,3},{5,4},{6,5},{7,6},{8,7},{9,8},{10,9},{11,1... | collective-permute-start | bytes 196616 | tf_op jit(solution)/shard_map/ppermute | solution.py:106
  25.1 0.9 collective-permute-start.2
  26.0 16.8 %collective-permute-done.2.refs_4_ = bf16[16,512]{1,0:T(8,128)(2,1)S(1)} collective-permute-done((bf16[16,512]{1,0:T(8,128)(2,1)S(1)}, bf16[16,512]{1,0:T(8,128)(2,1)S(1)}, u32[]{:S(2)}, u32[]{:S(2)}) %collective-permute-start.2) | collective-permute-done | bytes 16416 | tf_op jit(solution)/shard_map/ppermute | solution.py:116
  42.8 1.0 copy-done.15
  43.9 1.0 copy-done.17
  44.9 7.6 %shard_map.159 = (bf16[512,512]{1,0:T(8,128)(2,1)S(1)}, bf16[1024,512]{1,0:T(8,128)(2,1)}, f32[512,128]{1,0:T(8,128)S(1)}) custom-call(s32[1]{0:T(128)} %bitcast.2.refs_0_, bf16[512,512]{1,0:T(8,128)(2,1)S(1)} %copy-done.17, bf16[64,512]{1,0:T(8,128)(2,1)} %collective-permute-done.refs_2_, bf16[128,512]{1,0:T(8,128)(2,1)} %collective-permute-done.1.refs_3_, ...), custom_call_target="tpu_custom_call" | custom-call | flops 2147483648 | bytes 5232708 | tf_op jit(solution)/shard_map/pallas_call | solution.py:28
  52.5 0.8 copy-done.5
  53.3 0.7 copy-done.8
  54.0 11.8 %all-to-all-start = ((bf16[32,32,512]{2,1,0:T(8,128)(2,1)}), bf16[32,32,512]{2,1,0:T(8,128)(2,1)S(1)}, u32[]{:S(2)}, u32[]{:S(2)}) async-start(bf16[32,32,512]{2,1,0:T(8,128)(2,1)} %bitcast.41), calls=%async_computation | async-start | bytes 2097152 | tf_op jit(solution)/shard_map/all_to_all | solution.py:120
  65.8 0.1 pad_add_fusion.index_ref.refs_0_
  65.9 6.5 %shard_map.160.dact_ref = f32[1024,2048]{1,0:T(8,128)} custom-call(bf16[1024,512]{1,0:T(8,128)(2,1)S(1)} %bitcast.21, bf16[512,2048]{1,0:T(8,128)(2,1)} %bitcast.38), custom_call_target="tpu_custom_call" | custom-call | flops 2147483648 | bytes 11534336 | tf_op jit(solution)/shard_map/pallas_call | solution.py:28
  72.4 21.3 %all-to-all-done = bf16[32,32,512]{2,1,0:T(8,128)(2,1)S(1)} async-done(((bf16[32,32,512]{2,1,0:T(8,128)(2,1)}), bf16[32,32,512]{2,1,0:T(8,128)(2,1)S(1)}, u32[]{:S(2)}, u32[]{:S(2)}) %all-to-all-start) | async-done | bytes 1048608 | tf_op jit(solution)/shard_map/all_to_all | solution.py:120
  93.7 3.8 %copy-done = f32[1024,2048]{1,0:T(8,128)S(1)} copy-done((f32[1024,2048]{1,0:T(8,128)S(1)}, f32[1024,2048]{1,0:T(8,128)}, u32[]{:S(2)}) %copy-start) | copy-done | bytes 8388632
  97.5 13.0 %shard_map.161 = (bf16[1024,1024]{1,0:T(8,128)(2,1)}, bf16[1024,2048]{1,0:T(8,128)(2,1)}, bf16[1024,2048]{1,0:T(8,128)(2,1)}) custom-call(s32[2]{0:T(128)S(1)} %pad_add_fusion.index_ref.refs_0_, bf16[1024,512]{1,0:T(8,128)(2,1)S(1)} %bitcast.23, bf16[32,512]{1,0:T(8,128)(2,1)S(1)} %bitcast.29, bf16[512,2048]{1,0:T(8,128)(2,1)} %bitcast.42, ...), custom_call_target="tpu_custom_call" | custom-call | flops 6442450944 | bytes 24150024 | tf_op jit(solution)/shard_map/pallas_call | solution.py:28
  110.5 5.8 %all-to-all-start.2 = ((bf16[32,32,1024]{2,1,0:T(8,128)(2,1)}), bf16[32,32,1024]{2,1,0:T(8,128)(2,1)S(1)}, u32[]{:S(2)}, u32[]{:S(2)}) async-start(bf16[32,32,1024]{2,1,0:T(8,128)(2,1)} %bitcast.37), calls=%async_computation.2 | async-start | bytes 4194304 | tf_op jit(solution)/shard_map/all_to_all | solution.py:120
  116.3 1.2 copy-done.3
  117.5 2.2 %copy-done.22 = bf16[1024,2048]{1,0:T(8,128)(2,1)S(1)} copy-done((bf16[1024,2048]{1,0:T(8,128)(2,1)S(1)}, bf16[1024,2048]{1,0:T(8,128)(2,1)}, u32[]{:S(2)}) %copy-start.22) | copy-done | bytes 4194328
  119.7 2.2 %copy-done.23 = bf16[1024,2048]{1,0:T(8,128)(2,1)S(1)} copy-done((bf16[1024,2048]{1,0:T(8,128)(2,1)S(1)}, bf16[1024,2048]{1,0:T(8,128)(2,1)}, u32[]{:S(2)}) %copy-start.23) | copy-done | bytes 4194328
  121.9 8.7 %shard_map.162 = (bf16[2,256,2048]{2,1,0:T(8,128)(2,1)S(1)}, bf16[2,256,2048]{2,1,0:T(8,128)(2,1)S(1)}) custom-call(s32[2]{0:T(128)S(1)} %pad_add_fusion.index_ref.refs_0_, bf16[1024,512]{1,0:T(8,128)(2,1)S(1)} %bitcast.24, bf16[1024,512]{1,0:T(8,128)(2,1)S(1)} %bitcast.22, bf16[32,512]{1,0:T(8,128)(2,1)S(1)} %bitcast.30, bf16[1024,2048]{1,0:T(8,128)(2,1)S(1)} %copy-done.23, ...), custom_call_target="tpu_custom_call" | custom-call | flops 4294967296 | bytes 14712840 | tf_op jit(solution)/shard_map/pallas_call | solution.py:28
  130.6 0.1 collective-permute-start.3
  130.7 4.1 %collective-permute-done.3.given_ref = bf16[2,256,2048]{2,1,0:T(8,128)(2,1)S(1)} collective-permute-done((bf16[2,256,2048]{2,1,0:T(8,128)(2,1)S(1)}, bf16[2,256,2048]{2,1,0:T(8,128)(2,1)S(1)}, u32[]{:S(2)}, u32[]{:S(2)}) %collective-permute-start.3) | collective-permute-done | bytes 2097184 | tf_op jit(solution)/shard_map/ppermute | solution.py:643
  134.8 0.5 shard_map.163
  135.3 1.5 collective-permute-start.4
  136.8 0.6 collective-permute-start.5
  137.4 6.3 %collective-permute-done.4.up_part_ref = bf16[64,2048]{1,0:T(8,128)(2,1)S(1)} collective-permute-done((bf16[64,2048]{1,0:T(8,128)(2,1)S(1)}, bf16[64,2048]{1,0:T(8,128)(2,1)S(1)}, u32[]{:S(2)}, u32[]{:S(2)}) %collective-permute-start.4) | collective-permute-done | bytes 262176 | tf_op jit(solution)/shard_map/ppermute | solution.py:106
  143.7 2.3 %collective-permute-done.5.down_part_ref = bf16[64,2048]{1,0:T(8,128)(2,1)S(1)} collective-permute-done((bf16[64,2048]{1,0:T(8,128)(2,1)S(1)}, bf16[64,2048]{1,0:T(8,128)(2,1)S(1)}, u32[]{:S(2)}, u32[]{:S(2)}) %collective-permute-start.5) | collective-permute-done | bytes 262176 | tf_op jit(solution)/shard_map/ppermute | solution.py:106
  146.1 0.1 shard_map.164
  146.2 0.4 collective-permute-start.6
  146.6 1.7 %collective-permute-start.7 = (bf16[2,64,2048]{2,1,0:T(8,128)(2,1)S(1)}, bf16[2,64,2048]{2,1,0:T(8,128)(2,1)S(1)}, u32[]{:S(2)}, u32[]{:S(2)}) collective-permute-start(bf16[2,64,2048]{2,1,0:T(8,128)(2,1)S(1)} %get-tuple-element.45), channel_id=1, source_target_pairs={{64,0},{96,32},{128,64},{160,96},{192,128},{224,160},{0,192},{32,2... | collective-permute-start | bytes 1572872 | tf_op jit(solution)/shard_map/ppermute | solution.py:106
  148.3 10.8 %collective-permute-done.6.up_ref = bf16[2,64,2048]{2,1,0:T(8,128)(2,1)S(1)} collective-permute-done((bf16[2,64,2048]{2,1,0:T(8,128)(2,1)S(1)}, bf16[2,64,2048]{2,1,0:T(8,128)(2,1)S(1)}, u32[]{:S(2)}, u32[]{:S(2)}) %collective-permute-start.6) | collective-permute-done | bytes 524320 | tf_op jit(solution)/shard_map/ppermute | solution.py:106
  159.1 1.5 collective-permute-done.7.down_ref
  160.6 1.3 shard_map.165.refs_0_
  161.9 2.5 %all-to-all-done.2 = bf16[32,32,1024]{2,1,0:T(8,128)(2,1)S(1)} async-done(((bf16[32,32,1024]{2,1,0:T(8,128)(2,1)}), bf16[32,32,1024]{2,1,0:T(8,128)(2,1)S(1)}, u32[]{:S(2)}, u32[]{:S(2)}) %all-to-all-start.2) | async-done | bytes 2097184 | tf_op jit(solution)/shard_map/all_to_all | solution.py:120
  164.5 1.2 copy-done.1
  165.7 0.9 copy-done.9
  166.7 3.5 %shard_map.166 = (bf16[512,512]{1,0:T(8,128)(2,1)}, f32[512,512]{1,0:T(8,128)}) custom-call(f32[64,1,4096]{2,1,0:T(1,128)S(1)} %copy-done.1, s32[512,128]{1,0:T(8,128)S(1)} %get-tuple-element.32.refs_13_.refs_1_, bf16[1024,1024]{1,0:T(8,128)(2,1)S(1)} %bitcast.20, bf16[512,512]{1,0:T(8,128)(2,1)S(1)} %copy-done.6, f32[512,128]{1,0:T(8,128)S(1)} %copy-done.9, ...), custom_call_target="tpu_custom_call" | custom-call | flops 1073741824 | bytes 6326272 | tf_op jit(solution)/shard_map/pallas_call | solution.py:28
  (34 shorter events, 0.1 us)
Async XLA Ops:
  1.3 1.0 copy-start.7
  2.4 0.7 copy-start.11
  3.1 39.7 %copy-start.20 = (f32[512]{0:T(512)S(1)}, f32[512]{0:T(512)}, u32[]{:S(2)}) copy-start(f32[512]{0:T(512)} %param.21) | copy-start | bytes 6148
  3.1 39.7 %copy-start.21 = (f32[16]{0:T(128)S(1)}, f32[16]{0:T(128)}, u32[]{:S(2)}) copy-start(f32[16]{0:T(128)} %param.19) | copy-start | bytes 196
  3.5 0.7 copy-start.18
  4.2 38.6 %copy-start.10 = (bf16[512,32]{0,1:T(8,128)(2,1)S(1)}, bf16[512,32]{0,1:T(8,128)(2,1)}, u32[]{:S(2)}) copy-start(bf16[512,32]{0,1:T(8,128)(2,1)} %param.23) | copy-start | bytes 98308
  4.2 38.6 %copy-start.12 = (f32[512]{0:T(512)S(1)}, f32[512]{0:T(512)}, u32[]{:S(2)}) copy-start(f32[512]{0:T(512)} %param.22) | copy-start | bytes 6148
  4.2 38.6 %copy-start.13 = (bf16[512,1536]{1,0:T(8,128)(2,1)S(1)}, bf16[512,1536]{1,0:T(8,128)(2,1)}, u32[]{:S(2)}) copy-start(bf16[512,1536]{1,0:T(8,128)(2,1)} %refs_5_.1) | copy-start | bytes 4718596
  4.2 38.6 %copy-start.14 = (bf16[512,512]{1,0:T(8,128)(2,1)S(1)}, bf16[512,512]{1,0:T(8,128)(2,1)}, u32[]{:S(2)}) copy-start(bf16[512,512]{1,0:T(8,128)(2,1)} %refs_6_.1) | copy-start | bytes 1572868
  4.2 0.8 copy-start.19
  7.5 0.8 copy-start.16
  8.3 45.7 %all-to-all-start.1 = ((bf16[32,32,512]{2,1,0:T(8,128)(2,1)}), bf16[32,32,512]{2,1,0:T(8,128)(2,1)S(1)}, u32[]{:S(2)}, u32[]{:S(2)}) async-start(bf16[32,32,512]{2,1,0:T(8,128)(2,1)} %bitcast.40), calls=%async_computation.1 | async-start | bytes 2097152 | tf_op jit(solution)/shard_map/all_to_all | solution.py:120
  19.8 22.9 %collective-permute-start.1 = (bf16[128,512]{1,0:T(8,128)(2,1)}, bf16[128,512]{1,0:T(8,128)(2,1)}, u32[]{:S(2)}, u32[]{:S(2)}) collective-permute-start(bf16[128,512]{1,0:T(8,128)(2,1)} %copy-done.18), channel_id=1, source_target_pairs={{32,0},{64,32},{96,64},{128,96},{160,128},{192,160},{224,192},{0,2... | collective-permute-start | bytes 393224 | tf_op jit(solution)/shard_map/ppermute | solution.py:106
  19.9 22.9 %collective-permute-start = (bf16[64,512]{1,0:T(8,128)(2,1)S(1)}, bf16[64,512]{1,0:T(8,128)(2,1)}, u32[]{:S(2)}, u32[]{:S(2)}) collective-permute-start(bf16[64,512]{1,0:T(8,128)(2,1)S(1)} %get-tuple-element.28), channel_id=1, source_target_pairs={{1,0},{2,1},{3,2},{4,3},{5,4},{6,5},{7,6},{8,7},{9,8},{10,9},{11,1... | collective-permute-start | bytes 196616 | tf_op jit(solution)/shard_map/ppermute | solution.py:106
  25.1 17.6 %collective-permute-start.2 = (bf16[16,512]{1,0:T(8,128)(2,1)S(1)}, bf16[16,512]{1,0:T(8,128)(2,1)S(1)}, u32[]{:S(2)}, u32[]{:S(2)}) collective-permute-start(bf16[16,512]{1,0:T(8,128)(2,1)S(1)} %get-tuple-element.30), channel_id=1, source_target_pairs={{33,0},{34,1},{35,2},{36,3},{37,4},{38,5},{39,6},{40,7},{41,8},{42... | collective-permute-start | bytes 49160 | tf_op jit(solution)/shard_map/ppermute | solution.py:116
  42.8 1.0 copy-start.15
  43.9 1.0 copy-start.17
  52.5 0.8 copy-start.5
  53.3 0.7 copy-start.8
  54.0 39.7 %all-to-all-start = ((bf16[32,32,512]{2,1,0:T(8,128)(2,1)}), bf16[32,32,512]{2,1,0:T(8,128)(2,1)S(1)}, u32[]{:S(2)}, u32[]{:S(2)}) async-start(bf16[32,32,512]{2,1,0:T(8,128)(2,1)} %bitcast.41), calls=%async_computation | async-start | bytes 2097152 | tf_op jit(solution)/shard_map/all_to_all | solution.py:120
  93.7 16.8 %copy-start.2 = (bf16[32,32,512]{2,1,0:T(8,128)(2,1)}, bf16[32,32,512]{2,1,0:T(8,128)(2,1)S(1)}, u32[]{:S(2)}) copy-start(bf16[32,32,512]{2,1,0:T(8,128)(2,1)S(1)} %all-to-all-done) | copy-start | bytes 3145732
  93.7 3.8 %copy-start = (f32[1024,2048]{1,0:T(8,128)S(1)}, f32[1024,2048]{1,0:T(8,128)}, u32[]{:S(2)}) copy-start(f32[1024,2048]{1,0:T(8,128)} %shard_map.160.dact_ref) | copy-start | bytes 25165828
  110.5 54.0 %all-to-all-start.2 = ((bf16[32,32,1024]{2,1,0:T(8,128)(2,1)}), bf16[32,32,1024]{2,1,0:T(8,128)(2,1)S(1)}, u32[]{:S(2)}, u32[]{:S(2)}) async-start(bf16[32,32,1024]{2,1,0:T(8,128)(2,1)} %bitcast.37), calls=%async_computation.2 | async-start | bytes 4194304 | tf_op jit(solution)/shard_map/all_to_all | solution.py:120
  116.3 1.2 copy-start.3
  117.5 2.2 %copy-start.22 = (bf16[1024,2048]{1,0:T(8,128)(2,1)S(1)}, bf16[1024,2048]{1,0:T(8,128)(2,1)}, u32[]{:S(2)}) copy-start(bf16[1024,2048]{1,0:T(8,128)(2,1)} %get-tuple-element.36.refs_5_) | copy-start | bytes 12582916
  119.7 2.2 %copy-start.23 = (bf16[1024,2048]{1,0:T(8,128)(2,1)S(1)}, bf16[1024,2048]{1,0:T(8,128)(2,1)}, u32[]{:S(2)}) copy-start(bf16[1024,2048]{1,0:T(8,128)(2,1)} %get-tuple-element.35.refs_4_) | copy-start | bytes 12582916
  130.6 4.2 %collective-permute-start.3 = (bf16[2,256,2048]{2,1,0:T(8,128)(2,1)S(1)}, bf16[2,256,2048]{2,1,0:T(8,128)(2,1)S(1)}, u32[]{:S(2)}, u32[]{:S(2)}) collective-permute-start(bf16[2,256,2048]{2,1,0:T(8,128)(2,1)S(1)} %get-tuple-element.38), channel_id=1, source_target_pairs={{0,32},{32,0},{64,96},{96,64},{128,160},{160,128},{192,224},{224,1... | collective-permute-start | bytes 6291464 | tf_op jit(solution)/shard_map/ppermute | solution.py:643
  135.3 8.4 %collective-permute-start.4 = (bf16[64,2048]{1,0:T(8,128)(2,1)S(1)}, bf16[64,2048]{1,0:T(8,128)(2,1)S(1)}, u32[]{:S(2)}, u32[]{:S(2)}) collective-permute-start(bf16[64,2048]{1,0:T(8,128)(2,1)S(1)} %get-tuple-element.42), channel_id=1, source_target_pairs={{192,0},{224,32},{0,64},{32,96},{64,128},{96,160},{128,192},{160,2... | collective-permute-start | bytes 786440 | tf_op jit(solution)/shard_map/ppermute | solution.py:106
  136.8 9.3 %collective-permute-start.5 = (bf16[64,2048]{1,0:T(8,128)(2,1)S(1)}, bf16[64,2048]{1,0:T(8,128)(2,1)S(1)}, u32[]{:S(2)}, u32[]{:S(2)}) collective-permute-start(bf16[64,2048]{1,0:T(8,128)(2,1)S(1)} %get-tuple-element.43), channel_id=1, source_target_pairs={{64,0},{96,32},{128,64},{160,96},{192,128},{224,160},{0,192},{32,2... | collective-permute-start | bytes 786440 | tf_op jit(solution)/shard_map/ppermute | solution.py:106
  146.1 18.4 %copy-start.4 = (bf16[16,32,512]{2,1,0:T(8,128)(2,1)S(1)}, bf16[16,32,512]{2,1,0:T(8,128)(2,1)}, u32[]{:S(2)}) copy-start(bf16[16,32,512]{2,1,0:T(8,128)(2,1)} %param.27) | copy-start | bytes 1572868
  146.1 18.4 %copy-start.6 = (bf16[512,512]{1,0:T(8,128)(2,1)S(1)}, bf16[512,512]{1,0:T(8,128)(2,1)}, u32[]{:S(2)}) copy-start(bf16[512,512]{1,0:T(8,128)(2,1)} %copy-done.5) | copy-start | bytes 1572868
  146.2 12.9 %collective-permute-start.6 = (bf16[2,64,2048]{2,1,0:T(8,128)(2,1)S(1)}, bf16[2,64,2048]{2,1,0:T(8,128)(2,1)S(1)}, u32[]{:S(2)}, u32[]{:S(2)}) collective-permute-start(bf16[2,64,2048]{2,1,0:T(8,128)(2,1)S(1)} %get-tuple-element.44), channel_id=1, source_target_pairs={{192,0},{224,32},{0,64},{32,96},{64,128},{96,160},{128,192},{160,2... | collective-permute-start | bytes 1572872 | tf_op jit(solution)/shard_map/ppermute | solution.py:106
  146.6 14.1 %collective-permute-start.7 = (bf16[2,64,2048]{2,1,0:T(8,128)(2,1)S(1)}, bf16[2,64,2048]{2,1,0:T(8,128)(2,1)S(1)}, u32[]{:S(2)}, u32[]{:S(2)}) collective-permute-start(bf16[2,64,2048]{2,1,0:T(8,128)(2,1)S(1)} %get-tuple-element.45), channel_id=1, source_target_pairs={{64,0},{96,32},{128,64},{160,96},{192,128},{224,160},{0,192},{32,2... | collective-permute-start | bytes 1572872 | tf_op jit(solution)/shard_map/ppermute | solution.py:106
  164.5 1.2 copy-start.1
  165.7 0.9 copy-start.9

commit v3 on v2

--- a/solution.py
+++ b/solution.py
@@ -131,55 +131,49 @@
     return copies
 
 
-def slot_kernel(
-    expert_total,
-    capacity,
-    masked_ref,
-    ids_ref,
-    cot_ref,
-    send_ref,
-    row_ref,
-    col_ref,
-    cots,
-    staged,
-    sem,
-    sems,
-):
-    del masked_ref
-    load = pltpu.make_async_copy(cot_ref, cots, sem.at[0])
-    load.start()
-    tokens = cot_ref.shape[0]
+def slot_kernel(capacity, ids_ref, row_ref, col_ref):
+    tokens = ids_ref.shape[1]
+    expert_total = 2 * tokens // capacity
     ids = ids_ref[...]
     onehot = iota((expert_total, tokens), 0) == ids
     before = flag(iota((tokens, tokens), 0) < iota((tokens, tokens), 1))
     earlier = dot(flag(onehot), before)
     slot = jnp.sum(jnp.where(onehot, earlier, 0.0), axis=0, keepdims=True).astype(I32)
     target = ids * capacity + slot
-    load.wait()
-    copies = send_rows(
-        lambda start, step: flag(iota((step, tokens), 0) + start == target),
-        cots[...],
-        staged,
-        send_ref,
-        sems,
-    )
     row_ref[...] = target
     diagonal = iota((tokens, tokens), 0) == iota((tokens, tokens), 1)
     column = jnp.sum(jnp.where(diagonal, target, 0).astype(F32), axis=1, keepdims=True)
     col_ref[...] = jnp.broadcast_to(column.astype(I32), col_ref.shape)
-    for copy in copies:
-        copy.wait()
-
-
-def mask_kernel(patches_ref, mask_ref, token_ref, masked_ref, right_ref, low_ref, corner_ref):
+
+
+def mask_kernel(
+    patches_ref,
+    mask_ref,
+    token_ref,
+    masked_ref,
+    right_ref,
+    low_ref,
+    corner_ref,
+    patches,
+    mask,
+    sems,
+):
+    loads = [
+        pltpu.make_async_copy(patches_ref, patches, sems.at[0]),
+        pltpu.make_async_copy(mask_ref, mask, sems.at[1]),
+    ]
+    for load in loads:
+        load.start()
+    for load in loads:
+        load.wait()
     tokens = patches_ref.shape[0]
     height, lateral = mask_ref.shape
     in_row = flag(iota((tokens, height), 0) // lateral == iota((tokens, height), 1))
-    spread = dot(in_row, mask_ref[...].astype(F32).astype(BF16))
+    spread = dot(in_row, mask[...].astype(F32).astype(BF16))
     own = iota((tokens, lateral), 0) % lateral == iota((tokens, lateral), 1)
     hidden_patch = jnp.sum(jnp.where(own, spread, 0.0), axis=1, keepdims=True)
     masked = jnp.where(
-        hidden_patch > 0.5, token_ref[...].astype(F32), patches_ref[...].astype(F32)
+        hidden_patch > 0.5, token_ref[...].astype(F32), patches[...].astype(F32)
     ).astype(BF16)
     masked_ref[...] = masked
     low_ref[...] = masked[: SHIFT * lateral]
@@ -199,29 +193,49 @@
     right_ref,
     low_ref,
     corner_ref,
+    row_ref,
+    qkv_far,
+    proj_far,
+    scale_far,
+    bias_far,
+    attn_gain_far,
+    moe_gain_far,
+    cot_far,
+    hidden_ref,
+    send_ref,
     qkv_ref,
     proj_ref,
     scale_ref,
     bias_ref,
     attn_gain_ref,
     moe_gain_ref,
-    router_ref,
-    row_ref,
-    col_ref,
-    hidden_ref,
-    send_ref,
-    gate_ref,
+    sent_ref,
     blended_ref,
     staged,
+    load_sems,
     sems,
 ):
+    loads = [
+        pltpu.make_async_copy(source, target, load_sems.at[i])
+        for i, (source, target) in enumerate(
+            (
+                (qkv_far, qkv_ref),
+                (scale_far, scale_ref),
+                (bias_far, bias_ref),
+                (proj_far, proj_ref),
+                (attn_gain_far, attn_gain_ref),
+                (moe_gain_far, moe_gain_ref),
+                (cot_far, sent_ref.at[:, cot_far.shape[1] :]),
+            )
+        )
+    ]
+    for load in loads:
+        load.start()
     tokens, width = masked_ref.shape
     features = width // heads
     window = WIN * WIN
     across = lateral // WIN
     group = 128 // features
-    expert_total = router_ref.shape[0]
-    capacity = send_ref.shape[0] // expert_total
 
     source = jnp.concatenate([masked_ref[...], right_ref[...], low_ref[...], corner_ref[...]], axis=0)
 
@@ -245,9 +259,11 @@
     displaced_f = dot(moves, source)
     displaced = displaced_f.astype(BF16)
 
+    loads[0].wait()
     projected = dot(displaced, qkv_ref[...]).astype(BF16)
     head_of = flag(iota((width, heads), 0) // features == iota((width, heads), 1))
     of_head = flag(iota((heads, width), 1) // features == iota((heads, width), 0))
+    loads[1].wait()
     queries = projected[:, :width].astype(F32)
     keys = projected[:, width : 2 * width].astype(F32)
     query_norm = lax.rsqrt(dot_split(queries * queries, head_of) + 1e-06) * scale_ref[...]
@@ -256,6 +272,7 @@
     keys = (keys * dot_split(key_norm, of_head)).astype(BF16)
 
     block = group * window
+    loads[2].wait()
     biases = [
         jnp.concatenate([bias_ref[g * group + i] for i in range(group)], axis=1)
         for g in range(width // 128)
@@ -283,6 +300,8 @@
             both = dot(weights.astype(BF16), jnp.concatenate([wide_v, member], axis=1))
             blended_ref[rows, lanes] = (both[:, :128] / both[:, 128:]).astype(BF16)
 
+    for load in loads[3:]:
+        load.wait()
     projection = dot(blended_ref[...], proj_ref[...])
     branch, _ = normal_form(projection)
     hidden = displaced_f + branch * attn_gain_ref[...]
@@ -290,18 +309,14 @@
     hidden = hidden.reshape(tokens, width).astype(BF16)
     hidden_ref[...] = hidden
     normed, _ = normal_form(hidden.astype(F32))
-    normed = (normed * moe_gain_ref[...]).astype(BF16)
+    sent_ref[:, :width] = (normed * moe_gain_ref[...]).astype(BF16)
     copies = send_rows(
         lambda start, step: flag(iota((step, tokens), 0) + start == row_ref[...]),
-        normed,
+        sent_ref[...],
         staged,
         send_ref,
         sems,
     )
-    logits = dot_nt(normed, router_ref[...])
-    chosen = iota((tokens, expert_total), 1) == col_ref[:, :1] // capacity
-    gate = jax.nn.sigmoid(jnp.sum(jnp.where(chosen, logits, 0.0), axis=1, keepdims=True))
-    gate_ref[...] = jnp.broadcast_to(gate, gate_ref.shape)
     for copy in copies:
         copy.wait()
 
@@ -309,30 +324,24 @@
 PARTS = 4
 
 
-def early_kernel(d_ref, w_out_ref, dact_ref):
-    dact_ref[...] = dot(d_ref[...], w_out_ref[...])
-
-
 def expert_kernel(
     index_ref,
-    z_ref,
+    slots_ref,
     router_ref,
     w_in_ref,
     w_out_ref,
-    dact_ref,
     back_ref,
     act_ref,
     dpre_ref,
     w_in,
     w_out,
-    dact,
     act,
     dpre,
     back,
     load_sems,
     store_sems,
 ):
-    rows, width = z_ref.shape
+    rows, width = slots_ref.shape[0], slots_ref.shape[1] // 2
     units = w_in.shape[1]
     tile, chunk, piece = rows // PARTS, units // PARTS, width // 2
 
@@ -344,16 +353,12 @@
     def tiled(i, step):
         return slice(i * step, (i + 1) * step)
 
-    load_in = [
-        load(w_in_ref.at[:, tiled(i, chunk)], w_in.at[:, tiled(i, chunk)], i) for i in range(PARTS)
-    ]
-    load_dact = [load(dact_ref.at[tiled(0, tile)], dact.at[tiled(0, tile)], PARTS)]
-    load_out = load(w_out_ref, w_out, 2 * PARTS)
-    load_dact += [
-        load(dact_ref.at[tiled(i, tile)], dact.at[tiled(i, tile)], PARTS + i)
-        for i in range(1, PARTS)
-    ]
-    half_gate = 0.5 * slot_gates(z_ref[...], router_ref[...], index_ref[0])
+    loads = []
+    for i in range(PARTS):
+        part = tiled(i, chunk)
+        loads.append(load(w_in_ref.at[:, part], w_in.at[:, part], 2 * i))
+        loads.append(load(w_out_ref.at[:, part], w_out.at[:, part], 2 * i + 1))
+    half_gate = 0.5 * slot_gates(slots_ref[:, :width], router_ref[...], index_ref[0])
     stores = []
 
     def store(source, target):
@@ -362,19 +367,19 @@
         stores.append(copy)
 
     for r in range(PARTS + 1):
-        if r < PARTS:
-            load_dact[r].wait()
-        if r == 1:
-            load_out.wait()
         here, last = tiled(r, tile), tiled(r - 1, tile)
         for c in range(PARTS):
             part = tiled(c, chunk)
             if r < PARTS:
                 if r == 0:
-                    load_in[c].wait()
-                activation, slopes = doubled_gelu_parts(dot(z_ref[here], w_in[:, part]))
+                    loads[2 * c].wait()
+                    loads[2 * c + 1].wait()
+                activation, slopes = doubled_gelu_parts(
+                    dot(slots_ref[here, :width], w_in[:, part])
+                )
                 act[here, part] = activation.astype(BF16)
-                dpre[here, part] = (dact[here, part] * slopes).astype(BF16)
+                dact = dot(slots_ref[here, width:], w_out[:, part])
+                dpre[here, part] = (dact * slopes).astype(BF16)
             if r > 0:
                 half = tiled(c % 2, piece)
                 if c < 2:
@@ -392,9 +397,9 @@
 
 
 def grads_kernel(
-    lat_total, index_ref, z_ref, d_ref, router_ref, dpre_ref, act_ref, keep_ref, give_ref, zt, dt
+    lat_total, index_ref, slots_ref, router_ref, dpre_ref, act_ref, keep_ref, give_ref, zt, dt
 ):
-    width = z_ref.shape[1]
+    width = slots_ref.shape[1] // 2
     rows = width // lat_total
 
     @pl.when(pl.program_id(0) == 0)
@@ -404,9 +409,10 @@
         column, core = index_ref[1] // 2, index_ref[1] % 2
         block = (step + column) % (lat_total // 2) * 2 + (half + core) % 2
         moves = flag(iota((width, width), 1) == block * rows + inside)
-        half_gate = 0.5 * slot_gates(z_ref[...], router_ref[...], index_ref[0])
-        for slots_ref, turned in ((z_ref, zt), (d_ref, dt)):
-            scaled = (slots_ref[...].astype(F32) * half_gate).astype(BF16)
+        half_gate = 0.5 * slot_gates(slots_ref[:, :width], router_ref[...], index_ref[0])
+        for i, turned in enumerate((zt, dt)):
+            part = slots_ref[:, i * width : (i + 1) * width]
+            scaled = (part.astype(F32) * half_gate).astype(BF16)
             turned[...] = dot_nt(moves, scaled).astype(BF16)
 
     for i, (left, right) in enumerate(((zt, dpre_ref), (dt, act_ref))):
@@ -444,35 +450,61 @@
         out_ref[:, 0, i * units : (i + 1) * units] = total
 
 
+def ready_kernel(
+    capacity, col_ref, hidden_ref, router_ref, gain_ref, picks_ref, xhat_ref, gate_ref, inv_ref
+):
+    tokens = hidden_ref.shape[0]
+    picks_ref[...] = flag(iota(picks_ref.shape, 1) == col_ref[:, :1])
+    xhat, inv_std = normal_form(hidden_ref[...].astype(F32))
+    xhat_ref[...] = xhat
+    inv_ref[...] = jnp.broadcast_to(inv_std, inv_ref.shape)
+    chosen = iota((tokens, router_ref.shape[0]), 1) == col_ref[:, :1] // capacity
+    logits = dot_nt((xhat * gain_ref[...]).astype(BF16), router_ref[...])
+    gate = jax.nn.sigmoid(jnp.sum(jnp.where(chosen, logits, 0.0), axis=1, keepdims=True))
+    gate_ref[...] = jnp.broadcast_to(gate, gate_ref.shape)
+
+
 def final_kernel(
     capacity,
     grads_ref,
+    picks_ref,
+    xhat_ref,
+    gate_ref,
+    inv_ref,
     col_ref,
     back_ref,
     hidden_ref,
-    gate_ref,
     cot_ref,
     router_ref,
     gain_ref,
     block_ref,
     mixer_ref,
+    block,
+    mixer,
+    sems,
 ):
     del grads_ref
     tokens, width = hidden_ref.shape
-    picks = flag(iota((tokens, back_ref.shape[0]), 1) == col_ref[:, :1])
-    both = dot(picks, back_ref[...])
-    expert_out, dnormed = both[:, :width], both[:, width:]
-    gate, cot, hidden = gate_ref[:, :1], cot_ref[...].astype(F32), hidden_ref[...].astype(F32)
-    block_ref[...] = (hidden + gate * expert_out).astype(BF16)
-    dgate = jnp.sum(cot * expert_out, axis=1, keepdims=True)
-    dlogit = dgate * gate * (1.0 - gate)
-    chosen = flag(iota((tokens, router_ref.shape[0]), 1) == col_ref[:, :1] // capacity)
-    dnormed = dnormed + dlogit * dot(chosen, router_ref[...])
-    xhat, inv_std = normal_form(hidden)
-    scaled = dnormed * gain_ref[...]
-    first = jnp.mean(scaled, axis=-1, keepdims=True)
-    second = jnp.mean(scaled * xhat, axis=-1, keepdims=True)
-    mixer_ref[...] = cot + inv_std * (scaled - first - xhat * second)
+    span = tokens // PARTS
+    copies = []
+    for i in range(PARTS):
+        here = slice(i * span, (i + 1) * span)
+        both = dot(picks_ref[here], back_ref[...])
+        expert_out, dnormed = both[:, :width], both[:, width:]
+        gate, cot = gate_ref[here, :1], cot_ref[here].astype(F32)
+        block[here] = (hidden_ref[here].astype(F32) + gate * expert_out).astype(BF16)
+        dlogit = jnp.sum(cot * expert_out, axis=1, keepdims=True) * gate * (1.0 - gate)
+        chosen = flag(iota((span, router_ref.shape[0]), 1) == col_ref[here, :1] // capacity)
+        dnormed = dnormed + dlogit * dot(chosen, router_ref[...])
+        scaled, xhat = dnormed * gain_ref[...], xhat_ref[here]
+        first = jnp.mean(scaled, axis=-1, keepdims=True)
+        second = jnp.mean(scaled * xhat, axis=-1, keepdims=True)
+        mixer[here] = cot + inv_ref[here, :1] * (scaled - first - xhat * second)
+        for j, (source, target) in enumerate(((block, block_ref), (mixer, mixer_ref))):
+            copies.append(pltpu.make_async_copy(source.at[here], target.at[here], sems.at[i, j]))
+            copies[-1].start()
+    for copy in copies:
+        copy.wait()
 
 
 def per_device(
@@ -500,94 +532,79 @@
     w_in, w_out = w_in[0], w_out[0]
     units = w_in.shape[1]
 
+    dma = pltpu.SemaphoreType.DMA
     cot = cotangent.reshape(tokens, width)
     router_t = router.T
-    dma = pltpu.SemaphoreType.DMA
     masked, right, low, corner = call(
         mask_kernel,
         (
             shape((tokens, width), BF16),
-            shape((height * SHIFT, width), BF16),
-            shape((SHIFT * lateral, width), BF16),
-            shape((SHIFT * SHIFT, width), BF16),
+            far((height * SHIFT, width), BF16),
+            far((SHIFT * lateral, width), BF16),
+            far((SHIFT * SHIFT, width), BF16),
         ),
-        (WHOLE,) * 3,
-        patches.reshape(tokens, width),
-        patch_mask,
+        (FAR, FAR, WHOLE),
+        kept_far(patches.reshape(tokens, width)),
+        kept_far(patch_mask),
         mask_token.reshape(1, width),
+        scratch=[
+            pltpu.VMEM((tokens, width), BF16),
+            pltpu.VMEM((height, lateral), I32),
+            dma((2,)),
+        ],
     )
     right = passed_along(right, "lon", -1)
     low = passed_along(low, "lat", -1)
     corner = passed_diagonally(corner)
 
-    cot_send, target_row, target_col = call(
-        lambda *refs: slot_kernel(expert_total, capacity, *refs),
-        (
-            far((slot_total, width), BF16),
-            shape((1, tokens), I32),
-            shape((tokens, 128), I32),
-        ),
-        (UNREAD, WHOLE, FAR),
-        masked,
+    target_row, target_col = call(
+        lambda *refs: slot_kernel(capacity, *refs),
+        (shape((1, tokens), I32), shape((tokens, 128), I32)),
+        (WHOLE,),
         expert_ids.reshape(1, tokens),
-        kept_far(cot),
-        out_specs=(FAR, WHOLE, WHOLE),
-        scratch=[
-            pltpu.VMEM((tokens, width), BF16),
-            pltpu.VMEM((slot_total, width), BF16),
-            dma((1,)),
-            dma((PARTS,)),
-        ],
-        flops=2 * slot_total * tokens * width,
-    )
-    d_slots = exchanged(cot_send.reshape(expert_total, capacity, width)).reshape(slot_total, width)
-
+    )
     last = (lax.axis_index("lat") == lax.axis_size("lat") - 1).astype(I32).reshape(1)
-    hidden, normed_send, gate = call(
+    hidden, send = call(
         lambda *refs: attention_kernel(heads, height, lateral, *refs),
         (
-            shape((tokens, width), BF16),
-            far((slot_total, width), BF16),
-            shape((tokens, 128), F32),
+            far((tokens, width), BF16),
+            far((slot_total, 2 * width), BF16),
         ),
-        (SCALAR,) + (WHOLE,) * 13,
+        (SCALAR,) + (WHOLE,) * 5 + (FAR,) * 7,
         last,
         masked,
         right,
         low,
         corner,
-        w_qkv,
-        w_proj,
-        logit_scale.reshape(1, heads),
-        rel_bias,
-        attn_gain.reshape(1, width),
-        moe_gain.reshape(1, width),
-        router_t,
         target_row,
-        target_col,
-        out_specs=(WHOLE, FAR, WHOLE),
+        kept_far(w_qkv),
+        kept_far(w_proj),
+        kept_far(logit_scale.reshape(1, heads)),
+        kept_far(rel_bias),
+        kept_far(attn_gain.reshape(1, width)),
+        kept_far(moe_gain.reshape(1, width)),
+        kept_far(cot),
+        out_specs=(WHOLE, FAR),
         scratch=[
+            pltpu.VMEM(w_qkv.shape, BF16),
+            pltpu.VMEM(w_proj.shape, BF16),
+            pltpu.VMEM((1, heads), F32),
+            pltpu.VMEM(rel_bias.shape, F32),
+            pltpu.VMEM((1, width), F32),
+            pltpu.VMEM((1, width), F32),
+            pltpu.VMEM((tokens, 2 * width), BF16),
             pltpu.VMEM((tokens, width), BF16),
-            pltpu.VMEM((slot_total, width), BF16),
+            pltpu.VMEM((slot_total, 2 * width), BF16),
+            dma((7,)),
             dma((PARTS,)),
         ],
-        vmem=28,
-        flops=2 * tokens * width * (6 * width + slot_total),
-    )
-    z_slots = exchanged(normed_send.reshape(expert_total, capacity, width)).reshape(
-        slot_total, width
+        vmem=32,
+        flops=2 * tokens * width * (6 * width + 2 * slot_total),
+    )
+    slots = exchanged(send.reshape(expert_total, capacity, 2 * width)).reshape(
+        slot_total, 2 * width
     )
     chunk = units // PARTS
-    dact = call(
-        early_kernel,
-        far((slot_total, units), F32),
-        (WHOLE, pl.BlockSpec((width, chunk), lambda i: (0, i))),
-        d_slots,
-        kept_far(w_out),
-        grid=(PARTS,),
-        out_specs=pl.BlockSpec((slot_total, chunk), lambda i: (0, i)),
-        flops=2 * slot_total * width * units,
-    )
     index = jnp.stack([lax.axis_index("lon"), lax.axis_index("lat")]).astype(I32)
     back, activation, dpre = call(
         expert_kernel,
@@ -596,26 +613,24 @@
             far((slot_total, units), BF16),
             far((slot_total, units), BF16),
         ),
-        (SCALAR, WHOLE, WHOLE, FAR, FAR, FAR),
+        (SCALAR, WHOLE, WHOLE, FAR, FAR),
         index,
-        z_slots,
+        slots,
         router_t,
         kept_far(w_in),
         kept_far(w_out),
-        dact,
         out_specs=(FAR, FAR, FAR),
         scratch=[
             pltpu.VMEM((width, units), BF16),
             pltpu.VMEM((width, units), BF16),
-            pltpu.VMEM((slot_total, units), F32),
             pltpu.VMEM((slot_total, units), BF16),
             pltpu.VMEM((slot_total, units), BF16),
             pltpu.VMEM((slot_total, 2 * width), BF16),
-            dma((2 * PARTS + 1,)),
+            dma((2 * PARTS,)),
             dma((3 * PARTS,)),
         ],
         vmem=40,
-        flops=6 * slot_total * width * units,
+        flops=8 * slot_total * width * units,
     )
     back = exchanged(back.reshape(expert_total, capacity, 2 * width)).reshape(
         slot_total, 2 * width
@@ -627,13 +642,12 @@
     keep, give = call(
         lambda *refs: grads_kernel(lat_total, *refs),
         (shape((2, half, units), BF16),) * 2,
-        (SCALAR, WHOLE, WHOLE, WHOLE) + (pl.BlockSpec((slot_total, chunk), lambda i: (0, i)),) * 2,
+        (SCALAR, WHOLE, WHOLE) + (pl.BlockSpec((slot_total, chunk), lambda i: (0, i)),) * 2,
         index,
-        z_slots,
-        d_slots,
+        slots,
         router_t,
-        dpre,
-        activation,
+        kept_far(dpre),
+        kept_far(activation),
         grid=(PARTS,),
         out_specs=(pl.BlockSpec((2, half, chunk), lambda i: (0, 0, i)),) * 2,
         scratch=[pltpu.VMEM((width, slot_total), BF16)] * 2,
@@ -653,23 +667,39 @@
     weight_grads = call(
         total_kernel, far((rows, 1, 2 * units), F32), (WHOLE,) * 3, own, up, down
     )
-    span = tokens // PARTS
-    tall = pl.BlockSpec((span, width), lambda i: (i, 0))
-    thin = pl.BlockSpec((span, 128), lambda i: (i, 0))
+    moe_row = moe_gain.reshape(1, width)
+    thin = shape((tokens, 128), F32)
+    picks, xhat, gate, inv_std = call(
+        lambda *refs: ready_kernel(capacity, *refs),
+        (shape((tokens, slot_total), BF16), shape((tokens, width), F32), thin, thin),
+        (WHOLE,) * 4,
+        target_col,
+        hidden,
+        router_t,
+        moe_row,
+        flops=2 * tokens * slot_total * width,
+    )
     block_out, mixer_grad = call(
         lambda *refs: final_kernel(capacity, *refs),
         (far((tokens, width), BF16), far((tokens, width), F32)),
-        (UNREAD, thin, WHOLE, tall, thin, tall, WHOLE, WHOLE),
-        weight_grads,
+        (UNREAD,) + (WHOLE,) * 10,
+        kept_far(weight_grads),
+        picks,
+        xhat,
+        gate,
+        inv_std,
         target_col,
         back,
         hidden,
-        gate,
         cot,
         router_t,
-        moe_gain.reshape(1, width),
-        grid=(PARTS,),
-        out_specs=(tall, tall),
+        moe_row,
+        out_specs=(FAR, FAR),
+        scratch=[
+            pltpu.VMEM((tokens, width), BF16),
+            pltpu.VMEM((tokens, width), F32),
+            dma((PARTS, 2)),
+        ],
         flops=4 * slot_total * tokens * width,
     )
     return (

time: 173 us -> 162 us (0.936); the launches traced: 170 us -> 161 us
  waiting for transfers between devices: 65.7 us -> 80.5 us
  starting transfers between devices: 39.5 us -> 28 us
  local copies, waits for them, and re-layouts: 19.8 us -> 10.5 us
  Pallas kernels: 44.2 us -> 41 us
    all_to_all x3 -> x2, waiting for transfers between devices: 23.9 us -> 57.8 us  [exchanged(): return lax.all_to_all(slots, 'lon', split_axis=0, concat_axis=0, tiled=True)]
    ppermute x1, waiting for transfers between devices: 16.8 us -> 1.75 us  [passed_diagonally(): return lax.ppermute(block, ('lat', 'lon'), route)]
    all_to_all x3 -> x2, starting transfers between devices: 29 us -> 14.4 us  [exchanged(): return lax.all_to_all(slots, 'lon', split_axis=0, concat_axis=0, tiled=True)]
    unnamed x48 -> x28, local copies, waits for them, and re-layouts: 19.1 us -> 9.84 us
    ppermute x6, waiting for transfers between devices: 21 us -> 17 us  [passed_along(): return lax.ppermute(block, axis, route)]
    ppermute x6, starting transfers between devices: 9.5 us -> 12.8 us  [passed_along(): return lax.ppermute(block, axis, route)]
    pallas_call x10, Pallas kernels: 44.2 us -> 41 us  [call(): pl.pallas_call(body, grid=grid, out_shape=outs, in_specs=list(ins), out_s...]
  transfers between devices with their start and end apart: 11 -> 10, of which waited for: 8 -> 8; matrix products, arithmetic and copies ran while one was open for 0% -> 0% of each run, Pallas kernels for 15% -> 8%
where the time goes in v3:
time: 162 us; the launch traced here: 161 us
  waiting for transfers between devices  80.5 us (50%)
  Pallas kernels  41 us (25%)
  starting transfers between devices  28 us (17%)
  local copies, waits for them, and re-layouts  10.5 us (6%)
    all_to_all x2, waiting for transfers between devices, exchanged(): return lax.all_to_all(slots, 'lon', split_axis=0, concat_axis=0, tiled=True)  57.8 us
    pallas_call x10, Pallas kernels, call(): pl.pallas_call(body, grid=grid, out_shape=outs, in_specs=list(ins), out_s...  41 us
    ppermute x6, waiting for transfers between devices, passed_along(): return lax.ppermute(block, axis, route)  17 us
    all_to_all x2, starting transfers between devices, exchanged(): return lax.all_to_all(slots, 'lon', split_axis=0, concat_axis=0, tiled=True)  14.4 us
    ppermute x6, starting transfers between devices, passed_along(): return lax.ppermute(block, axis, route)  12.8 us
    unnamed x28, local copies, waits for them, and re-layouts  9.84 us
    ppermute x1, waiting for transfers between devices, per_device(): given = lax.ppermute(give, 'lat', [(i, i ^ 1) for i in range(lat_total)])  4.01 us
  transfers between devices with their start and end apart: 10, of which 8 were waited for; matrix products, arithmetic and copies ran while one was open for 0% of the time, Pallas kernels for 8%

profile of v3, /device:TPU:6, one launch (start us, length us, event | category | flops | bytes accessed | tf_op | source)
XLA Modules:
  0.0 161.0 jit_solution(4169379224930103997)
XLA Ops:
  0.6 0.7 reshape.54.token_ref
  1.3 2.1 %shard_map.157 = (bf16[512,512]{1,0:T(8,128)(2,1)S(1)}, bf16[64,512]{1,0:T(8,128)(2,1)}, bf16[128,512]{1,0:T(8,128)(2,1)}, bf16[16,512]{1,0:T(8,128)(2,1)}) custom-call(bf16[512,512]{1,0:T(8,128)(2,1)} %bitcast.33, s32[16,32]{1,0:T(8,128)} %mask_ref.1, bf16[1,512]{1,0:T(2,128)(2,1)S(1)} %reshape.54.token_ref), custom_call_target="tpu_custom_call" | custom-call | bytes 1264640 | tf_op jit(solution)/shard_map/pallas_call | solution.py:28
  3.5 0.3 collective-permute-start.1
  3.7 8.3 %collective-permute-start = (bf16[64,512]{1,0:T(8,128)(2,1)}, bf16[64,512]{1,0:T(8,128)(2,1)S(1)}, u32[]{:S(2)}, u32[]{:S(2)}) collective-permute-start(bf16[64,512]{1,0:T(8,128)(2,1)} %get-tuple-element.30), channel_id=1, source_target_pairs={{1,0},{2,1},{3,2},{4,3},{5,4},{6,5},{7,6},{8,7},{9,8},{10,9},{11,1... | collective-permute-start | bytes 196616 | tf_op jit(solution)/shard_map/ppermute | solution.py:106
  12.0 0.6 collective-permute-start.2
  12.6 0.7 copy-done.12
  13.3 0.3 shard_map.158
  13.7 1.7 %collective-permute-done.2.refs_4_ = bf16[16,512]{1,0:T(8,128)(2,1)S(1)} collective-permute-done((bf16[16,512]{1,0:T(8,128)(2,1)}, bf16[16,512]{1,0:T(8,128)(2,1)S(1)}, u32[]{:S(2)}, u32[]{:S(2)}) %collective-permute-start.2) | collective-permute-done | bytes 16416 | tf_op jit(solution)/shard_map/ppermute | solution.py:116
  15.4 0.0 collective-permute-done.refs_2_
  15.4 0.0 collective-permute-done.1.refs_3_
  15.4 9.5 %shard_map.159 = (bf16[512,512]{1,0:T(8,128)(2,1)}, bf16[1024,1024]{1,0:T(8,128)(2,1)}) custom-call(s32[1]{0:T(128)} %bitcast.2.refs_0_, bf16[512,512]{1,0:T(8,128)(2,1)S(1)} %get-tuple-element.29.refs_1_, bf16[64,512]{1,0:T(8,128)(2,1)S(1)} %collective-permute-done.refs_2_, bf16[128,512]{1,0:T(8,128)(2,1)S(1)} %collective-permute-done.1.refs_3_, ...), custom_call_target="tpu_custom_call" | custom-call | flops 2684354560 | bytes 6248516 | tf_op jit(solution)/shard_map/pallas_call | solution.py:28
  24.9 0.0 copy-start.11
  24.9 6.6 %all-to-all-start = ((bf16[32,32,1024]{2,1,0:T(8,128)(2,1)}), bf16[32,32,1024]{2,1,0:T(8,128)(2,1)S(1)}, u32[]{:S(2)}, u32[]{:S(2)}) async-start(bf16[32,32,1024]{2,1,0:T(8,128)(2,1)} %bitcast.32), calls=%async_computation | async-start | bytes 4194304 | tf_op jit(solution)/shard_map/all_to_all | solution.py:120
  31.5 0.1 pad_add_fusion.index_ref.refs_0_
  31.6 49.1 %all-to-all-done = bf16[32,32,1024]{2,1,0:T(8,128)(2,1)S(1)} async-done(((bf16[32,32,1024]{2,1,0:T(8,128)(2,1)}), bf16[32,32,1024]{2,1,0:T(8,128)(2,1)S(1)}, u32[]{:S(2)}, u32[]{:S(2)}) %all-to-all-start) | async-done | bytes 2097184 | tf_op jit(solution)/shard_map/all_to_all | solution.py:120
  80.7 0.0 copy-done.11
  80.7 14.0 %shard_map.160 = (bf16[1024,1024]{1,0:T(8,128)(2,1)}, bf16[1024,2048]{1,0:T(8,128)(2,1)}, bf16[1024,2048]{1,0:T(8,128)(2,1)}) custom-call(s32[2]{0:T(128)S(1)} %pad_add_fusion.index_ref.refs_0_, bf16[1024,1024]{1,0:T(8,128)(2,1)S(1)} %bitcast.19, bf16[32,512]{1,0:T(8,128)(2,1)S(1)} %bitcast.23, bf16[512,2048]{1,0:T(8,128)(2,1)} %bitcast.34, ...), custom_call_target="tpu_custom_call" | custom-call | flops 8589934592 | bytes 16809992 | tf_op jit(solution)/shard_map/pallas_call | solution.py:28
  94.7 0.0 copy-done
  94.7 7.8 %all-to-all-start.1 = ((bf16[32,32,1024]{2,1,0:T(8,128)(2,1)}), bf16[32,32,1024]{2,1,0:T(8,128)(2,1)S(1)}, u32[]{:S(2)}, u32[]{:S(2)}) async-start(bf16[32,32,1024]{2,1,0:T(8,128)(2,1)} %bitcast.31), calls=%async_computation.1 | async-start | bytes 4194304 | tf_op jit(solution)/shard_map/all_to_all | solution.py:120
  102.5 0.0 copy-start.1
  102.5 1.6 copy-done.1
  104.1 9.4 %shard_map.161 = (bf16[2,256,2048]{2,1,0:T(8,128)(2,1)S(1)}, bf16[2,256,2048]{2,1,0:T(8,128)(2,1)S(1)}) custom-call(s32[2]{0:T(128)S(1)} %pad_add_fusion.index_ref.refs_0_, bf16[1024,1024]{1,0:T(8,128)(2,1)S(1)} %bitcast.20, bf16[32,512]{1,0:T(8,128)(2,1)S(1)} %bitcast.24, bf16[1024,2048]{1,0:T(8,128)(2,1)} %get-tuple-element.35.refs_3_, ...), custom_call_target="tpu_custom_call" | custom-call | flops 4294967296 | bytes 14712840 | tf_op jit(solution)/shard_map/pallas_call | solution.py:28
  113.5 0.2 collective-permute-start.3
  113.8 4.0 %collective-permute-done.3.given_ref = bf16[2,256,2048]{2,1,0:T(8,128)(2,1)S(1)} collective-permute-done((bf16[2,256,2048]{2,1,0:T(8,128)(2,1)S(1)}, bf16[2,256,2048]{2,1,0:T(8,128)(2,1)S(1)}, u32[]{:S(2)}, u32[]{:S(2)}) %collective-permute-start.3) | collective-permute-done | bytes 2097184 | tf_op jit(solution)/shard_map/ppermute | solution.py:657
  117.8 0.5 shard_map.162
  118.3 0.9 collective-permute-start.4
  119.1 1.2 collective-permute-start.5
  120.4 6.3 %collective-permute-done.4.up_part_ref = bf16[64,2048]{1,0:T(8,128)(2,1)S(1)} collective-permute-done((bf16[64,2048]{1,0:T(8,128)(2,1)S(1)}, bf16[64,2048]{1,0:T(8,128)(2,1)S(1)}, u32[]{:S(2)}, u32[]{:S(2)}) %collective-permute-start.4) | collective-permute-done | bytes 262176 | tf_op jit(solution)/shard_map/ppermute | solution.py:106
  126.7 1.7 %collective-permute-done.5.down_part_ref = bf16[64,2048]{1,0:T(8,128)(2,1)S(1)} collective-permute-done((bf16[64,2048]{1,0:T(8,128)(2,1)S(1)}, bf16[64,2048]{1,0:T(8,128)(2,1)S(1)}, u32[]{:S(2)}, u32[]{:S(2)}) %collective-permute-start.5) | collective-permute-done | bytes 262176 | tf_op jit(solution)/shard_map/ppermute | solution.py:106
  128.4 0.1 shard_map.163
  128.5 0.6 collective-permute-start.6
  129.1 1.5 collective-permute-start.7
  130.6 0.0 copy-done.5
  130.7 1.0 shard_map.165
  131.6 0.0 copy-start.2
  131.6 1.0 copy-done.2
  132.6 0.7 copy-done.7
  133.3 0.7 copy-done.9
  134.0 7.5 %collective-permute-done.6.up_ref = bf16[2,64,2048]{2,1,0:T(8,128)(2,1)S(1)} collective-permute-done((bf16[2,64,2048]{2,1,0:T(8,128)(2,1)S(1)}, bf16[2,64,2048]{2,1,0:T(8,128)(2,1)S(1)}, u32[]{:S(2)}, u32[]{:S(2)}) %collective-permute-start.6) | collective-permute-done | bytes 524320 | tf_op jit(solution)/shard_map/ppermute | solution.py:106
  141.4 1.5 collective-permute-done.7.down_ref
  143.0 1.3 shard_map.164.refs_0_
  144.3 8.7 %all-to-all-done.1 = bf16[32,32,1024]{2,1,0:T(8,128)(2,1)S(1)} async-done(((bf16[32,32,1024]{2,1,0:T(8,128)(2,1)}), bf16[32,32,1024]{2,1,0:T(8,128)(2,1)S(1)}, u32[]{:S(2)}, u32[]{:S(2)}) %all-to-all-start.1) | async-done | bytes 2097184 | tf_op jit(solution)/shard_map/all_to_all | solution.py:120
  153.0 1.2 copy-done.3
  154.2 1.0 copy-done.4
  155.2 1.0 copy-done.6
  156.3 0.9 copy-done.8
  157.2 0.9 copy-done.10
  158.2 2.7 %shard_map.166 = (bf16[512,512]{1,0:T(8,128)(2,1)}, f32[512,512]{1,0:T(8,128)}) custom-call(f32[64,1,4096]{2,1,0:T(1,128)} %shard_map.164.refs_0_, bf16[512,1024]{1,0:T(8,128)(2,1)S(1)} %get-tuple-element.48.refs_1_, f32[512,512]{1,0:T(8,128)S(1)} %copy-done.3, f32[512,128]{1,0:T(8,128)S(1)} %copy-done.8, f32[512,128]{1,0:T(8,128)S(1)} %copy-done.10, ...), custom_call_target="tpu_custom_call" | custom-call | flops 1073741824 | bytes 8685568 | tf_op jit(solution)/shard_map/pallas_call | solution.py:28
  (12 shorter events, 0.0 us)
Async XLA Ops:
  3.5 12.0 %collective-permute-start.1 = (bf16[128,512]{1,0:T(8,128)(2,1)}, bf16[128,512]{1,0:T(8,128)(2,1)S(1)}, u32[]{:S(2)}, u32[]{:S(2)}) collective-permute-start(bf16[128,512]{1,0:T(8,128)(2,1)} %get-tuple-element.31), channel_id=1, source_target_pairs={{32,0},{64,32},{96,64},{128,96},{160,128},{192,160},{224,192},{0,2... | collective-permute-start | bytes 393224 | tf_op jit(solution)/shard_map/ppermute | solution.py:106
  3.7 11.7 %collective-permute-start = (bf16[64,512]{1,0:T(8,128)(2,1)}, bf16[64,512]{1,0:T(8,128)(2,1)S(1)}, u32[]{:S(2)}, u32[]{:S(2)}) collective-permute-start(bf16[64,512]{1,0:T(8,128)(2,1)} %get-tuple-element.30), channel_id=1, source_target_pairs={{1,0},{2,1},{3,2},{4,3},{5,4},{6,5},{7,6},{8,7},{9,8},{10,9},{11,1... | collective-permute-start | bytes 196616 | tf_op jit(solution)/shard_map/ppermute | solution.py:106
  12.0 3.4 %collective-permute-start.2 = (bf16[16,512]{1,0:T(8,128)(2,1)}, bf16[16,512]{1,0:T(8,128)(2,1)S(1)}, u32[]{:S(2)}, u32[]{:S(2)}) collective-permute-start(bf16[16,512]{1,0:T(8,128)(2,1)} %get-tuple-element.32), channel_id=1, source_target_pairs={{33,0},{34,1},{35,2},{36,3},{37,4},{38,5},{39,6},{40,7},{41,8},{42... | collective-permute-start | bytes 49160 | tf_op jit(solution)/shard_map/ppermute | solution.py:116
  12.6 0.7 copy-start.12
  24.9 55.8 %copy-start.11 = (bf16[512,32]{0,1:T(8,128)(2,1)S(1)}, bf16[512,32]{0,1:T(8,128)(2,1)}, u32[]{:S(2)}) copy-start(bf16[512,32]{0,1:T(8,128)(2,1)} %param.23) | copy-start | bytes 98308
  24.9 55.7 %all-to-all-start = ((bf16[32,32,1024]{2,1,0:T(8,128)(2,1)}), bf16[32,32,1024]{2,1,0:T(8,128)(2,1)S(1)}, u32[]{:S(2)}, u32[]{:S(2)}) async-start(bf16[32,32,1024]{2,1,0:T(8,128)(2,1)} %bitcast.32), calls=%async_computation | async-start | bytes 4194304 | tf_op jit(solution)/shard_map/all_to_all | solution.py:120
  80.7 14.0 %copy-start = (bf16[32,32,1024]{2,1,0:T(8,128)(2,1)}, bf16[32,32,1024]{2,1,0:T(8,128)(2,1)S(1)}, u32[]{:S(2)}) copy-start(bf16[32,32,1024]{2,1,0:T(8,128)(2,1)S(1)} %all-to-all-done) | copy-start | bytes 6291460
  94.7 58.3 %all-to-all-start.1 = ((bf16[32,32,1024]{2,1,0:T(8,128)(2,1)}), bf16[32,32,1024]{2,1,0:T(8,128)(2,1)S(1)}, u32[]{:S(2)}, u32[]{:S(2)}) async-start(bf16[32,32,1024]{2,1,0:T(8,128)(2,1)} %bitcast.31), calls=%async_computation.1 | async-start | bytes 4194304 | tf_op jit(solution)/shard_map/all_to_all | solution.py:120
  102.5 1.6 copy-start.1
  113.5 4.2 %collective-permute-start.3 = (bf16[2,256,2048]{2,1,0:T(8,128)(2,1)S(1)}, bf16[2,256,2048]{2,1,0:T(8,128)(2,1)S(1)}, u32[]{:S(2)}, u32[]{:S(2)}) collective-permute-start(bf16[2,256,2048]{2,1,0:T(8,128)(2,1)S(1)} %get-tuple-element.38), channel_id=1, source_target_pairs={{0,32},{32,0},{64,96},{96,64},{128,160},{160,128},{192,224},{224,1... | collective-permute-start | bytes 6291464 | tf_op jit(solution)/shard_map/ppermute | solution.py:657
  117.8 12.9 %copy-start.5 = (bf16[512,512]{1,0:T(8,128)(2,1)S(1)}, bf16[512,512]{1,0:T(8,128)(2,1)}, u32[]{:S(2)}) copy-start(bf16[512,512]{1,0:T(8,128)(2,1)} %get-tuple-element.47.refs_1_.refs_7_) | copy-start | bytes 1572868
  117.8 12.9 %copy-start.13 = (f32[512]{0:T(512)S(1)}, f32[512]{0:T(512)}, u32[]{:S(2)}) copy-start(f32[512]{0:T(512)} %param.22) | copy-start | bytes 6148
  118.3 8.4 %collective-permute-start.4 = (bf16[64,2048]{1,0:T(8,128)(2,1)S(1)}, bf16[64,2048]{1,0:T(8,128)(2,1)S(1)}, u32[]{:S(2)}, u32[]{:S(2)}) collective-permute-start(bf16[64,2048]{1,0:T(8,128)(2,1)S(1)} %get-tuple-element.42), channel_id=1, source_target_pairs={{192,0},{224,32},{0,64},{32,96},{64,128},{96,160},{128,192},{160,2... | collective-permute-start | bytes 786440 | tf_op jit(solution)/shard_map/ppermute | solution.py:106
  119.1 9.3 %collective-permute-start.5 = (bf16[64,2048]{1,0:T(8,128)(2,1)S(1)}, bf16[64,2048]{1,0:T(8,128)(2,1)S(1)}, u32[]{:S(2)}, u32[]{:S(2)}) collective-permute-start(bf16[64,2048]{1,0:T(8,128)(2,1)S(1)} %get-tuple-element.43), channel_id=1, source_target_pairs={{64,0},{96,32},{128,64},{160,96},{192,128},{224,160},{0,192},{32,2... | collective-permute-start | bytes 786440 | tf_op jit(solution)/shard_map/ppermute | solution.py:106
  128.5 12.9 %collective-permute-start.6 = (bf16[2,64,2048]{2,1,0:T(8,128)(2,1)S(1)}, bf16[2,64,2048]{2,1,0:T(8,128)(2,1)S(1)}, u32[]{:S(2)}, u32[]{:S(2)}) collective-permute-start(bf16[2,64,2048]{2,1,0:T(8,128)(2,1)S(1)} %get-tuple-element.44), channel_id=1, source_target_pairs={{192,0},{224,32},{0,64},{32,96},{64,128},{96,160},{128,192},{160,2... | collective-permute-start | bytes 1572872 | tf_op jit(solution)/shard_map/ppermute | solution.py:106
  129.1 13.9 %collective-permute-start.7 = (bf16[2,64,2048]{2,1,0:T(8,128)(2,1)S(1)}, bf16[2,64,2048]{2,1,0:T(8,128)(2,1)S(1)}, u32[]{:S(2)}, u32[]{:S(2)}) collective-permute-start(bf16[2,64,2048]{2,1,0:T(8,128)(2,1)S(1)} %get-tuple-element.45), channel_id=1, source_target_pairs={{64,0},{96,32},{128,64},{160,96},{192,128},{224,160},{0,192},{32,2... | collective-permute-start | bytes 1572872 | tf_op jit(solution)/shard_map/ppermute | solution.py:106
  131.6 1.0 copy-start.2
  132.6 0.7 copy-start.7
  133.3 0.7 copy-start.9
  153.0 1.2 copy-start.3
  154.2 1.0 copy-start.4
  155.2 1.0 copy-start.6
  156.3 0.9 copy-start.8
  157.2 0.9 copy-start.10

commit v4 on v3

--- a/solution.py
+++ b/solution.py
@@ -21,7 +21,9 @@
 UNREAD = pl.BlockSpec(memory_space=pl.ANY)
 
 
-def call(body, outs, ins, *operands, scratch=(), grid=(), out_specs=None, vmem=16, flops=0):
+def call(
+    body, outs, ins, *operands, scratch=(), grid=(), out_specs=None, vmem=16, flops=0, aliases=None
+):
     if out_specs is None:
         out_specs = jax.tree.map(lambda _: WHOLE, outs)
     moved = sum(math.prod(x.shape) * x.dtype.itemsize for x in (*operands, *jax.tree.leaves(outs)))
@@ -32,6 +34,7 @@
         in_specs=list(ins),
         out_specs=out_specs,
         scratch_shapes=list(scratch),
+        input_output_aliases=aliases or {},
         cost_estimate=pl.CostEstimate(
             flops=int(flops), transcendentals=0, bytes_accessed=int(moved)
         ),
@@ -120,30 +123,75 @@
     return lax.all_to_all(slots, "lon", split_axis=0, concat_axis=0, tiled=True)
 
 
-def send_rows(placed_rows, rows, staged_ref, out_ref, sems):
+def send_rows(placed_ref, rows, staged_ref, out_ref, sems):
     copies = []
+    step = out_ref.shape[0] // sems.shape[0]
     for i in range(sems.shape[0]):
-        step = out_ref.shape[0] // sems.shape[0]
         part = slice(i * step, (i + 1) * step)
-        staged_ref[part] = dot(placed_rows(i * step, step), rows).astype(BF16)
+        staged_ref[part] = dot(placed_ref[part], rows).astype(BF16)
         copies.append(pltpu.make_async_copy(staged_ref.at[part], out_ref.at[part], sems.at[i]))
         copies[-1].start()
     return copies
 
 
-def slot_kernel(capacity, ids_ref, row_ref, col_ref):
-    tokens = ids_ref.shape[1]
-    expert_total = 2 * tokens // capacity
+def origins(tokens, height, lateral):
+    across = lateral // WIN
+    place = iota((tokens, 1), 0)
+    which, inside = place // (WIN * WIN), place % (WIN * WIN)
+    row = which // across * WIN + inside // WIN + SHIFT
+    column = which % across * WIN + inside % WIN + SHIFT
+    right_base = tokens
+    low_base = right_base + height * SHIFT
+    corner_base = low_base + SHIFT * lateral
+    local = row * lateral + column
+    from_right = right_base + row * SHIFT + column - lateral
+    from_low = low_base + (row - height) * lateral + column
+    from_corner = corner_base + (row - height) * SHIFT + column - lateral
+    return jnp.where(
+        row < height,
+        jnp.where(column < lateral, local, from_right),
+        jnp.where(column < lateral, from_low, from_corner),
+    )
+
+
+def plan_kernel(
+    expert_total,
+    height,
+    lateral,
+    ids_far,
+    cot_far,
+    col_ref,
+    placed_ref,
+    moves_ref,
+    send_ref,
+    ids_ref,
+    cot_ref,
+    staged,
+    load_sems,
+    sems,
+):
+    load_ids = pltpu.make_async_copy(ids_far, ids_ref, load_sems.at[0])
+    load_cot = pltpu.make_async_copy(cot_far, cot_ref, load_sems.at[1])
+    load_ids.start()
+    load_cot.start()
+    tokens, width = cot_ref.shape
+    slot_total = placed_ref.shape[0]
+    moves_ref[...] = flag(iota(moves_ref.shape, 1) == origins(tokens, height, lateral))
+    before = flag(iota((tokens, tokens), 0) < iota((tokens, tokens), 1))
+    load_ids.wait()
     ids = ids_ref[...]
     onehot = iota((expert_total, tokens), 0) == ids
-    before = flag(iota((tokens, tokens), 0) < iota((tokens, tokens), 1))
     earlier = dot(flag(onehot), before)
     slot = jnp.sum(jnp.where(onehot, earlier, 0.0), axis=0, keepdims=True).astype(I32)
-    target = ids * capacity + slot
-    row_ref[...] = target
+    target = ids * (slot_total // expert_total) + slot
+    placed_ref[...] = flag(iota(placed_ref.shape, 0) == target)
+    load_cot.wait()
+    copies = send_rows(placed_ref, cot_ref[...], staged, send_ref.at[:, width:], sems)
     diagonal = iota((tokens, tokens), 0) == iota((tokens, tokens), 1)
     column = jnp.sum(jnp.where(diagonal, target, 0).astype(F32), axis=1, keepdims=True)
     col_ref[...] = jnp.broadcast_to(column.astype(I32), col_ref.shape)
+    for copy in copies:
+        copy.wait()
 
 
 def mask_kernel(
@@ -173,7 +221,7 @@
     own = iota((tokens, lateral), 0) % lateral == iota((tokens, lateral), 1)
     hidden_patch = jnp.sum(jnp.where(own, spread, 0.0), axis=1, keepdims=True)
     masked = jnp.where(
-        hidden_patch > 0.5, token_ref[...].astype(F32), patches[...].astype(F32)
+        hidden_patch > 0.5, token_ref[...].astype(F32)[None, :], patches[...].astype(F32)
     ).astype(BF16)
     masked_ref[...] = masked
     low_ref[...] = masked[: SHIFT * lateral]
@@ -193,14 +241,15 @@
     right_ref,
     low_ref,
     corner_ref,
-    row_ref,
+    placed_ref,
+    moves_ref,
+    sent_far,
     qkv_far,
     proj_far,
     scale_far,
     bias_far,
     attn_gain_far,
     moe_gain_far,
-    cot_far,
     hidden_ref,
     send_ref,
     qkv_ref,
@@ -209,12 +258,12 @@
     bias_ref,
     attn_gain_ref,
     moe_gain_ref,
-    sent_ref,
     blended_ref,
     staged,
     load_sems,
     sems,
 ):
+    del sent_far
     loads = [
         pltpu.make_async_copy(source, target, load_sems.at[i])
         for i, (source, target) in enumerate(
@@ -225,7 +274,6 @@
                 (proj_far, proj_ref),
                 (attn_gain_far, attn_gain_ref),
                 (moe_gain_far, moe_gain_ref),
-                (cot_far, sent_ref.at[:, cot_far.shape[1] :]),
             )
         )
     ]
@@ -239,24 +287,7 @@
 
     source = jnp.concatenate([masked_ref[...], right_ref[...], low_ref[...], corner_ref[...]], axis=0)
 
-    place = iota((tokens, 1), 0)
-    which, inside = place // window, place % window
-    row = which // across * WIN + inside // WIN + SHIFT
-    column = which % across * WIN + inside % WIN + SHIFT
-    right_base = tokens
-    low_base = right_base + height * SHIFT
-    corner_base = low_base + SHIFT * lateral
-    local = row * lateral + column
-    from_right = right_base + row * SHIFT + column - lateral
-    from_low = low_base + (row - height) * lateral + column
-    from_corner = corner_base + (row - height) * SHIFT + column - lateral
-    origin = jnp.where(
-        row < height,
-        jnp.where(column < lateral, local, from_right),
-        jnp.where(column < lateral, from_low, from_corner),
-    )
-    moves = flag(iota((tokens, source.shape[0]), 1) == origin)
-    displaced_f = dot(moves, source)
+    displaced_f = dot(moves_ref[...], source)
     displaced = displaced_f.astype(BF16)
 
     loads[0].wait()
@@ -266,8 +297,8 @@
     loads[1].wait()
     queries = projected[:, :width].astype(F32)
     keys = projected[:, width : 2 * width].astype(F32)
-    query_norm = lax.rsqrt(dot_split(queries * queries, head_of) + 1e-06) * scale_ref[...]
-    key_norm = lax.rsqrt(dot_split(keys * keys, head_of) + 1e-06)
+    query_norm = lax.rsqrt(dot((queries * queries).astype(BF16), head_of) + 1e-06) * scale_ref[...]
+    key_norm = lax.rsqrt(dot((keys * keys).astype(BF16), head_of) + 1e-06)
     queries = (queries * dot_split(query_norm, of_head)).astype(BF16)
     keys = (keys * dot_split(key_norm, of_head)).astype(BF16)
 
@@ -309,14 +340,8 @@
     hidden = hidden.reshape(tokens, width).astype(BF16)
     hidden_ref[...] = hidden
     normed, _ = normal_form(hidden.astype(F32))
-    sent_ref[:, :width] = (normed * moe_gain_ref[...]).astype(BF16)
-    copies = send_rows(
-        lambda start, step: flag(iota((step, tokens), 0) + start == row_ref[...]),
-        sent_ref[...],
-        staged,
-        send_ref,
-        sems,
-    )
+    normed = (normed * moe_gain_ref[...]).astype(BF16)
+    copies = send_rows(placed_ref, normed, staged, send_ref.at[:, :width], sems)
     for copy in copies:
         copy.wait()
 
@@ -450,56 +475,78 @@
         out_ref[:, 0, i * units : (i + 1) * units] = total
 
 
-def ready_kernel(
-    capacity, col_ref, hidden_ref, router_ref, gain_ref, picks_ref, xhat_ref, gate_ref, inv_ref
-):
+def ready_kernel(capacity, col_ref, hidden_ref, router_ref, gain_ref, facts_ref):
     tokens = hidden_ref.shape[0]
-    picks_ref[...] = flag(iota(picks_ref.shape, 1) == col_ref[:, :1])
-    xhat, inv_std = normal_form(hidden_ref[...].astype(F32))
-    xhat_ref[...] = xhat
-    inv_ref[...] = jnp.broadcast_to(inv_std, inv_ref.shape)
-    chosen = iota((tokens, router_ref.shape[0]), 1) == col_ref[:, :1] // capacity
+    hidden = hidden_ref[...].astype(F32)
+    average = jnp.mean(hidden, axis=-1, keepdims=True)
+    xhat, inv_std = normal_form(hidden)
+    target = col_ref[:, :1]
+    chosen = iota((tokens, router_ref.shape[0]), 1) == target // capacity
     logits = dot_nt((xhat * gain_ref[...]).astype(BF16), router_ref[...])
     gate = jax.nn.sigmoid(jnp.sum(jnp.where(chosen, logits, 0.0), axis=1, keepdims=True))
-    gate_ref[...] = jnp.broadcast_to(gate, gate_ref.shape)
+    lane = iota(facts_ref.shape, 1)
+    facts = jnp.where(lane == 0, target.astype(F32), gate)
+    facts_ref[...] = jnp.where(lane == 2, average, jnp.where(lane == 3, inv_std, facts))
 
 
 def final_kernel(
     capacity,
     grads_ref,
-    picks_ref,
-    xhat_ref,
-    gate_ref,
-    inv_ref,
-    col_ref,
+    facts_far,
+    hidden_far,
+    cot_far,
+    router_far,
+    gain_far,
     back_ref,
+    block_ref,
+    mixer_ref,
+    facts_ref,
     hidden_ref,
     cot_ref,
     router_ref,
     gain_ref,
-    block_ref,
-    mixer_ref,
     block,
     mixer,
+    load_sems,
     sems,
 ):
     del grads_ref
+    loads = [
+        pltpu.make_async_copy(source, target, load_sems.at[i])
+        for i, (source, target) in enumerate(
+            (
+                (facts_far, facts_ref),
+                (hidden_far, hidden_ref),
+                (cot_far, cot_ref),
+                (router_far, router_ref),
+                (gain_far, gain_ref),
+            )
+        )
+    ]
+    for load in loads:
+        load.start()
     tokens, width = hidden_ref.shape
     span = tokens // PARTS
     copies = []
+    loads[0].wait()
     for i in range(PARTS):
         here = slice(i * span, (i + 1) * span)
-        both = dot(picks_ref[here], back_ref[...])
+        target = facts_ref[here, 0:1].astype(I32)
+        gate, average, inv_std = (facts_ref[here, j : j + 1] for j in (1, 2, 3))
+        both = dot(flag(iota((span, back_ref.shape[0]), 1) == target), back_ref[...])
+        if i == 0:
+            for load in loads[1:]:
+                load.wait()
         expert_out, dnormed = both[:, :width], both[:, width:]
-        gate, cot = gate_ref[here, :1], cot_ref[here].astype(F32)
-        block[here] = (hidden_ref[here].astype(F32) + gate * expert_out).astype(BF16)
+        hidden, cot = hidden_ref[here].astype(F32), cot_ref[here].astype(F32)
+        block[here] = (hidden + gate * expert_out).astype(BF16)
         dlogit = jnp.sum(cot * expert_out, axis=1, keepdims=True) * gate * (1.0 - gate)
-        chosen = flag(iota((span, router_ref.shape[0]), 1) == col_ref[here, :1] // capacity)
+        chosen = flag(iota((span, router_ref.shape[0]), 1) == target // capacity)
         dnormed = dnormed + dlogit * dot(chosen, router_ref[...])
-        scaled, xhat = dnormed * gain_ref[...], xhat_ref[here]
+        scaled, xhat = dnormed * gain_ref[...], (hidden - average) * inv_std
         first = jnp.mean(scaled, axis=-1, keepdims=True)
         second = jnp.mean(scaled * xhat, axis=-1, keepdims=True)
-        mixer[here] = cot + inv_ref[here, :1] * (scaled - first - xhat * second)
+        mixer[here] = cot + inv_std * (scaled - first - xhat * second)
         for j, (source, target) in enumerate(((block, block_ref), (mixer, mixer_ref))):
             copies.append(pltpu.make_async_copy(source.at[here], target.at[here], sems.at[i, j]))
             copies[-1].start()
@@ -546,7 +593,7 @@
         (FAR, FAR, WHOLE),
         kept_far(patches.reshape(tokens, width)),
         kept_far(patch_mask),
-        mask_token.reshape(1, width),
+        mask_token,
         scratch=[
             pltpu.VMEM((tokens, width), BF16),
             pltpu.VMEM((height, lateral), I32),
@@ -557,11 +604,27 @@
     low = passed_along(low, "lat", -1)
     corner = passed_diagonally(corner)
 
-    target_row, target_col = call(
-        lambda *refs: slot_kernel(capacity, *refs),
-        (shape((1, tokens), I32), shape((tokens, 128), I32)),
-        (WHOLE,),
-        expert_ids.reshape(1, tokens),
+    halo_total = (height + lateral + SHIFT) * SHIFT
+    target_col, placed, moves, send = call(
+        lambda *refs: plan_kernel(expert_total, height, lateral, *refs),
+        (
+            shape((tokens, 128), I32),
+            shape((slot_total, tokens), BF16),
+            shape((tokens, tokens + halo_total), BF16),
+            far((slot_total, 2 * width), BF16),
+        ),
+        (FAR, FAR),
+        kept_far(expert_ids.reshape(1, tokens)),
+        kept_far(cot),
+        out_specs=(WHOLE, WHOLE, WHOLE, FAR),
+        scratch=[
+            pltpu.VMEM((1, tokens), I32),
+            pltpu.VMEM((tokens, width), BF16),
+            pltpu.VMEM((slot_total, width), BF16),
+            dma((2,)),
+            dma((PARTS,)),
+        ],
+        flops=2 * slot_total * tokens * width,
     )
     last = (lax.axis_index("lat") == lax.axis_size("lat") - 1).astype(I32).reshape(1)
     hidden, send = call(
@@ -570,20 +633,22 @@
             far((tokens, width), BF16),
             far((slot_total, 2 * width), BF16),
         ),
-        (SCALAR,) + (WHOLE,) * 5 + (FAR,) * 7,
+        (SCALAR,) + (WHOLE,) * 6 + (FAR,) * 7,
         last,
         masked,
         right,
         low,
         corner,
-        target_row,
+        placed,
+        moves,
+        kept_far(send),
         kept_far(w_qkv),
         kept_far(w_proj),
         kept_far(logit_scale.reshape(1, heads)),
         kept_far(rel_bias),
         kept_far(attn_gain.reshape(1, width)),
         kept_far(moe_gain.reshape(1, width)),
-        kept_far(cot),
+        aliases={7: 1},
         out_specs=(WHOLE, FAR),
         scratch=[
             pltpu.VMEM(w_qkv.shape, BF16),
@@ -592,14 +657,13 @@
             pltpu.VMEM(rel_bias.shape, F32),
             pltpu.VMEM((1, width), F32),
             pltpu.VMEM((1, width), F32),
-            pltpu.VMEM((tokens, 2 * width), BF16),
             pltpu.VMEM((tokens, width), BF16),
-            pltpu.VMEM((slot_total, 2 * width), BF16),
-            dma((7,)),
+            pltpu.VMEM((slot_total, width), BF16),
+            dma((6,)),
             dma((PARTS,)),
         ],
         vmem=32,
-        flops=2 * tokens * width * (6 * width + 2 * slot_total),
+        flops=2 * tokens * width * (6 * width + slot_total),
     )
     slots = exchanged(send.reshape(expert_total, capacity, 2 * width)).reshape(
         slot_total, 2 * width
@@ -668,10 +732,9 @@
         total_kernel, far((rows, 1, 2 * units), F32), (WHOLE,) * 3, own, up, down
     )
     moe_row = moe_gain.reshape(1, width)
-    thin = shape((tokens, 128), F32)
-    picks, xhat, gate, inv_std = call(
+    facts = call(
         lambda *refs: ready_kernel(capacity, *refs),
-        (shape((tokens, slot_total), BF16), shape((tokens, width), F32), thin, thin),
+        far((tokens, 128), F32),
         (WHOLE,) * 4,
         target_col,
         hidden,
@@ -682,22 +745,24 @@
     block_out, mixer_grad = call(
         lambda *refs: final_kernel(capacity, *refs),
         (far((tokens, width), BF16), far((tokens, width), F32)),
-        (UNREAD,) + (WHOLE,) * 10,
+        (UNREAD,) + (FAR,) * 5 + (WHOLE,),
         kept_far(weight_grads),
-        picks,
-        xhat,
-        gate,
-        inv_std,
-        target_col,
+        kept_far(facts),
+        kept_far(hidden),
+        kept_far(cot),
+        kept_far(router_t),
+        kept_far(moe_row),
         back,
-        hidden,
-        cot,
-        router_t,
-        moe_row,
         out_specs=(FAR, FAR),
         scratch=[
+            pltpu.VMEM((tokens, 128), F32),
+            pltpu.VMEM((tokens, width), BF16),
+            pltpu.VMEM((tokens, width), BF16),
+            pltpu.VMEM((expert_total, width), BF16),
+            pltpu.VMEM((1, width), F32),
             pltpu.VMEM((tokens, width), BF16),
             pltpu.VMEM((tokens, width), F32),
+            dma((5,)),
             dma((PARTS, 2)),
         ],
         flops=4 * slot_total * tokens * width,

time: 162 us -> 157 us (0.969)
  local copies, waits for them, and re-layouts: 10.5 us -> 2.27 us
  Pallas kernels: 41 us -> 45 us
    unnamed x28 -> x12, local copies, waits for them, and re-layouts: 9.84 us -> 2.27 us
    pallas_call x10, Pallas kernels: 41 us -> 45 us  [call(): pl.pallas_call(body, grid=grid, out_shape=outs, in_specs=list(ins), out_s...]
    ppermute x1, waiting for transfers between devices: 1.75 us -> 0.01 us  [passed_diagonally(): return lax.ppermute(block, ('lat', 'lon'), route)]
    ppermute x6, waiting for transfers between devices: 17 us -> 18.7 us  [passed_along(): return lax.ppermute(block, axis, route)]
  transfers between devices with their start and end apart: 10 -> 10, of which waited for: 8 -> 7; matrix products, arithmetic and copies ran while one was open for 0% -> 0% of each run, Pallas kernels for 8% -> 10%
where the time goes in v4:
time: 157 us
  waiting for transfers between devices  80.5 us (51%)
  Pallas kernels  45 us (29%)
  starting transfers between devices  27.8 us (18%)
  local copies, waits for them, and re-layouts  2.27 us (1%)
    all_to_all x2, waiting for transfers between devices, exchanged(): return lax.all_to_all(slots, 'lon', split_axis=0, concat_axis=0, tiled=True)  57.7 us
    pallas_call x10, Pallas kernels, call(): pl.pallas_call(body, grid=grid, out_shape=outs, in_specs=list(ins), out_s...  45 us
    ppermute x6, waiting for transfers between devices, passed_along(): return lax.ppermute(block, axis, route)  18.7 us
    all_to_all x2, starting transfers between devices, exchanged(): return lax.all_to_all(slots, 'lon', split_axis=0, concat_axis=0, tiled=True)  14.2 us
    ppermute x6, starting transfers between devices, passed_along(): return lax.ppermute(block, axis, route)  12.8 us
    ppermute x1, waiting for transfers between devices, per_device(): given = lax.ppermute(give, 'lat', [(i, i ^ 1) for i in range(lat_total)])  4.01 us
  transfers between devices with their start and end apart: 10, of which 7 were waited for; matrix products, arithmetic and copies ran while one was open for 0% of the time, Pallas kernels for 10%

profile of v4, /device:TPU:6, one launch (start us, length us, event | category | flops | bytes accessed | tf_op | source)
XLA Modules:
  0.0 156.6 jit_solution(13098314186622740359)
XLA Ops:
  0.6 0.0 copy-start.5
  0.6 0.7 copy-done.5
  1.3 2.1 %shard_map.157 = (bf16[512,512]{1,0:T(8,128)(2,1)S(1)}, bf16[64,512]{1,0:T(8,128)(2,1)}, bf16[128,512]{1,0:T(8,128)(2,1)}, bf16[16,512]{1,0:T(8,128)(2,1)}) custom-call(bf16[512,512]{1,0:T(8,128)(2,1)} %bitcast.30, s32[16,32]{1,0:T(8,128)} %mask_ref.1, bf16[512]{0:T(512)(128)(2,1)S(1)} %copy-done.5), custom_call_target="tpu_custom_call" | custom-call | bytes 1264640 | tf_op jit(solution)/shard_map/pallas_call | solution.py:30
  3.5 0.3 collective-permute-start.1
  3.7 8.3 %collective-permute-start = (bf16[64,512]{1,0:T(8,128)(2,1)}, bf16[64,512]{1,0:T(8,128)(2,1)S(1)}, u32[]{:S(2)}, u32[]{:S(2)}) collective-permute-start(bf16[64,512]{1,0:T(8,128)(2,1)} %get-tuple-element.28), channel_id=1, source_target_pairs={{1,0},{2,1},{3,2},{4,3},{5,4},{6,5},{7,6},{8,7},{9,8},{10,9},{11,1... | collective-permute-start | bytes 196616 | tf_op jit(solution)/shard_map/ppermute | solution.py:109
  12.0 0.6 collective-permute-start.2
  12.6 2.9 %shard_map.158 = (s32[512,128]{1,0:T(8,128)S(1)}, bf16[1024,512]{1,0:T(8,128)(2,1)S(1)}, bf16[512,720]{1,0:T(8,128)(2,1)S(1)}, bf16[1024,1024]{1,0:T(8,128)(2,1)}) custom-call(s32[1,512]{1,0:T(1,128)} %bitcast.37, bf16[512,512]{1,0:T(8,128)(2,1)} %bitcast.31), custom_call_target="tpu_custom_call" | custom-call | flops 536870912 | bytes 4671488 | tf_op jit(solution)/shard_map/pallas_call | solution.py:30
  15.5 0.0 collective-permute-done.2.refs_4_
  15.5 0.0 collective-permute-done.refs_2_
  15.5 0.0 collective-permute-done.1.refs_3_
  15.5 8.6 %shard_map.159 = (bf16[512,512]{1,0:T(8,128)(2,1)}, bf16[1024,1024]{1,0:T(8,128)(2,1)}) custom-call(s32[1]{0:T(128)} %bitcast.2.refs_0_, bf16[512,512]{1,0:T(8,128)(2,1)S(1)} %get-tuple-element.27.refs_1_, bf16[64,512]{1,0:T(8,128)(2,1)S(1)} %collective-permute-done.refs_2_, ...), custom_call_target="tpu_custom_call", output_to_operand_aliasing={{1}: (7, {})} | custom-call | flops 2147483648 | bytes 9605188 | tf_op jit(solution)/shard_map/pallas_call | solution.py:30
  24.2 0.0 copy-start.3
  24.2 6.5 %all-to-all-start = ((bf16[32,32,1024]{2,1,0:T(8,128)(2,1)}), bf16[32,32,1024]{2,1,0:T(8,128)(2,1)S(1)}, u32[]{:S(2)}, u32[]{:S(2)}) async-start(bf16[32,32,1024]{2,1,0:T(8,128)(2,1)} %bitcast.29), calls=%async_computation | async-start | bytes 4194304 | tf_op jit(solution)/shard_map/all_to_all | solution.py:123
  30.6 0.1 pad_add_fusion.index_ref.refs_0_
  30.7 49.1 %all-to-all-done = bf16[32,32,1024]{2,1,0:T(8,128)(2,1)S(1)} async-done(((bf16[32,32,1024]{2,1,0:T(8,128)(2,1)}), bf16[32,32,1024]{2,1,0:T(8,128)(2,1)S(1)}, u32[]{:S(2)}, u32[]{:S(2)}) %all-to-all-start) | async-done | bytes 2097184 | tf_op jit(solution)/shard_map/all_to_all | solution.py:123
  79.9 0.0 copy-start
  79.9 0.0 copy-done.3
  79.9 14.0 %shard_map.160 = (bf16[1024,1024]{1,0:T(8,128)(2,1)}, bf16[1024,2048]{1,0:T(8,128)(2,1)}, bf16[1024,2048]{1,0:T(8,128)(2,1)}) custom-call(s32[2]{0:T(128)S(1)} %pad_add_fusion.index_ref.refs_0_, bf16[1024,1024]{1,0:T(8,128)(2,1)S(1)} %bitcast.19, bf16[32,512]{1,0:T(8,128)(2,1)S(1)} %bitcast.22, bf16[512,2048]{1,0:T(8,128)(2,1)} %bitcast.33, ...), custom_call_target="tpu_custom_call" | custom-call | flops 8589934592 | bytes 16809992 | tf_op jit(solution)/shard_map/pallas_call | solution.py:30
  93.9 0.0 copy-done
  93.9 7.7 %all-to-all-start.1 = ((bf16[32,32,1024]{2,1,0:T(8,128)(2,1)}), bf16[32,32,1024]{2,1,0:T(8,128)(2,1)S(1)}, u32[]{:S(2)}, u32[]{:S(2)}) async-start(bf16[32,32,1024]{2,1,0:T(8,128)(2,1)} %bitcast.28), calls=%async_computation.1 | async-start | bytes 4194304 | tf_op jit(solution)/shard_map/all_to_all | solution.py:123
  101.7 0.0 copy-start.1
  101.7 1.6 %copy-done.1 = bf16[32,32,1024]{2,1,0:T(8,128)(2,1)S(1)} copy-done((bf16[32,32,1024]{2,1,0:T(8,128)(2,1)S(1)}, bf16[32,32,1024]{2,1,0:T(8,128)(2,1)}, u32[]{:S(2)}) %copy-start.1) | copy-done | bytes 2097176
  103.2 9.4 %shard_map.161 = (bf16[2,256,2048]{2,1,0:T(8,128)(2,1)S(1)}, bf16[2,256,2048]{2,1,0:T(8,128)(2,1)S(1)}) custom-call(s32[2]{0:T(128)S(1)} %pad_add_fusion.index_ref.refs_0_, bf16[1024,1024]{1,0:T(8,128)(2,1)S(1)} %bitcast.20, bf16[32,512]{1,0:T(8,128)(2,1)S(1)} %bitcast.23, bf16[1024,2048]{1,0:T(8,128)(2,1)} %get-tuple-element.35.refs_3_, ...), custom_call_target="tpu_custom_call" | custom-call | flops 4294967296 | bytes 14712840 | tf_op jit(solution)/shard_map/pallas_call | solution.py:30
  112.7 0.2 collective-permute-start.3
  112.9 4.0 %collective-permute-done.3.given_ref = bf16[2,256,2048]{2,1,0:T(8,128)(2,1)S(1)} collective-permute-done((bf16[2,256,2048]{2,1,0:T(8,128)(2,1)S(1)}, bf16[2,256,2048]{2,1,0:T(8,128)(2,1)S(1)}, u32[]{:S(2)}, u32[]{:S(2)}) %collective-permute-start.3) | collective-permute-done | bytes 2097184 | tf_op jit(solution)/shard_map/ppermute | solution.py:721
  116.9 0.0 copy-start.2
  117.0 0.0 copy-start.4
  117.0 0.5 shard_map.162
  117.5 0.9 collective-permute-start.4
  118.4 1.2 collective-permute-start.5
  119.6 6.3 %collective-permute-done.4.up_part_ref = bf16[64,2048]{1,0:T(8,128)(2,1)S(1)} collective-permute-done((bf16[64,2048]{1,0:T(8,128)(2,1)S(1)}, bf16[64,2048]{1,0:T(8,128)(2,1)S(1)}, u32[]{:S(2)}, u32[]{:S(2)}) %collective-permute-start.4) | collective-permute-done | bytes 262176 | tf_op jit(solution)/shard_map/ppermute | solution.py:109
  125.9 1.7 %collective-permute-done.5.down_part_ref = bf16[64,2048]{1,0:T(8,128)(2,1)S(1)} collective-permute-done((bf16[64,2048]{1,0:T(8,128)(2,1)S(1)}, bf16[64,2048]{1,0:T(8,128)(2,1)S(1)}, u32[]{:S(2)}, u32[]{:S(2)}) %collective-permute-start.5) | collective-permute-done | bytes 262176 | tf_op jit(solution)/shard_map/ppermute | solution.py:109
  127.6 0.1 shard_map.163
  127.8 0.6 collective-permute-start.6
  128.3 1.5 collective-permute-start.7
  129.9 0.0 copy-done.2
  129.9 0.0 copy-done.4
  129.9 1.6 %shard_map.165.refs_1_ = f32[512,128]{1,0:T(8,128)} custom-call(s32[512,128]{1,0:T(8,128)S(1)} %get-tuple-element.46.refs_0_, bf16[512,512]{1,0:T(8,128)(2,1)S(1)} %copy-done.2, bf16[32,512]{1,0:T(8,128)(2,1)S(1)} %bitcast.24, f32[1,512]{1,0:T(1,128)S(1)} %bitcast.27), custom_call_target="tpu_custom_call" | custom-call | flops 536870912 | bytes 1083392 | tf_op jit(solution)/shard_map/pallas_call | solution.py:30
  131.5 9.1 %collective-permute-done.6.up_ref = bf16[2,64,2048]{2,1,0:T(8,128)(2,1)S(1)} collective-permute-done((bf16[2,64,2048]{2,1,0:T(8,128)(2,1)S(1)}, bf16[2,64,2048]{2,1,0:T(8,128)(2,1)S(1)}, u32[]{:S(2)}, u32[]{:S(2)}) %collective-permute-start.6) | collective-permute-done | bytes 524320 | tf_op jit(solution)/shard_map/ppermute | solution.py:109
  140.7 1.5 collective-permute-done.7.down_ref
  142.2 1.3 shard_map.164.refs_0_
  143.5 8.6 %all-to-all-done.1 = bf16[32,32,1024]{2,1,0:T(8,128)(2,1)S(1)} async-done(((bf16[32,32,1024]{2,1,0:T(8,128)(2,1)}), bf16[32,32,1024]{2,1,0:T(8,128)(2,1)S(1)}, u32[]{:S(2)}, u32[]{:S(2)}) %all-to-all-start.1) | async-done | bytes 2097184 | tf_op jit(solution)/shard_map/all_to_all | solution.py:123
  152.1 4.3 %shard_map.166 = (bf16[512,512]{1,0:T(8,128)(2,1)}, f32[512,512]{1,0:T(8,128)}) custom-call(f32[64,1,4096]{2,1,0:T(1,128)} %shard_map.164.refs_0_, f32[512,128]{1,0:T(8,128)} %shard_map.165.refs_1_, bf16[512,512]{1,0:T(8,128)(2,1)} %get-tuple-element.47.refs_1_.refs_2_, bf16[512,512]{1,0:T(8,128)(2,1)} %bitcast.32, bf16[32,512]{1,0:T(8,128)(2,1)} %bitcast.21, ...), custom_call_target="tpu_custom_call" | custom-call | flops 1073741824 | bytes 6064128 | tf_op jit(solution)/shard_map/pallas_call | solution.py:30
Async XLA Ops:
  0.6 0.7 copy-start.5
  3.5 12.1 %collective-permute-start.1 = (bf16[128,512]{1,0:T(8,128)(2,1)}, bf16[128,512]{1,0:T(8,128)(2,1)S(1)}, u32[]{:S(2)}, u32[]{:S(2)}) collective-permute-start(bf16[128,512]{1,0:T(8,128)(2,1)} %get-tuple-element.29), channel_id=1, source_target_pairs={{32,0},{64,32},{96,64},{128,96},{160,128},{192,160},{224,192},{0,2... | collective-permute-start | bytes 393224 | tf_op jit(solution)/shard_map/ppermute | solution.py:109
  3.7 11.8 %collective-permute-start = (bf16[64,512]{1,0:T(8,128)(2,1)}, bf16[64,512]{1,0:T(8,128)(2,1)S(1)}, u32[]{:S(2)}, u32[]{:S(2)}) collective-permute-start(bf16[64,512]{1,0:T(8,128)(2,1)} %get-tuple-element.28), channel_id=1, source_target_pairs={{1,0},{2,1},{3,2},{4,3},{5,4},{6,5},{7,6},{8,7},{9,8},{10,9},{11,1... | collective-permute-start | bytes 196616 | tf_op jit(solution)/shard_map/ppermute | solution.py:109
  12.0 3.5 %collective-permute-start.2 = (bf16[16,512]{1,0:T(8,128)(2,1)}, bf16[16,512]{1,0:T(8,128)(2,1)S(1)}, u32[]{:S(2)}, u32[]{:S(2)}) collective-permute-start(bf16[16,512]{1,0:T(8,128)(2,1)} %get-tuple-element.30), channel_id=1, source_target_pairs={{33,0},{34,1},{35,2},{36,3},{37,4},{38,5},{39,6},{40,7},{41,8},{42... | collective-permute-start | bytes 49160 | tf_op jit(solution)/shard_map/ppermute | solution.py:119
  24.2 55.7 %copy-start.3 = (bf16[512,32]{0,1:T(8,128)(2,1)S(1)}, bf16[512,32]{0,1:T(8,128)(2,1)}, u32[]{:S(2)}) copy-start(bf16[512,32]{0,1:T(8,128)(2,1)} %param.23) | copy-start | bytes 98308
  24.2 55.7 %all-to-all-start = ((bf16[32,32,1024]{2,1,0:T(8,128)(2,1)}), bf16[32,32,1024]{2,1,0:T(8,128)(2,1)S(1)}, u32[]{:S(2)}, u32[]{:S(2)}) async-start(bf16[32,32,1024]{2,1,0:T(8,128)(2,1)} %bitcast.29), calls=%async_computation | async-start | bytes 4194304 | tf_op jit(solution)/shard_map/all_to_all | solution.py:123
  79.9 14.0 %copy-start = (bf16[32,32,1024]{2,1,0:T(8,128)(2,1)}, bf16[32,32,1024]{2,1,0:T(8,128)(2,1)S(1)}, u32[]{:S(2)}) copy-start(bf16[32,32,1024]{2,1,0:T(8,128)(2,1)S(1)} %all-to-all-done) | copy-start | bytes 6291460
  93.9 58.2 %all-to-all-start.1 = ((bf16[32,32,1024]{2,1,0:T(8,128)(2,1)}), bf16[32,32,1024]{2,1,0:T(8,128)(2,1)S(1)}, u32[]{:S(2)}, u32[]{:S(2)}) async-start(bf16[32,32,1024]{2,1,0:T(8,128)(2,1)} %bitcast.28), calls=%async_computation.1 | async-start | bytes 4194304 | tf_op jit(solution)/shard_map/all_to_all | solution.py:123
  101.7 1.6 %copy-start.1 = (bf16[32,32,1024]{2,1,0:T(8,128)(2,1)S(1)}, bf16[32,32,1024]{2,1,0:T(8,128)(2,1)}, u32[]{:S(2)}) copy-start(bf16[32,32,1024]{2,1,0:T(8,128)(2,1)} %copy-done) | copy-start | bytes 6291460
  112.7 4.2 %collective-permute-start.3 = (bf16[2,256,2048]{2,1,0:T(8,128)(2,1)S(1)}, bf16[2,256,2048]{2,1,0:T(8,128)(2,1)S(1)}, u32[]{:S(2)}, u32[]{:S(2)}) collective-permute-start(bf16[2,256,2048]{2,1,0:T(8,128)(2,1)S(1)} %get-tuple-element.38), channel_id=1, source_target_pairs={{0,32},{32,0},{64,96},{96,64},{128,160},{160,128},{192,224},{224,1... | collective-permute-start | bytes 6291464 | tf_op jit(solution)/shard_map/ppermute | solution.py:721
  116.9 12.9 %copy-start.2 = (bf16[512,512]{1,0:T(8,128)(2,1)S(1)}, bf16[512,512]{1,0:T(8,128)(2,1)}, u32[]{:S(2)}) copy-start(bf16[512,512]{1,0:T(8,128)(2,1)} %get-tuple-element.47.refs_1_.refs_2_) | copy-start | bytes 1572868
  117.0 12.9 %copy-start.4 = (f32[512]{0:T(512)S(1)}, f32[512]{0:T(512)}, u32[]{:S(2)}) copy-start(f32[512]{0:T(512)} %param.22) | copy-start | bytes 6148
  117.5 8.4 %collective-permute-start.4 = (bf16[64,2048]{1,0:T(8,128)(2,1)S(1)}, bf16[64,2048]{1,0:T(8,128)(2,1)S(1)}, u32[]{:S(2)}, u32[]{:S(2)}) collective-permute-start(bf16[64,2048]{1,0:T(8,128)(2,1)S(1)} %get-tuple-element.42), channel_id=1, source_target_pairs={{192,0},{224,32},{0,64},{32,96},{64,128},{96,160},{128,192},{160,2... | collective-permute-start | bytes 786440 | tf_op jit(solution)/shard_map/ppermute | solution.py:109
  118.4 9.3 %collective-permute-start.5 = (bf16[64,2048]{1,0:T(8,128)(2,1)S(1)}, bf16[64,2048]{1,0:T(8,128)(2,1)S(1)}, u32[]{:S(2)}, u32[]{:S(2)}) collective-permute-start(bf16[64,2048]{1,0:T(8,128)(2,1)S(1)} %get-tuple-element.43), channel_id=1, source_target_pairs={{64,0},{96,32},{128,64},{160,96},{192,128},{224,160},{0,192},{32,2... | collective-permute-start | bytes 786440 | tf_op jit(solution)/shard_map/ppermute | solution.py:109
  127.8 12.9 %collective-permute-start.6 = (bf16[2,64,2048]{2,1,0:T(8,128)(2,1)S(1)}, bf16[2,64,2048]{2,1,0:T(8,128)(2,1)S(1)}, u32[]{:S(2)}, u32[]{:S(2)}) collective-permute-start(bf16[2,64,2048]{2,1,0:T(8,128)(2,1)S(1)} %get-tuple-element.44), channel_id=1, source_target_pairs={{192,0},{224,32},{0,64},{32,96},{64,128},{96,160},{128,192},{160,2... | collective-permute-start | bytes 1572872 | tf_op jit(solution)/shard_map/ppermute | solution.py:109
  128.3 13.9 %collective-permute-start.7 = (bf16[2,64,2048]{2,1,0:T(8,128)(2,1)S(1)}, bf16[2,64,2048]{2,1,0:T(8,128)(2,1)S(1)}, u32[]{:S(2)}, u32[]{:S(2)}) collective-permute-start(bf16[2,64,2048]{2,1,0:T(8,128)(2,1)S(1)} %get-tuple-element.45), channel_id=1, source_target_pairs={{64,0},{96,32},{128,64},{160,96},{192,128},{224,160},{0,192},{32,2... | collective-permute-start | bytes 1572872 | tf_op jit(solution)/shard_map/ppermute | solution.py:109

commit v5 on v4

--- a/solution.py
+++ b/solution.py
@@ -75,11 +75,6 @@
 def halves(values):
     high = values.astype(BF16)
     return high, (values - high.astype(F32)).astype(BF16)
-
-
-def dot_split(values, ones):
-    high, low = halves(values)
-    return dot(high, ones) + dot(low, ones)
 
 
 def iota(dims, axis):
@@ -204,11 +199,13 @@
     corner_ref,
     patches,
     mask,
+    token,
     sems,
 ):
     loads = [
         pltpu.make_async_copy(patches_ref, patches, sems.at[0]),
         pltpu.make_async_copy(mask_ref, mask, sems.at[1]),
+        pltpu.make_async_copy(token_ref, token, sems.at[2]),
     ]
     for load in loads:
         load.start()
@@ -221,7 +218,7 @@
     own = iota((tokens, lateral), 0) % lateral == iota((tokens, lateral), 1)
     hidden_patch = jnp.sum(jnp.where(own, spread, 0.0), axis=1, keepdims=True)
     masked = jnp.where(
-        hidden_patch > 0.5, token_ref[...].astype(F32)[None, :], patches[...].astype(F32)
+        hidden_patch > 0.5, token[...].astype(F32)[None, :], patches[...].astype(F32)
     ).astype(BF16)
     masked_ref[...] = masked
     low_ref[...] = masked[: SHIFT * lateral]
@@ -250,8 +247,9 @@
     bias_far,
     attn_gain_far,
     moe_gain_far,
+    hidden_far,
+    send_ref,
     hidden_ref,
-    send_ref,
     qkv_ref,
     proj_ref,
     scale_ref,
@@ -262,6 +260,7 @@
     staged,
     load_sems,
     sems,
+    hidden_sem,
 ):
     del sent_far
     loads = [
@@ -299,8 +298,9 @@
     keys = projected[:, width : 2 * width].astype(F32)
     query_norm = lax.rsqrt(dot((queries * queries).astype(BF16), head_of) + 1e-06) * scale_ref[...]
     key_norm = lax.rsqrt(dot((keys * keys).astype(BF16), head_of) + 1e-06)
-    queries = (queries * dot_split(query_norm, of_head)).astype(BF16)
-    keys = (keys * dot_split(key_norm, of_head)).astype(BF16)
+    twice = jnp.concatenate([of_head, of_head], axis=0)
+    queries = (queries * dot(jnp.concatenate(halves(query_norm), axis=1), twice)).astype(BF16)
+    keys = (keys * dot(jnp.concatenate(halves(key_norm), axis=1), twice)).astype(BF16)
 
     block = group * window
     loads[2].wait()
@@ -315,22 +315,47 @@
         iota((window, block), 1) % window >= window // 2
     )
     allowed = jnp.where(split, 1.0, jnp.where(flag_ref[0] == 1, 0.0, 1.0))
-    for w in range(tokens // window):
+    groups = width // 128
+
+    def spread(rows, g, start, source):
+        part = source[rows, start + g * 128 : start + (g + 1) * 128]
+        return jnp.concatenate([part] * group, axis=0) * member
+
+    def score(w):
         rows = slice(w * window, (w + 1) * window)
-        for g in range(width // 128):
-            lanes = slice(g * 128, (g + 1) * 128)
-            q = queries[rows, lanes]
-            k = keys[rows, lanes]
-            v = projected[rows, 2 * width + g * 128 : 2 * width + (g + 1) * 128]
-            wide_k = jnp.concatenate([k] * group, axis=0) * member
-            wide_v = jnp.concatenate([v] * group, axis=0) * member
-            scores = dot_nt(q, wide_k) + biases[g]
-            weights = jnp.exp(scores)
-            if w >= across * (height // WIN - 1):
-                weights = weights * allowed
-            both = dot(weights.astype(BF16), jnp.concatenate([wide_v, member], axis=1))
-            blended_ref[rows, lanes] = (both[:, :128] / both[:, 128:]).astype(BF16)
-
+        return [
+            dot_nt(queries[rows, g * 128 : (g + 1) * 128], spread(rows, g, 0, keys)) + biases[g]
+            for g in range(groups)
+        ]
+
+    def weigh(w, scores):
+        weights = [jnp.exp(part) for part in scores]
+        if w >= across * (height // WIN - 1):
+            weights = [part * allowed for part in weights]
+        return [part.astype(BF16) for part in weights]
+
+    def blend(w, weights):
+        rows = slice(w * window, (w + 1) * window)
+        both = [
+            dot(
+                weights[g],
+                jnp.concatenate([spread(rows, g, 2 * width, projected), member], axis=1),
+            )
+            for g in range(groups)
+        ]
+        for g in range(groups):
+            part = both[g][:, :128] / both[g][:, 128:]
+            blended_ref[rows, g * 128 : (g + 1) * 128] = part.astype(BF16)
+
+    windows = tokens // window
+    scores, weights = {}, {}
+    for step in range(windows + 2):
+        if step < windows:
+            scores[step] = score(step)
+        if 0 <= step - 1 < windows:
+            weights[step - 1] = weigh(step - 1, scores.pop(step - 1))
+        if 0 <= step - 2:
+            blend(step - 2, weights.pop(step - 2))
     for load in loads[3:]:
         load.wait()
     projection = dot(blended_ref[...], proj_ref[...])
@@ -339,14 +364,17 @@
     hidden = hidden.reshape(height // WIN, across, WIN, WIN, width).transpose(0, 2, 1, 3, 4)
     hidden = hidden.reshape(tokens, width).astype(BF16)
     hidden_ref[...] = hidden
+    store = pltpu.make_async_copy(hidden_ref, hidden_far, hidden_sem.at[0])
+    store.start()
     normed, _ = normal_form(hidden.astype(F32))
     normed = (normed * moe_gain_ref[...]).astype(BF16)
     copies = send_rows(placed_ref, normed, staged, send_ref.at[:, :width], sems)
-    for copy in copies:
+    for copy in (store, *copies):
         copy.wait()
 
 
 PARTS = 4
+TILES = 4
 
 
 def expert_kernel(
@@ -368,7 +396,7 @@
 ):
     rows, width = slots_ref.shape[0], slots_ref.shape[1] // 2
     units = w_in.shape[1]
-    tile, chunk, piece = rows // PARTS, units // PARTS, width // 2
+    tile, chunk, piece = rows // TILES, units // PARTS, width // 2
 
     def load(source, target, i):
         copy = pltpu.make_async_copy(source, target, load_sems.at[i])
@@ -383,7 +411,6 @@
         part = tiled(i, chunk)
         loads.append(load(w_in_ref.at[:, part], w_in.at[:, part], 2 * i))
         loads.append(load(w_out_ref.at[:, part], w_out.at[:, part], 2 * i + 1))
-    half_gate = 0.5 * slot_gates(slots_ref[:, :width], router_ref[...], index_ref[0])
     stores = []
 
     def store(source, target):
@@ -391,11 +418,13 @@
         copy.start()
         stores.append(copy)
 
-    for r in range(PARTS + 1):
+    for r in range(TILES + 1):
         here, last = tiled(r, tile), tiled(r - 1, tile)
+        if r == 1:
+            half_gate = 0.5 * slot_gates(slots_ref[:, :width], router_ref[...], index_ref[0])
         for c in range(PARTS):
             part = tiled(c, chunk)
-            if r < PARTS:
+            if r < TILES:
                 if r == 0:
                     loads[2 * c].wait()
                     loads[2 * c + 1].wait()
@@ -412,7 +441,7 @@
                 else:
                     result = half_gate[last] * dot_nt(dpre[last], w_in[half])
                 back[last, tiled(c, piece)] = result.astype(BF16)
-        if r < PARTS:
+        if r < TILES:
             store(act.at[here], act_ref.at[here])
             store(dpre.at[here], dpre_ref.at[here])
         if r > 0:
@@ -485,13 +514,13 @@
     logits = dot_nt((xhat * gain_ref[...]).astype(BF16), router_ref[...])
     gate = jax.nn.sigmoid(jnp.sum(jnp.where(chosen, logits, 0.0), axis=1, keepdims=True))
     lane = iota(facts_ref.shape, 1)
-    facts = jnp.where(lane == 0, target.astype(F32), gate)
-    facts_ref[...] = jnp.where(lane == 2, average, jnp.where(lane == 3, inv_std, facts))
+    facts_ref[...] = jnp.where(lane == 0, gate, jnp.where(lane == 1, average, inv_std))
 
 
 def final_kernel(
     capacity,
     grads_ref,
+    col_ref,
     facts_far,
     hidden_far,
     cot_far,
@@ -528,15 +557,14 @@
     tokens, width = hidden_ref.shape
     span = tokens // PARTS
     copies = []
-    loads[0].wait()
     for i in range(PARTS):
         here = slice(i * span, (i + 1) * span)
-        target = facts_ref[here, 0:1].astype(I32)
-        gate, average, inv_std = (facts_ref[here, j : j + 1] for j in (1, 2, 3))
+        target = col_ref[here, 0:1]
         both = dot(flag(iota((span, back_ref.shape[0]), 1) == target), back_ref[...])
         if i == 0:
-            for load in loads[1:]:
+            for load in loads:
                 load.wait()
+        gate, average, inv_std = (facts_ref[here, j : j + 1] for j in range(3))
         expert_out, dnormed = both[:, :width], both[:, width:]
         hidden, cot = hidden_ref[here].astype(F32), cot_ref[here].astype(F32)
         block[here] = (hidden + gate * expert_out).astype(BF16)
@@ -590,14 +618,15 @@
             far((SHIFT * lateral, width), BF16),
             far((SHIFT * SHIFT, width), BF16),
         ),
-        (FAR, FAR, WHOLE),
+        (FAR, FAR, FAR),
         kept_far(patches.reshape(tokens, width)),
         kept_far(patch_mask),
-        mask_token,
+        kept_far(mask_token),
         scratch=[
             pltpu.VMEM((tokens, width), BF16),
             pltpu.VMEM((height, lateral), I32),
-            dma((2,)),
+            pltpu.VMEM((width,), BF16),
+            dma((3,)),
         ],
     )
     right = passed_along(right, "lon", -1)
@@ -649,8 +678,9 @@
         kept_far(attn_gain.reshape(1, width)),
         kept_far(moe_gain.reshape(1, width)),
         aliases={7: 1},
-        out_specs=(WHOLE, FAR),
+        out_specs=(FAR, FAR),
         scratch=[
+            pltpu.VMEM((tokens, width), BF16),
             pltpu.VMEM(w_qkv.shape, BF16),
             pltpu.VMEM(w_proj.shape, BF16),
             pltpu.VMEM((1, heads), F32),
@@ -661,6 +691,7 @@
             pltpu.VMEM((slot_total, width), BF16),
             dma((6,)),
             dma((PARTS,)),
+            dma((1,)),
         ],
         vmem=32,
         flops=2 * tokens * width * (6 * width + slot_total),
@@ -691,7 +722,7 @@
             pltpu.VMEM((slot_total, units), BF16),
             pltpu.VMEM((slot_total, 2 * width), BF16),
             dma((2 * PARTS,)),
-            dma((3 * PARTS,)),
+            dma((3 * TILES,)),
         ],
         vmem=40,
         flops=8 * slot_total * width * units,
@@ -745,8 +776,9 @@
     block_out, mixer_grad = call(
         lambda *refs: final_kernel(capacity, *refs),
         (far((tokens, width), BF16), far((tokens, width), F32)),
-        (UNREAD,) + (FAR,) * 5 + (WHOLE,),
+        (UNREAD, WHOLE) + (FAR,) * 5 + (WHOLE,),
         kept_far(weight_grads),
+        target_col,
         kept_far(facts),
         kept_far(hidden),
         kept_far(cot),

time: 157 us -> 155 us (0.987)
  no operation moved by 1% of the time
where the time goes in v5:
time: 155 us
  waiting for transfers between devices  80.6 us (52%)
  Pallas kernels  43.5 us (28%)
  starting transfers between devices  27.9 us (18%)
  local copies, waits for them, and re-layouts  1.6 us (1%)
    all_to_all x2, waiting for transfers between devices, exchanged(): return lax.all_to_all(slots, 'lon', split_axis=0, concat_axis=0, tiled=True)  57.7 us
    pallas_call x10, Pallas kernels, call(): pl.pallas_call(body, grid=grid, out_shape=outs, in_specs=list(ins), out_s...  43.5 us
    ppermute x6, waiting for transfers between devices, passed_along(): return lax.ppermute(block, axis, route)  18.9 us
    all_to_all x2, starting transfers between devices, exchanged(): return lax.all_to_all(slots, 'lon', split_axis=0, concat_axis=0, tiled=True)  14.2 us
    ppermute x6, starting transfers between devices, passed_along(): return lax.ppermute(block, axis, route)  12.8 us
    ppermute x1, waiting for transfers between devices, per_device(): given = lax.ppermute(give, 'lat', [(i, i ^ 1) for i in range(lat_total)])  4 us
  transfers between devices with their start and end apart: 10, of which 7 were waited for; matrix products, arithmetic and copies ran while one was open for 0% of the time, Pallas kernels for 10%

profile of v5, /device:TPU:6, one launch (start us, length us, event | category | flops | bytes accessed | tf_op | source)
XLA Modules:
  0.0 154.5 jit_solution(15144693699382917229)
XLA Ops:
  0.6 2.2 %shard_map.157 = (bf16[512,512]{1,0:T(8,128)(2,1)S(1)}, bf16[64,512]{1,0:T(8,128)(2,1)}, bf16[128,512]{1,0:T(8,128)(2,1)}, bf16[16,512]{1,0:T(8,128)(2,1)}) custom-call(bf16[512,512]{1,0:T(8,128)(2,1)} %bitcast.32, s32[16,32]{1,0:T(8,128)} %mask_ref.1, bf16[512]{0:T(512)(128)(2,1)} %token_ref.1), custom_call_target="tpu_custom_call" | custom-call | bytes 1264640 | tf_op jit(solution)/shard_map/pallas_call | solution.py:30
  2.8 0.3 collective-permute-start.1
  3.1 8.3 %collective-permute-start = (bf16[64,512]{1,0:T(8,128)(2,1)}, bf16[64,512]{1,0:T(8,128)(2,1)S(1)}, u32[]{:S(2)}, u32[]{:S(2)}) collective-permute-start(bf16[64,512]{1,0:T(8,128)(2,1)} %get-tuple-element.28), channel_id=1, source_target_pairs={{1,0},{2,1},{3,2},{4,3},{5,4},{6,5},{7,6},{8,7},{9,8},{10,9},{11,1... | collective-permute-start | bytes 196616 | tf_op jit(solution)/shard_map/ppermute | solution.py:104
  11.4 0.6 collective-permute-start.2
  12.0 2.9 %shard_map.158 = (s32[512,128]{1,0:T(8,128)S(1)}, bf16[1024,512]{1,0:T(8,128)(2,1)S(1)}, bf16[512,720]{1,0:T(8,128)(2,1)S(1)}, bf16[1024,1024]{1,0:T(8,128)(2,1)}) custom-call(s32[1,512]{1,0:T(1,128)} %bitcast.37, bf16[512,512]{1,0:T(8,128)(2,1)} %bitcast.30), custom_call_target="tpu_custom_call" | custom-call | flops 536870912 | bytes 4671488 | tf_op jit(solution)/shard_map/pallas_call | solution.py:30
  14.8 0.0 collective-permute-done.2.refs_4_
  14.9 0.0 collective-permute-done.refs_2_
  14.9 0.0 collective-permute-done.1.refs_3_
  14.9 8.0 %shard_map.159 = (bf16[512,512]{1,0:T(8,128)(2,1)}, bf16[1024,1024]{1,0:T(8,128)(2,1)}) custom-call(s32[1]{0:T(128)} %bitcast.2.refs_0_, bf16[512,512]{1,0:T(8,128)(2,1)S(1)} %get-tuple-element.27.refs_1_, bf16[64,512]{1,0:T(8,128)(2,1)S(1)} %collective-permute-done.refs_2_, ...), custom_call_target="tpu_custom_call", output_to_operand_aliasing={{1}: (7, {})} | custom-call | flops 2147483648 | bytes 9605188 | tf_op jit(solution)/shard_map/pallas_call | solution.py:30
  22.9 0.0 copy-start.3
  22.9 6.5 %all-to-all-start = ((bf16[32,32,1024]{2,1,0:T(8,128)(2,1)}), bf16[32,32,1024]{2,1,0:T(8,128)(2,1)S(1)}, u32[]{:S(2)}, u32[]{:S(2)}) async-start(bf16[32,32,1024]{2,1,0:T(8,128)(2,1)} %bitcast.29), calls=%async_computation | async-start | bytes 4194304 | tf_op jit(solution)/shard_map/all_to_all | solution.py:118
  29.3 0.1 pad_add_fusion.index_ref.refs_0_
  29.4 49.1 %all-to-all-done = bf16[32,32,1024]{2,1,0:T(8,128)(2,1)S(1)} async-done(((bf16[32,32,1024]{2,1,0:T(8,128)(2,1)}), bf16[32,32,1024]{2,1,0:T(8,128)(2,1)S(1)}, u32[]{:S(2)}, u32[]{:S(2)}) %all-to-all-start) | async-done | bytes 2097184 | tf_op jit(solution)/shard_map/all_to_all | solution.py:118
  78.5 0.0 copy-start
  78.5 0.0 copy-done.3
  78.5 13.6 %shard_map.160 = (bf16[1024,1024]{1,0:T(8,128)(2,1)}, bf16[1024,2048]{1,0:T(8,128)(2,1)}, bf16[1024,2048]{1,0:T(8,128)(2,1)}) custom-call(s32[2]{0:T(128)S(1)} %pad_add_fusion.index_ref.refs_0_, bf16[1024,1024]{1,0:T(8,128)(2,1)S(1)} %bitcast.19, bf16[32,512]{1,0:T(8,128)(2,1)S(1)} %bitcast.22, bf16[512,2048]{1,0:T(8,128)(2,1)} %bitcast.33, ...), custom_call_target="tpu_custom_call" | custom-call | flops 8589934592 | bytes 16809992 | tf_op jit(solution)/shard_map/pallas_call | solution.py:30
  92.1 0.0 copy-done
  92.1 7.8 %all-to-all-start.1 = ((bf16[32,32,1024]{2,1,0:T(8,128)(2,1)}), bf16[32,32,1024]{2,1,0:T(8,128)(2,1)S(1)}, u32[]{:S(2)}, u32[]{:S(2)}) async-start(bf16[32,32,1024]{2,1,0:T(8,128)(2,1)} %bitcast.28), calls=%async_computation.1 | async-start | bytes 4194304 | tf_op jit(solution)/shard_map/all_to_all | solution.py:118
  99.9 0.0 copy-start.1
  99.9 1.6 %copy-done.1 = bf16[32,32,1024]{2,1,0:T(8,128)(2,1)S(1)} copy-done((bf16[32,32,1024]{2,1,0:T(8,128)(2,1)S(1)}, bf16[32,32,1024]{2,1,0:T(8,128)(2,1)}, u32[]{:S(2)}) %copy-start.1) | copy-done | bytes 2097176
  101.5 9.4 %shard_map.161 = (bf16[2,256,2048]{2,1,0:T(8,128)(2,1)S(1)}, bf16[2,256,2048]{2,1,0:T(8,128)(2,1)S(1)}) custom-call(s32[2]{0:T(128)S(1)} %pad_add_fusion.index_ref.refs_0_, bf16[1024,1024]{1,0:T(8,128)(2,1)S(1)} %bitcast.20, bf16[32,512]{1,0:T(8,128)(2,1)S(1)} %bitcast.23, bf16[1024,2048]{1,0:T(8,128)(2,1)} %get-tuple-element.35.refs_3_, ...), custom_call_target="tpu_custom_call" | custom-call | flops 4294967296 | bytes 14712840 | tf_op jit(solution)/shard_map/pallas_call | solution.py:30
  110.9 0.2 collective-permute-start.3
  111.2 4.0 %collective-permute-done.3.given_ref = bf16[2,256,2048]{2,1,0:T(8,128)(2,1)S(1)} collective-permute-done((bf16[2,256,2048]{2,1,0:T(8,128)(2,1)S(1)}, bf16[2,256,2048]{2,1,0:T(8,128)(2,1)S(1)}, u32[]{:S(2)}, u32[]{:S(2)}) %collective-permute-start.3) | collective-permute-done | bytes 2097184 | tf_op jit(solution)/shard_map/ppermute | solution.py:752
  115.2 0.0 copy-start.2
  115.2 0.0 copy-start.4
  115.2 0.5 shard_map.162
  115.7 0.9 collective-permute-start.4
  116.6 1.2 collective-permute-start.5
  117.8 6.3 %collective-permute-done.4.up_part_ref = bf16[64,2048]{1,0:T(8,128)(2,1)S(1)} collective-permute-done((bf16[64,2048]{1,0:T(8,128)(2,1)S(1)}, bf16[64,2048]{1,0:T(8,128)(2,1)S(1)}, u32[]{:S(2)}, u32[]{:S(2)}) %collective-permute-start.4) | collective-permute-done | bytes 262176 | tf_op jit(solution)/shard_map/ppermute | solution.py:104
  124.2 1.7 %collective-permute-done.5.down_part_ref = bf16[64,2048]{1,0:T(8,128)(2,1)S(1)} collective-permute-done((bf16[64,2048]{1,0:T(8,128)(2,1)S(1)}, bf16[64,2048]{1,0:T(8,128)(2,1)S(1)}, u32[]{:S(2)}, u32[]{:S(2)}) %collective-permute-start.5) | collective-permute-done | bytes 262176 | tf_op jit(solution)/shard_map/ppermute | solution.py:104
  125.9 0.1 shard_map.163
  126.0 0.6 collective-permute-start.6
  126.6 1.5 collective-permute-start.7
  128.1 0.0 copy-done.2
  128.1 0.0 copy-done.4
  128.1 1.5 shard_map.165.refs_2_
  129.6 9.3 %collective-permute-done.6.up_ref = bf16[2,64,2048]{2,1,0:T(8,128)(2,1)S(1)} collective-permute-done((bf16[2,64,2048]{2,1,0:T(8,128)(2,1)S(1)}, bf16[2,64,2048]{2,1,0:T(8,128)(2,1)S(1)}, u32[]{:S(2)}, u32[]{:S(2)}) %collective-permute-start.6) | collective-permute-done | bytes 524320 | tf_op jit(solution)/shard_map/ppermute | solution.py:104
  138.9 1.5 collective-permute-done.7.down_ref
  140.5 1.3 shard_map.164.refs_0_
  141.8 8.6 %all-to-all-done.1 = bf16[32,32,1024]{2,1,0:T(8,128)(2,1)S(1)} async-done(((bf16[32,32,1024]{2,1,0:T(8,128)(2,1)}), bf16[32,32,1024]{2,1,0:T(8,128)(2,1)S(1)}, u32[]{:S(2)}, u32[]{:S(2)}) %all-to-all-start.1) | async-done | bytes 2097184 | tf_op jit(solution)/shard_map/all_to_all | solution.py:118
  150.4 4.0 %shard_map.166 = (bf16[512,512]{1,0:T(8,128)(2,1)}, f32[512,512]{1,0:T(8,128)}) custom-call(f32[64,1,4096]{2,1,0:T(1,128)} %shard_map.164.refs_0_, s32[512,128]{1,0:T(8,128)S(1)} %get-tuple-element.46.refs_0_.refs_1_, f32[512,128]{1,0:T(8,128)} %shard_map.165.refs_2_, bf16[512,512]{1,0:T(8,128)(2,1)} %get-tuple-element.47.refs_1_.refs_3_, ...), custom_call_target="tpu_custom_call" | custom-call | flops 1073741824 | bytes 6326272 | tf_op jit(solution)/shard_map/pallas_call | solution.py:30
Async XLA Ops:
  2.8 12.1 %collective-permute-start.1 = (bf16[128,512]{1,0:T(8,128)(2,1)}, bf16[128,512]{1,0:T(8,128)(2,1)S(1)}, u32[]{:S(2)}, u32[]{:S(2)}) collective-permute-start(bf16[128,512]{1,0:T(8,128)(2,1)} %get-tuple-element.29), channel_id=1, source_target_pairs={{32,0},{64,32},{96,64},{128,96},{160,128},{192,160},{224,192},{0,2... | collective-permute-start | bytes 393224 | tf_op jit(solution)/shard_map/ppermute | solution.py:104
  3.1 11.8 %collective-permute-start = (bf16[64,512]{1,0:T(8,128)(2,1)}, bf16[64,512]{1,0:T(8,128)(2,1)S(1)}, u32[]{:S(2)}, u32[]{:S(2)}) collective-permute-start(bf16[64,512]{1,0:T(8,128)(2,1)} %get-tuple-element.28), channel_id=1, source_target_pairs={{1,0},{2,1},{3,2},{4,3},{5,4},{6,5},{7,6},{8,7},{9,8},{10,9},{11,1... | collective-permute-start | bytes 196616 | tf_op jit(solution)/shard_map/ppermute | solution.py:104
  11.4 3.5 %collective-permute-start.2 = (bf16[16,512]{1,0:T(8,128)(2,1)}, bf16[16,512]{1,0:T(8,128)(2,1)S(1)}, u32[]{:S(2)}, u32[]{:S(2)}) collective-permute-start(bf16[16,512]{1,0:T(8,128)(2,1)} %get-tuple-element.30), channel_id=1, source_target_pairs={{33,0},{34,1},{35,2},{36,3},{37,4},{38,5},{39,6},{40,7},{41,8},{42... | collective-permute-start | bytes 49160 | tf_op jit(solution)/shard_map/ppermute | solution.py:114
  22.9 55.6 %copy-start.3 = (bf16[512,32]{0,1:T(8,128)(2,1)S(1)}, bf16[512,32]{0,1:T(8,128)(2,1)}, u32[]{:S(2)}) copy-start(bf16[512,32]{0,1:T(8,128)(2,1)} %param.23) | copy-start | bytes 98308
  22.9 55.6 %all-to-all-start = ((bf16[32,32,1024]{2,1,0:T(8,128)(2,1)}), bf16[32,32,1024]{2,1,0:T(8,128)(2,1)S(1)}, u32[]{:S(2)}, u32[]{:S(2)}) async-start(bf16[32,32,1024]{2,1,0:T(8,128)(2,1)} %bitcast.29), calls=%async_computation | async-start | bytes 4194304 | tf_op jit(solution)/shard_map/all_to_all | solution.py:118
  78.5 13.6 %copy-start = (bf16[32,32,1024]{2,1,0:T(8,128)(2,1)}, bf16[32,32,1024]{2,1,0:T(8,128)(2,1)S(1)}, u32[]{:S(2)}) copy-start(bf16[32,32,1024]{2,1,0:T(8,128)(2,1)S(1)} %all-to-all-done) | copy-start | bytes 6291460
  92.1 58.3 %all-to-all-start.1 = ((bf16[32,32,1024]{2,1,0:T(8,128)(2,1)}), bf16[32,32,1024]{2,1,0:T(8,128)(2,1)S(1)}, u32[]{:S(2)}, u32[]{:S(2)}) async-start(bf16[32,32,1024]{2,1,0:T(8,128)(2,1)} %bitcast.28), calls=%async_computation.1 | async-start | bytes 4194304 | tf_op jit(solution)/shard_map/all_to_all | solution.py:118
  99.9 1.6 %copy-start.1 = (bf16[32,32,1024]{2,1,0:T(8,128)(2,1)S(1)}, bf16[32,32,1024]{2,1,0:T(8,128)(2,1)}, u32[]{:S(2)}) copy-start(bf16[32,32,1024]{2,1,0:T(8,128)(2,1)} %copy-done) | copy-start | bytes 6291460
  110.9 4.2 %collective-permute-start.3 = (bf16[2,256,2048]{2,1,0:T(8,128)(2,1)S(1)}, bf16[2,256,2048]{2,1,0:T(8,128)(2,1)S(1)}, u32[]{:S(2)}, u32[]{:S(2)}) collective-permute-start(bf16[2,256,2048]{2,1,0:T(8,128)(2,1)S(1)} %get-tuple-element.38), channel_id=1, source_target_pairs={{0,32},{32,0},{64,96},{96,64},{128,160},{160,128},{192,224},{224,1... | collective-permute-start | bytes 6291464 | tf_op jit(solution)/shard_map/ppermute | solution.py:752
  115.2 12.9 %copy-start.2 = (bf16[512,512]{1,0:T(8,128)(2,1)S(1)}, bf16[512,512]{1,0:T(8,128)(2,1)}, u32[]{:S(2)}) copy-start(bf16[512,512]{1,0:T(8,128)(2,1)} %get-tuple-element.47.refs_1_.refs_3_) | copy-start | bytes 1572868
  115.2 12.9 %copy-start.4 = (f32[512]{0:T(512)S(1)}, f32[512]{0:T(512)}, u32[]{:S(2)}) copy-start(f32[512]{0:T(512)} %param.22) | copy-start | bytes 6148
  115.7 8.4 %collective-permute-start.4 = (bf16[64,2048]{1,0:T(8,128)(2,1)S(1)}, bf16[64,2048]{1,0:T(8,128)(2,1)S(1)}, u32[]{:S(2)}, u32[]{:S(2)}) collective-permute-start(bf16[64,2048]{1,0:T(8,128)(2,1)S(1)} %get-tuple-element.42), channel_id=1, source_target_pairs={{192,0},{224,32},{0,64},{32,96},{64,128},{96,160},{128,192},{160,2... | collective-permute-start | bytes 786440 | tf_op jit(solution)/shard_map/ppermute | solution.py:104
  116.6 9.3 %collective-permute-start.5 = (bf16[64,2048]{1,0:T(8,128)(2,1)S(1)}, bf16[64,2048]{1,0:T(8,128)(2,1)S(1)}, u32[]{:S(2)}, u32[]{:S(2)}) collective-permute-start(bf16[64,2048]{1,0:T(8,128)(2,1)S(1)} %get-tuple-element.43), channel_id=1, source_target_pairs={{64,0},{96,32},{128,64},{160,96},{192,128},{224,160},{0,192},{32,2... | collective-permute-start | bytes 786440 | tf_op jit(solution)/shard_map/ppermute | solution.py:104
  126.0 12.9 %collective-permute-start.6 = (bf16[2,64,2048]{2,1,0:T(8,128)(2,1)S(1)}, bf16[2,64,2048]{2,1,0:T(8,128)(2,1)S(1)}, u32[]{:S(2)}, u32[]{:S(2)}) collective-permute-start(bf16[2,64,2048]{2,1,0:T(8,128)(2,1)S(1)} %get-tuple-element.44), channel_id=1, source_target_pairs={{192,0},{224,32},{0,64},{32,96},{64,128},{96,160},{128,192},{160,2... | collective-permute-start | bytes 1572872 | tf_op jit(solution)/shard_map/ppermute | solution.py:104
  126.6 13.9 %collective-permute-start.7 = (bf16[2,64,2048]{2,1,0:T(8,128)(2,1)S(1)}, bf16[2,64,2048]{2,1,0:T(8,128)(2,1)S(1)}, u32[]{:S(2)}, u32[]{:S(2)}) collective-permute-start(bf16[2,64,2048]{2,1,0:T(8,128)(2,1)S(1)} %get-tuple-element.45), channel_id=1, source_target_pairs={{64,0},{96,32},{128,64},{160,96},{192,128},{224,160},{0,192},{32,2... | collective-permute-start | bytes 1572872 | tf_op jit(solution)/shard_map/ppermute | solution.py:104

commit v6 on v5

--- a/solution.py
+++ b/solution.py
@@ -381,36 +381,23 @@
     index_ref,
     slots_ref,
     router_ref,
-    w_in_ref,
-    w_out_ref,
+    w_in,
+    w_out,
     back_ref,
     act_ref,
     dpre_ref,
-    w_in,
-    w_out,
     act,
     dpre,
     back,
-    load_sems,
     store_sems,
 ):
     rows, width = slots_ref.shape[0], slots_ref.shape[1] // 2
     units = w_in.shape[1]
     tile, chunk, piece = rows // TILES, units // PARTS, width // 2
 
-    def load(source, target, i):
-        copy = pltpu.make_async_copy(source, target, load_sems.at[i])
-        copy.start()
-        return copy
-
     def tiled(i, step):
         return slice(i * step, (i + 1) * step)
 
-    loads = []
-    for i in range(PARTS):
-        part = tiled(i, chunk)
-        loads.append(load(w_in_ref.at[:, part], w_in.at[:, part], 2 * i))
-        loads.append(load(w_out_ref.at[:, part], w_out.at[:, part], 2 * i + 1))
     stores = []
 
     def store(source, target):
@@ -425,9 +412,6 @@
         for c in range(PARTS):
             part = tiled(c, chunk)
             if r < TILES:
-                if r == 0:
-                    loads[2 * c].wait()
-                    loads[2 * c + 1].wait()
                 activation, slopes = doubled_gelu_parts(
                     dot(slots_ref[here, :width], w_in[:, part])
                 )
@@ -708,23 +692,20 @@
             far((slot_total, units), BF16),
             far((slot_total, units), BF16),
         ),
-        (SCALAR, WHOLE, WHOLE, FAR, FAR),
+        (SCALAR,) + (WHOLE,) * 4,
         index,
         slots,
         router_t,
-        kept_far(w_in),
-        kept_far(w_out),
+        w_in,
+        w_out,
         out_specs=(FAR, FAR, FAR),
         scratch=[
-            pltpu.VMEM((width, units), BF16),
-            pltpu.VMEM((width, units), BF16),
             pltpu.VMEM((slot_total, units), BF16),
             pltpu.VMEM((slot_total, units), BF16),
             pltpu.VMEM((slot_total, 2 * width), BF16),
-            dma((2 * PARTS,)),
             dma((3 * TILES,)),
         ],
-        vmem=40,
+        vmem=32,
         flops=8 * slot_total * width * units,
     )
     back = exchanged(back.reshape(expert_total, capacity, 2 * width)).reshape(

time: 155 us -> 157 us (1.013)
  local copies, waits for them, and re-layouts: 1.6 us -> 5.54 us
  Pallas kernels: 43.5 us -> 41.5 us
    unnamed x10 -> x14, local copies, waits for them, and re-layouts: 1.6 us -> 5.54 us
    pallas_call x10, Pallas kernels: 43.5 us -> 41.5 us  [call(): pl.pallas_call(body, grid=grid, out_shape=outs, in_specs=list(ins), out_s...]
where the time goes in v6:
time: 157 us; the launch traced here: 156 us
  waiting for transfers between devices  80.6 us (51%)
  Pallas kernels  41.5 us (26%)
  starting transfers between devices  27.9 us (18%)
  local copies, waits for them, and re-layouts  5.54 us (4%)
    all_to_all x2, waiting for transfers between devices, exchanged(): return lax.all_to_all(slots, 'lon', split_axis=0, concat_axis=0, tiled=True)  57.7 us
    pallas_call x10, Pallas kernels, call(): pl.pallas_call(body, grid=grid, out_shape=outs, in_specs=list(ins), out_s...  41.5 us
    ppermute x6, waiting for transfers between devices, passed_along(): return lax.ppermute(block, axis, route)  18.9 us
    all_to_all x2, starting transfers between devices, exchanged(): return lax.all_to_all(slots, 'lon', split_axis=0, concat_axis=0, tiled=True)  14.3 us
    ppermute x6, starting transfers between devices, passed_along(): return lax.ppermute(block, axis, route)  12.8 us
    unnamed x14, local copies, waits for them, and re-layouts  5.54 us
    ppermute x1, waiting for transfers between devices, per_device(): given = lax.ppermute(give, 'lat', [(i, i ^ 1) for i in range(lat_total)])  4.02 us
  transfers between devices with their start and end apart: 10, of which 7 were waited for; matrix products, arithmetic and copies ran while one was open for 0% of the time, Pallas kernels for 10%

profile of v6, /device:TPU:6, one launch (start us, length us, event | category | flops | bytes accessed | tf_op | source)
XLA Modules:
  0.0 156.5 jit_solution(4158075856218933287)
XLA Ops:
  0.6 2.2 %shard_map.157 = (bf16[512,512]{1,0:T(8,128)(2,1)S(1)}, bf16[64,512]{1,0:T(8,128)(2,1)}, bf16[128,512]{1,0:T(8,128)(2,1)}, bf16[16,512]{1,0:T(8,128)(2,1)}) custom-call(bf16[512,512]{1,0:T(8,128)(2,1)} %bitcast.34, s32[16,32]{1,0:T(8,128)} %mask_ref.1, bf16[512]{0:T(512)(128)(2,1)} %token_ref.1), custom_call_target="tpu_custom_call" | custom-call | bytes 1264640 | tf_op jit(solution)/shard_map/pallas_call | solution.py:30
  2.8 0.3 collective-permute-start.1
  3.1 8.3 %collective-permute-start = (bf16[64,512]{1,0:T(8,128)(2,1)}, bf16[64,512]{1,0:T(8,128)(2,1)S(1)}, u32[]{:S(2)}, u32[]{:S(2)}) collective-permute-start(bf16[64,512]{1,0:T(8,128)(2,1)} %get-tuple-element.28), channel_id=1, source_target_pairs={{1,0},{2,1},{3,2},{4,3},{5,4},{6,5},{7,6},{8,7},{9,8},{10,9},{11,1... | collective-permute-start | bytes 196616 | tf_op jit(solution)/shard_map/ppermute | solution.py:104
  11.4 0.6 collective-permute-start.2
  12.0 2.9 %shard_map.158 = (s32[512,128]{1,0:T(8,128)S(1)}, bf16[1024,512]{1,0:T(8,128)(2,1)S(1)}, bf16[512,720]{1,0:T(8,128)(2,1)S(1)}, bf16[1024,1024]{1,0:T(8,128)(2,1)}) custom-call(s32[1,512]{1,0:T(1,128)} %bitcast.37, bf16[512,512]{1,0:T(8,128)(2,1)} %bitcast.32), custom_call_target="tpu_custom_call" | custom-call | flops 536870912 | bytes 4671488 | tf_op jit(solution)/shard_map/pallas_call | solution.py:30
  14.8 0.0 collective-permute-done.2.refs_4_
  14.9 0.0 collective-permute-done.refs_2_
  14.9 0.0 collective-permute-done.1.refs_3_
  14.9 8.0 %shard_map.159 = (bf16[512,512]{1,0:T(8,128)(2,1)}, bf16[1024,1024]{1,0:T(8,128)(2,1)}) custom-call(s32[1]{0:T(128)} %bitcast.2.refs_0_, bf16[512,512]{1,0:T(8,128)(2,1)S(1)} %get-tuple-element.27.refs_1_, bf16[64,512]{1,0:T(8,128)(2,1)S(1)} %collective-permute-done.refs_2_, ...), custom_call_target="tpu_custom_call", output_to_operand_aliasing={{1}: (7, {})} | custom-call | flops 2147483648 | bytes 9605188 | tf_op jit(solution)/shard_map/pallas_call | solution.py:30
  22.8 0.0 copy-start.3
  22.9 6.5 %all-to-all-start = ((bf16[32,32,1024]{2,1,0:T(8,128)(2,1)}), bf16[32,32,1024]{2,1,0:T(8,128)(2,1)S(1)}, u32[]{:S(2)}, u32[]{:S(2)}) async-start(bf16[32,32,1024]{2,1,0:T(8,128)(2,1)} %bitcast.31), calls=%async_computation | async-start | bytes 4194304 | tf_op jit(solution)/shard_map/all_to_all | solution.py:118
  29.3 0.1 pad_add_fusion.index_ref.refs_0_
  29.4 49.1 %all-to-all-done = bf16[32,32,1024]{2,1,0:T(8,128)(2,1)S(1)} async-done(((bf16[32,32,1024]{2,1,0:T(8,128)(2,1)}), bf16[32,32,1024]{2,1,0:T(8,128)(2,1)S(1)}, u32[]{:S(2)}, u32[]{:S(2)}) %all-to-all-start) | async-done | bytes 2097184 | tf_op jit(solution)/shard_map/all_to_all | solution.py:118
  78.5 0.0 copy-start
  78.5 0.0 copy-done.3
  78.5 0.0 copy-start.5
  78.5 2.3 %copy-done.5 = bf16[1,512,2048]{2,1,0:T(8,128)(2,1)S(1)} copy-done((bf16[1,512,2048]{2,1,0:T(8,128)(2,1)S(1)}, bf16[1,512,2048]{2,1,0:T(8,128)(2,1)}, u32[]{:S(2)}) %copy-start.5) | copy-done | bytes 2097176
  80.8 0.0 copy-start.6
  80.8 1.6 %copy-done.6 = bf16[1,512,2048]{2,1,0:T(8,128)(2,1)S(1)} copy-done((bf16[1,512,2048]{2,1,0:T(8,128)(2,1)S(1)}, bf16[1,512,2048]{2,1,0:T(8,128)(2,1)}, u32[]{:S(2)}) %copy-start.6) | copy-done | bytes 2097176
  82.4 11.6 %shard_map.160 = (bf16[1024,1024]{1,0:T(8,128)(2,1)}, bf16[1024,2048]{1,0:T(8,128)(2,1)}, bf16[1024,2048]{1,0:T(8,128)(2,1)}) custom-call(s32[2]{0:T(128)S(1)} %pad_add_fusion.index_ref.refs_0_, bf16[1024,1024]{1,0:T(8,128)(2,1)S(1)} %bitcast.19, bf16[32,512]{1,0:T(8,128)(2,1)S(1)} %bitcast.22, bf16[512,2048]{1,0:T(8,128)(2,1)S(1)} %bitcast.28, ...), custom_call_target="tpu_custom_call" | custom-call | flops 8589934592 | bytes 16809992 | tf_op jit(solution)/shard_map/pallas_call | solution.py:30
  94.0 0.0 copy-done
  94.0 7.8 %all-to-all-start.1 = ((bf16[32,32,1024]{2,1,0:T(8,128)(2,1)}), bf16[32,32,1024]{2,1,0:T(8,128)(2,1)S(1)}, u32[]{:S(2)}, u32[]{:S(2)}) async-start(bf16[32,32,1024]{2,1,0:T(8,128)(2,1)} %bitcast.30), calls=%async_computation.1 | async-start | bytes 4194304 | tf_op jit(solution)/shard_map/all_to_all | solution.py:118
  101.8 0.0 copy-start.1
  101.8 1.6 %copy-done.1 = bf16[32,32,1024]{2,1,0:T(8,128)(2,1)S(1)} copy-done((bf16[32,32,1024]{2,1,0:T(8,128)(2,1)S(1)}, bf16[32,32,1024]{2,1,0:T(8,128)(2,1)}, u32[]{:S(2)}) %copy-start.1) | copy-done | bytes 2097176
  103.4 9.4 %shard_map.161 = (bf16[2,256,2048]{2,1,0:T(8,128)(2,1)S(1)}, bf16[2,256,2048]{2,1,0:T(8,128)(2,1)S(1)}) custom-call(s32[2]{0:T(128)S(1)} %pad_add_fusion.index_ref.refs_0_, bf16[1024,1024]{1,0:T(8,128)(2,1)S(1)} %bitcast.20, bf16[32,512]{1,0:T(8,128)(2,1)S(1)} %bitcast.23, bf16[1024,2048]{1,0:T(8,128)(2,1)} %get-tuple-element.35.refs_3_, ...), custom_call_target="tpu_custom_call" | custom-call | flops 4294967296 | bytes 14712840 | tf_op jit(solution)/shard_map/pallas_call | solution.py:30
  112.9 0.2 collective-permute-start.3
  113.1 4.0 %collective-permute-done.3.given_ref = bf16[2,256,2048]{2,1,0:T(8,128)(2,1)S(1)} collective-permute-done((bf16[2,256,2048]{2,1,0:T(8,128)(2,1)S(1)}, bf16[2,256,2048]{2,1,0:T(8,128)(2,1)S(1)}, u32[]{:S(2)}, u32[]{:S(2)}) %collective-permute-start.3) | collective-permute-done | bytes 2097184 | tf_op jit(solution)/shard_map/ppermute | solution.py:733
  117.1 0.0 copy-start.2
  117.1 0.0 copy-start.4
  117.1 0.5 shard_map.162
  117.7 0.9 collective-permute-start.4
  118.5 1.2 collective-permute-start.5
  119.8 6.3 %collective-permute-done.4.up_part_ref = bf16[64,2048]{1,0:T(8,128)(2,1)S(1)} collective-permute-done((bf16[64,2048]{1,0:T(8,128)(2,1)S(1)}, bf16[64,2048]{1,0:T(8,128)(2,1)S(1)}, u32[]{:S(2)}, u32[]{:S(2)}) %collective-permute-start.4) | collective-permute-done | bytes 262176 | tf_op jit(solution)/shard_map/ppermute | solution.py:104
  126.1 1.7 %collective-permute-done.5.down_part_ref = bf16[64,2048]{1,0:T(8,128)(2,1)S(1)} collective-permute-done((bf16[64,2048]{1,0:T(8,128)(2,1)S(1)}, bf16[64,2048]{1,0:T(8,128)(2,1)S(1)}, u32[]{:S(2)}, u32[]{:S(2)}) %collective-permute-start.5) | collective-permute-done | bytes 262176 | tf_op jit(solution)/shard_map/ppermute | solution.py:104
  127.8 0.1 shard_map.163
  127.9 0.6 collective-permute-start.6
  128.5 1.5 collective-permute-start.7
  130.0 0.0 copy-done.2
  130.1 0.0 copy-done.4
  130.1 1.5 shard_map.165.refs_2_
  131.5 9.3 %collective-permute-done.6.up_ref = bf16[2,64,2048]{2,1,0:T(8,128)(2,1)S(1)} collective-permute-done((bf16[2,64,2048]{2,1,0:T(8,128)(2,1)S(1)}, bf16[2,64,2048]{2,1,0:T(8,128)(2,1)S(1)}, u32[]{:S(2)}, u32[]{:S(2)}) %collective-permute-start.6) | collective-permute-done | bytes 524320 | tf_op jit(solution)/shard_map/ppermute | solution.py:104
  140.8 1.5 collective-permute-done.7.down_ref
  142.4 1.3 shard_map.164.refs_0_
  143.7 8.6 %all-to-all-done.1 = bf16[32,32,1024]{2,1,0:T(8,128)(2,1)S(1)} async-done(((bf16[32,32,1024]{2,1,0:T(8,128)(2,1)}), bf16[32,32,1024]{2,1,0:T(8,128)(2,1)S(1)}, u32[]{:S(2)}, u32[]{:S(2)}) %all-to-all-start.1) | async-done | bytes 2097184 | tf_op jit(solution)/shard_map/all_to_all | solution.py:118
  152.3 4.0 %shard_map.166 = (bf16[512,512]{1,0:T(8,128)(2,1)}, f32[512,512]{1,0:T(8,128)}) custom-call(f32[64,1,4096]{2,1,0:T(1,128)} %shard_map.164.refs_0_, s32[512,128]{1,0:T(8,128)S(1)} %get-tuple-element.46.refs_0_.refs_1_, f32[512,128]{1,0:T(8,128)} %shard_map.165.refs_2_, bf16[512,512]{1,0:T(8,128)(2,1)} %get-tuple-element.47.refs_1_.refs_3_, ...), custom_call_target="tpu_custom_call" | custom-call | flops 1073741824 | bytes 6326272 | tf_op jit(solution)/shard_map/pallas_call | solution.py:30
Async XLA Ops:
  2.8 12.1 %collective-permute-start.1 = (bf16[128,512]{1,0:T(8,128)(2,1)}, bf16[128,512]{1,0:T(8,128)(2,1)S(1)}, u32[]{:S(2)}, u32[]{:S(2)}) collective-permute-start(bf16[128,512]{1,0:T(8,128)(2,1)} %get-tuple-element.29), channel_id=1, source_target_pairs={{32,0},{64,32},{96,64},{128,96},{160,128},{192,160},{224,192},{0,2... | collective-permute-start | bytes 393224 | tf_op jit(solution)/shard_map/ppermute | solution.py:104
  3.1 11.8 %collective-permute-start = (bf16[64,512]{1,0:T(8,128)(2,1)}, bf16[64,512]{1,0:T(8,128)(2,1)S(1)}, u32[]{:S(2)}, u32[]{:S(2)}) collective-permute-start(bf16[64,512]{1,0:T(8,128)(2,1)} %get-tuple-element.28), channel_id=1, source_target_pairs={{1,0},{2,1},{3,2},{4,3},{5,4},{6,5},{7,6},{8,7},{9,8},{10,9},{11,1... | collective-permute-start | bytes 196616 | tf_op jit(solution)/shard_map/ppermute | solution.py:104
  11.4 3.5 %collective-permute-start.2 = (bf16[16,512]{1,0:T(8,128)(2,1)}, bf16[16,512]{1,0:T(8,128)(2,1)S(1)}, u32[]{:S(2)}, u32[]{:S(2)}) collective-permute-start(bf16[16,512]{1,0:T(8,128)(2,1)} %get-tuple-element.30), channel_id=1, source_target_pairs={{33,0},{34,1},{35,2},{36,3},{37,4},{38,5},{39,6},{40,7},{41,8},{42... | collective-permute-start | bytes 49160 | tf_op jit(solution)/shard_map/ppermute | solution.py:114
  22.8 55.6 %copy-start.3 = (bf16[512,32]{0,1:T(8,128)(2,1)S(1)}, bf16[512,32]{0,1:T(8,128)(2,1)}, u32[]{:S(2)}) copy-start(bf16[512,32]{0,1:T(8,128)(2,1)} %param.23) | copy-start | bytes 98308
  22.9 55.6 %all-to-all-start = ((bf16[32,32,1024]{2,1,0:T(8,128)(2,1)}), bf16[32,32,1024]{2,1,0:T(8,128)(2,1)S(1)}, u32[]{:S(2)}, u32[]{:S(2)}) async-start(bf16[32,32,1024]{2,1,0:T(8,128)(2,1)} %bitcast.31), calls=%async_computation | async-start | bytes 4194304 | tf_op jit(solution)/shard_map/all_to_all | solution.py:118
  78.5 15.5 %copy-start = (bf16[32,32,1024]{2,1,0:T(8,128)(2,1)}, bf16[32,32,1024]{2,1,0:T(8,128)(2,1)S(1)}, u32[]{:S(2)}) copy-start(bf16[32,32,1024]{2,1,0:T(8,128)(2,1)S(1)} %all-to-all-done) | copy-start | bytes 6291460
  78.5 2.3 %copy-start.5 = (bf16[1,512,2048]{2,1,0:T(8,128)(2,1)S(1)}, bf16[1,512,2048]{2,1,0:T(8,128)(2,1)}, u32[]{:S(2)}) copy-start(bf16[1,512,2048]{2,1,0:T(8,128)(2,1)} %param.25) | copy-start | bytes 6291460
  80.8 1.6 %copy-start.6 = (bf16[1,512,2048]{2,1,0:T(8,128)(2,1)S(1)}, bf16[1,512,2048]{2,1,0:T(8,128)(2,1)}, u32[]{:S(2)}) copy-start(bf16[1,512,2048]{2,1,0:T(8,128)(2,1)} %param.26) | copy-start | bytes 6291460
  94.0 58.3 %all-to-all-start.1 = ((bf16[32,32,1024]{2,1,0:T(8,128)(2,1)}), bf16[32,32,1024]{2,1,0:T(8,128)(2,1)S(1)}, u32[]{:S(2)}, u32[]{:S(2)}) async-start(bf16[32,32,1024]{2,1,0:T(8,128)(2,1)} %bitcast.30), calls=%async_computation.1 | async-start | bytes 4194304 | tf_op jit(solution)/shard_map/all_to_all | solution.py:118
  101.8 1.6 %copy-start.1 = (bf16[32,32,1024]{2,1,0:T(8,128)(2,1)S(1)}, bf16[32,32,1024]{2,1,0:T(8,128)(2,1)}, u32[]{:S(2)}) copy-start(bf16[32,32,1024]{2,1,0:T(8,128)(2,1)} %copy-done) | copy-start | bytes 6291460
  112.9 4.2 %collective-permute-start.3 = (bf16[2,256,2048]{2,1,0:T(8,128)(2,1)S(1)}, bf16[2,256,2048]{2,1,0:T(8,128)(2,1)S(1)}, u32[]{:S(2)}, u32[]{:S(2)}) collective-permute-start(bf16[2,256,2048]{2,1,0:T(8,128)(2,1)S(1)} %get-tuple-element.38), channel_id=1, source_target_pairs={{0,32},{32,0},{64,96},{96,64},{128,160},{160,128},{192,224},{224,1... | collective-permute-start | bytes 6291464 | tf_op jit(solution)/shard_map/ppermute | solution.py:733
  117.1 12.9 %copy-start.2 = (bf16[512,512]{1,0:T(8,128)(2,1)S(1)}, bf16[512,512]{1,0:T(8,128)(2,1)}, u32[]{:S(2)}) copy-start(bf16[512,512]{1,0:T(8,128)(2,1)} %get-tuple-element.47.refs_1_.refs_3_) | copy-start | bytes 1572868
  117.1 12.9 %copy-start.4 = (f32[512]{0:T(512)S(1)}, f32[512]{0:T(512)}, u32[]{:S(2)}) copy-start(f32[512]{0:T(512)} %param.22) | copy-start | bytes 6148
  117.7 8.4 %collective-permute-start.4 = (bf16[64,2048]{1,0:T(8,128)(2,1)S(1)}, bf16[64,2048]{1,0:T(8,128)(2,1)S(1)}, u32[]{:S(2)}, u32[]{:S(2)}) collective-permute-start(bf16[64,2048]{1,0:T(8,128)(2,1)S(1)} %get-tuple-element.42), channel_id=1, source_target_pairs={{192,0},{224,32},{0,64},{32,96},{64,128},{96,160},{128,192},{160,2... | collective-permute-start | bytes 786440 | tf_op jit(solution)/shard_map/ppermute | solution.py:104
  118.5 9.3 %collective-permute-start.5 = (bf16[64,2048]{1,0:T(8,128)(2,1)S(1)}, bf16[64,2048]{1,0:T(8,128)(2,1)S(1)}, u32[]{:S(2)}, u32[]{:S(2)}) collective-permute-start(bf16[64,2048]{1,0:T(8,128)(2,1)S(1)} %get-tuple-element.43), channel_id=1, source_target_pairs={{64,0},{96,32},{128,64},{160,96},{192,128},{224,160},{0,192},{32,2... | collective-permute-start | bytes 786440 | tf_op jit(solution)/shard_map/ppermute | solution.py:104
  127.9 12.9 %collective-permute-start.6 = (bf16[2,64,2048]{2,1,0:T(8,128)(2,1)S(1)}, bf16[2,64,2048]{2,1,0:T(8,128)(2,1)S(1)}, u32[]{:S(2)}, u32[]{:S(2)}) collective-permute-start(bf16[2,64,2048]{2,1,0:T(8,128)(2,1)S(1)} %get-tuple-element.44), channel_id=1, source_target_pairs={{192,0},{224,32},{0,64},{32,96},{64,128},{96,160},{128,192},{160,2... | collective-permute-start | bytes 1572872 | tf_op jit(solution)/shard_map/ppermute | solution.py:104
  128.5 13.9 %collective-permute-start.7 = (bf16[2,64,2048]{2,1,0:T(8,128)(2,1)S(1)}, bf16[2,64,2048]{2,1,0:T(8,128)(2,1)S(1)}, u32[]{:S(2)}, u32[]{:S(2)}) collective-permute-start(bf16[2,64,2048]{2,1,0:T(8,128)(2,1)S(1)} %get-tuple-element.45), channel_id=1, source_target_pairs={{64,0},{96,32},{128,64},{160,96},{192,128},{224,160},{0,192},{32,2... | collective-permute-start | bytes 1572872 | tf_op jit(solution)/shard_map/ppermute | solution.py:104
